TPU v7x, 32 devices: a whole 2x2x4 slice. The times are simulated.
32 devices in a mesh: dom: 8 (over z, y), sub: 4 (over x, core).
Axes of the slice: x: 2, y: 2, z: 4, core: 2. Of those that a mesh axis runs over, the one named last changes fastest.
Arguments:
- features: bfloat16 [32768, 256], P(('dom', 'sub')), may hold values from -6 to 6
- cotangent: bfloat16 [32768, 256], P(('dom', 'sub')), may hold values from -6 to 6
- w_self_one: bfloat16 [256, 256], replicated, may hold values from -0.375 to 0.375
- w_nbr_one: bfloat16 [256, 256], replicated, may hold values from -0.375 to 0.375
- bias_one: float32 [256], replicated, may hold values from -4 to 4
- w_self_two: bfloat16 [256, 256], replicated, may hold values from -0.375 to 0.375
- w_nbr_two: bfloat16 [256, 256], replicated, may hold values from -0.375 to 0.375
- in_count: int32 [32768], P(('dom', 'sub')), may hold values from 0 to 7
- send_list: int32 [32, 32, 4], P(('dom', 'sub')), may hold values from 0 to 1023
- src_slot: int32 [32, 2048], P(('dom', 'sub')), may hold values from 0 to 1151
- dst_slot: int32 [32, 2048], P(('dom', 'sub')), may hold values from 0 to 1151
- edge_count: int32 [32], P(('dom', 'sub')), may hold values from 512 to 2048, as said below
Outputs:
- grad_features: bfloat16 [32768, 256], P(('dom', 'sub'))
- grad_weights: float32 [4, 256, 256], replicated
- grad_bias: float32 [256], replicated
Inputs may be any that keep to these rules, and one draw needn't show every extreme that they name: Each device's first edge_count slots are live; one device has all 2048 live in every draw.
All inputs are finite; a program needn't handle non-finite values.
Results may differ from a plain program's by a relative error of at most 0.0056.
Values may be sent and summed in bfloat16 or wider, within the bound.
No kernel may reach another device: no remote copies, remote signals or barrier semaphores. Data moves between devices by JAX's collectives and lax.ppermute only.
A program may use at most 64 MiB of HBM per device.

v0:
```python
import math

import jax
import jax.numpy as jnp
from jax import lax
from jax.sharding import PartitionSpec as P


def to_mirrors(master_rows, send_list):
    picked_rows = jnp.take(master_rows, send_list[0], axis=0)
    feature_dim = master_rows.shape[1]
    received = lax.all_to_all(picked_rows, ("dom", "sub"), split_axis=0, concat_axis=0, tiled=True)
    return received.reshape(-1, feature_dim)


def to_masters(mirror_partial, send_list, node_dev):
    feature_dim = mirror_partial.shape[1]
    per_peer = send_list.shape[2]
    sectioned_rows = mirror_partial.reshape(-1, per_peer, feature_dim)
    received = lax.all_to_all(
        sectioned_rows, ("dom", "sub"), split_axis=0, concat_axis=0, tiled=True
    )
    flat_rows = received.reshape(-1, feature_dim)
    owners = send_list[0].reshape(-1)
    placing = (jnp.arange(node_dev, dtype=jnp.int32)[:, None] == owners[None, :]).astype(
        jnp.float32
    )
    return jnp.dot(
        placing, flat_rows, precision=lax.Precision.HIGHEST, preferred_element_type=jnp.float32
    )


def spread(slot_table, from_slot, into_slot, live_count):
    slot_total = slot_table.shape[0]
    edge_slots = from_slot.shape[0]
    feature_dim = slot_table.shape[1]
    block_rows = math.gcd(512, edge_slots)
    slot_ids = jnp.arange(slot_total, dtype=jnp.int32)[None, :]

    def one_block(turn_index, total):
        offset = turn_index * block_rows
        from_part = lax.dynamic_slice_in_dim(from_slot, offset, block_rows)
        into_part = lax.dynamic_slice_in_dim(into_slot, offset, block_rows)
        live_rows = (jnp.arange(block_rows, dtype=jnp.int32) + offset < live_count)[:, None]
        picking = ((from_part[:, None] == slot_ids) & live_rows).astype(slot_table.dtype)
        picked_rows = jnp.dot(picking, slot_table, preferred_element_type=jnp.float32).astype(
            slot_table.dtype
        )
        placing = (into_part[:, None] == slot_ids).astype(slot_table.dtype)
        return total + tdot(placing, picked_rows)

    start_total = jnp.zeros((slot_total, feature_dim), jnp.float32)
    block_count = edge_slots // block_rows
    return lax.fori_loop(0, block_count, one_block, start_total)


def tdot(left, right):
    return lax.dot_general(
        left, right, (((0,), (0,)), ((), ())), preferred_element_type=jnp.float32
    )


def dot_transposed(left, right):
    return lax.dot_general(
        left, right, (((1,), (1,)), ((), ())), preferred_element_type=jnp.float32
    )


def silu_grad(value):
    sigmoid_v = jax.nn.sigmoid(value)
    return sigmoid_v * (1.0 + value * (1.0 - sigmoid_v))


def shards(
    features,
    cotangent,
    w_self_one,
    w_nbr_one,
    bias_one,
    w_self_two,
    w_nbr_two,
    in_count,
    send_list,
    src_slot,
    dst_slot,
    edge_count,
):
    node_dev = features.shape[0]
    width = features.shape[1]
    sources = src_slot[0]
    targets = dst_slot[0]
    live_count = edge_count[0]
    inverse = (1.0 / jnp.maximum(in_count, 1).astype(jnp.float32))[:, None]

    def gather_sum(master_rows, from_slot, into_slot):
        slot_table = jnp.concatenate([master_rows, to_mirrors(master_rows, send_list)], axis=0)
        partial_value = spread(slot_table, from_slot, into_slot, live_count)
        return partial_value[:node_dev] + to_masters(partial_value[node_dev:], send_list, node_dev)

    mean_one = (gather_sum(features, sources, targets) * inverse).astype(jnp.bfloat16)
    z_one = (
        jnp.dot(features, w_self_one, preferred_element_type=jnp.float32)
        + jnp.dot(mean_one, w_nbr_one, preferred_element_type=jnp.float32)
        + bias_one
    )
    h_one = jax.nn.silu(z_one).astype(jnp.bfloat16)
    message_two = (dot_transposed(cotangent, w_nbr_two) * inverse).astype(jnp.bfloat16)
    paired = jnp.concatenate([h_one, message_two], axis=1)
    slot_table = jnp.concatenate([paired, to_mirrors(paired, send_list)], axis=0)
    forward_part = spread(slot_table[:, :width], sources, targets, live_count)
    backward_part = spread(slot_table[:, width:], targets, sources, live_count)
    joined = jnp.concatenate([forward_part, backward_part], axis=1)
    summed = joined[:node_dev] + to_masters(joined[node_dev:], send_list, node_dev)
    forward_sum = summed[:, :width]
    backward_sum = summed[:, width:]
    mean_two = (forward_sum * inverse).astype(jnp.bfloat16)
    late_self = tdot(h_one, cotangent)
    late_nbr = tdot(mean_two, cotangent)
    grad_h_one = dot_transposed(cotangent, w_self_two) + backward_sum
    grad_z_one = (grad_h_one * silu_grad(z_one)).astype(jnp.bfloat16)
    message_one = (dot_transposed(grad_z_one, w_nbr_one) * inverse).astype(jnp.bfloat16)
    early_self = tdot(features, grad_z_one)
    early_nbr = tdot(mean_one, grad_z_one)
    early_bias = jnp.sum(grad_z_one.astype(jnp.float32), axis=0)
    grad_features = (
        dot_transposed(grad_z_one, w_self_one) + gather_sum(message_one, targets, sources)
    ).astype(jnp.bfloat16)
    self_one, nbr_one, bias_sum, self_two, nbr_two = lax.psum(
        (early_self, early_nbr, early_bias, late_self, late_nbr), ("dom", "sub")
    )
    norm_factor = jnp.float32(node_dev * lax.axis_size("dom") * lax.axis_size("sub")) ** (-0.5)
    grad_weights = jnp.stack([self_one, nbr_one, self_two, nbr_two]) * norm_factor
    grad_bias = bias_sum * norm_factor
    return (grad_features, grad_weights, grad_bias)


def solution(mesh):
    return jax.shard_map(
        shards,
        mesh=mesh,
        in_specs=(
            P(("dom", "sub"), None),
            P(("dom", "sub"), None),
            P(),
            P(),
            P(),
            P(),
            P(),
            P(("dom", "sub")),
            P(("dom", "sub"), None, None),
            P(("dom", "sub"), None),
            P(("dom", "sub"), None),
            P(("dom", "sub")),
        ),
        out_specs=(P(("dom", "sub"), None), P(), P()),
        check_vma=False,
    )
```

profile of v0, /device:TPU:0, one launch (start us, length us, event | category | flops | bytes accessed | tf_op | source)
XLA Modules:
  0.0 327.8 jit_solution(14620767086165137964)
XLA Ops:
  13.1 7.3 %all-to-all-start = ((bf16[32,4,256]{2,1,0:T(4,128)(2,1)}), bf16[32,4,256]{2,1,0:T(4,128)(2,1)S(1)}, u32[]{:S(2)}, u32[]{:S(2)}) async-start(bf16[32,4,256]{2,1,0:T(4,128)(2,1)} %broadcast_select_fusion.2), calls=%async_computation | async-start | bytes 131072 | tf_op jit(solution)/shard_map/all_to_all | solution.py:12
  23.1 4.7 %all-to-all-done = bf16[32,4,256]{2,1,0:T(4,128)(2,1)S(1)} async-done(((bf16[32,4,256]{2,1,0:T(4,128)(2,1)}), bf16[32,4,256]{2,1,0:T(4,128)(2,1)S(1)}, u32[]{:S(2)}, u32[]{:S(2)}) %all-to-all-start) | async-done | bytes 65568 | tf_op jit(solution)/shard_map/all_to_all | solution.py:12
  27.9 13.7 %while.60 = (s32[]{:T(128)}, f32[1152,256]{1,0:T(8,128)S(1)}, s32[2048]{0:T(1024)}, s32[2048]{0:T(1024)S(1)}, s32[]{:T(128)}, /*index=5*/bf16[1152,256]{1,0:T(8,...) while((s32[]{:T(128)}, f32[1152,256]{1,0:T(8,128)S(1)}, s32[2048]{0:T(1024)}, ...), condition=%wide.region_1.3_spmd.clone.clone, body=%wide.region_0.0_spmd.clone.clone.sunk | while | flops 606471168 | bytes 2962605 | solution.py:54
  45.3 7.9 %all-to-all-done.1 = f32[32,4,256]{2,1,0:T(4,128)S(1)} async-done(((f32[32,4,256]{2,1,0:T(4,128)}), f32[32,4,256]{2,1,0:T(4,128)S(1)}, u32[]{:S(2)}, u32[]{:S(2)}) %all-to-all-start.1) | async-done | bytes 131104 | tf_op jit(solution)/shard_map/all_to_all | solution.py:20
  61.4 8.2 %all-to-all-done.2 = bf16[32,4,512]{2,1,0:T(4,128)(2,1)S(1)} async-done(((bf16[32,4,512]{2,1,0:T(4,128)(2,1)}), bf16[32,4,512]{2,1,0:T(4,128)(2,1)S(1)}, u32[]{:S(2)}, u32[]{:S(2)}) %all-to-all-start.2) | async-done | bytes 131104 | tf_op jit(solution)/shard_map/all_to_all | solution.py:12
  70.7 20.1 %while.61 = (s32[]{:T(128)}, f32[1152,256]{1,0:T(8,128)}, s32[2048]{0:T(1024)}, s32[2048]{0:T(1024)S(1)}, s32[]{:T(128)}, /*index=5*/bf16[1152,256]{1,0:T(8,128)...) while((s32[]{:T(128)}, f32[1152,256]{1,0:T(8,128)}, s32[2048]{0:T(1024)}, ...), condition=%wide.region_3.5_spmd.clone.clone, body=%wide.region_2.4_spmd.clone.clone.sunk | while | flops 606471168 | bytes 2962605 | solution.py:54
  76.3 3.8 %convolution_add_fusion.14 = f32[1152,256]{1,0:T(8,128)} fusion(f32[1152,256]{1,0:T(8,128)} %get-tuple-element.935, s32[512]{0:T(512)S(1)} %dynamic_slice.82, bf16[1152,256]{1,0:T(8,128)(2,1)S(1)} %get-tuple-element.949, s32[512]{0:T(512)S(1)} %dynamic_slice.83, pred[512]{0:T(512)(128)(4,1)S(1)} %add_compare_fusion.9, pred[]{:T(512)S(6)} %compare.13), kind=kOutput, calls=%fused_computation.19.clone.1 | convolution fusion | flops 606470144 | bytes 2953729 | tf_op jit(solution)/shard_map/while/body/eval_jaxpr/dot_general | solution.py:58
  81.6 3.8 %convolution_add_fusion.14 = f32[1152,256]{1,0:T(8,128)} fusion(f32[1152,256]{1,0:T(8,128)} %get-tuple-element.935, s32[512]{0:T(512)S(1)} %dynamic_slice.82, bf16[1152,256]{1,0:T(8,128)(2,1)S(1)} %get-tuple-element.949, s32[512]{0:T(512)S(1)} %dynamic_slice.83, pred[512]{0:T(512)(128)(4,1)S(1)} %add_compare_fusion.9, pred[]{:T(512)S(6)} %compare.13), kind=kOutput, calls=%fused_computation.19.clone.1 | convolution fusion | flops 606470144 | bytes 2953729 | tf_op jit(solution)/shard_map/while/body/eval_jaxpr/dot_general | solution.py:58
  87.0 3.8 %convolution_add_fusion.14 = f32[1152,256]{1,0:T(8,128)} fusion(f32[1152,256]{1,0:T(8,128)} %get-tuple-element.935, s32[512]{0:T(512)S(1)} %dynamic_slice.82, bf16[1152,256]{1,0:T(8,128)(2,1)S(1)} %get-tuple-element.949, s32[512]{0:T(512)S(1)} %dynamic_slice.83, pred[512]{0:T(512)(128)(4,1)S(1)} %add_compare_fusion.9, pred[]{:T(512)S(6)} %compare.13), kind=kOutput, calls=%fused_computation.19.clone.1 | convolution fusion | flops 606470144 | bytes 2953729 | tf_op jit(solution)/shard_map/while/body/eval_jaxpr/dot_general | solution.py:58
  92.3 29.0 %while.62 = (s32[]{:T(128)}, f32[1152,256]{1,0:T(8,128)}, s32[2048]{0:T(1024)S(1)}, s32[2048]{0:T(1024)}, s32[]{:T(128)}, /*index=5*/bf16[1152,256]{1,0:T(8,128)(2,1)}, s32[]{:T(128)}, s32[]{:T(128)}, s32[]{:T(128)}, s32[]{:T(128)}) while((s32[]{:T(128)}, f32[1152,256]{1,0:T(8,128)}, s32[2048]{0:T(1024)S(1)}, ...), condition=%wide.region_5.7_spmd.clone.clone, body=%wide.region_4.6_spmd.clone.clone.sunk | while | flops 606471168 | bytes 2962605 | solution.py:54
  95.5 3.7 %convolution_add_fusion.15 = f32[1152,256]{1,0:T(8,128)} fusion(f32[1152,256]{1,0:T(8,128)} %get-tuple-element.965, s32[512]{0:T(512)} %dynamic_slice.84, bf16[1152,256]{1,0:T(8,128)(2,1)} %get-tuple-element.979, s32[512]{0:T(512)} %dynamic_slice.85, pred[512]{0:T(512)(128)(4,1)} %add_compare_fusion.10, pred[]{:T(512)S(6)} %compare.14), kind=kOutput, calls=%fused_computation.29.clone.1 | convolution fusion | flops 606470144 | bytes 2953729 | tf_op jit(solution)/shard_map/while/body/eval_jaxpr/dot_general | solution.py:58
  102.5 4.1 %convolution_add_fusion.15 = f32[1152,256]{1,0:T(8,128)} fusion(f32[1152,256]{1,0:T(8,128)} %get-tuple-element.965, s32[512]{0:T(512)} %dynamic_slice.84, bf16[1152,256]{1,0:T(8,128)(2,1)} %get-tuple-element.979, s32[512]{0:T(512)} %dynamic_slice.85, pred[512]{0:T(512)(128)(4,1)} %add_compare_fusion.10, pred[]{:T(512)S(6)} %compare.14), kind=kOutput, calls=%fused_computation.29.clone.1 | convolution fusion | flops 606470144 | bytes 2953729 | tf_op jit(solution)/shard_map/while/body/eval_jaxpr/dot_general | solution.py:58
  109.8 4.1 %convolution_add_fusion.15 = f32[1152,256]{1,0:T(8,128)} fusion(f32[1152,256]{1,0:T(8,128)} %get-tuple-element.965, s32[512]{0:T(512)} %dynamic_slice.84, bf16[1152,256]{1,0:T(8,128)(2,1)} %get-tuple-element.979, s32[512]{0:T(512)} %dynamic_slice.85, pred[512]{0:T(512)(128)(4,1)} %add_compare_fusion.10, pred[]{:T(512)S(6)} %compare.14), kind=kOutput, calls=%fused_computation.29.clone.1 | convolution fusion | flops 606470144 | bytes 2953729 | tf_op jit(solution)/shard_map/while/body/eval_jaxpr/dot_general | solution.py:58
  117.1 4.1 %convolution_add_fusion.15 = f32[1152,256]{1,0:T(8,128)} fusion(f32[1152,256]{1,0:T(8,128)} %get-tuple-element.965, s32[512]{0:T(512)} %dynamic_slice.84, bf16[1152,256]{1,0:T(8,128)(2,1)} %get-tuple-element.979, s32[512]{0:T(512)} %dynamic_slice.85, pred[512]{0:T(512)(128)(4,1)} %add_compare_fusion.10, pred[]{:T(512)S(6)} %compare.14), kind=kOutput, calls=%fused_computation.29.clone.1 | convolution fusion | flops 606470144 | bytes 2953729 | tf_op jit(solution)/shard_map/while/body/eval_jaxpr/dot_general | solution.py:58
  125.1 3.5 %all-to-all-start.3 = ((f32[32,4,512]{2,1,0:T(4,128)}), f32[32,4,512]{2,1,0:T(4,128)}, u32[]{:S(2)}, u32[]{:S(2)}) async-start(f32[32,4,512]{2,1,0:T(4,128)} %reshape.107), calls=%async_computation.3 | async-start | bytes 524288 | tf_op jit(solution)/shard_map/all_to_all | solution.py:20
  130.7 8.3 %all-to-all-done.3 = f32[32,4,512]{2,1,0:T(4,128)} async-done(((f32[32,4,512]{2,1,0:T(4,128)}), f32[32,4,512]{2,1,0:T(4,128)}, u32[]{:S(2)}, u32[]{:S(2)}) %all-to-all-start.3) | async-done | bytes 262176 | tf_op jit(solution)/shard_map/all_to_all | solution.py:20
  150.8 6.4 %all-to-all-done.4 = bf16[32,4,256]{2,1,0:T(4,128)(2,1)S(1)} async-done(((bf16[32,4,256]{2,1,0:T(4,128)(2,1)}), bf16[32,4,256]{2,1,0:T(4,128)(2,1)S(1)}, u32[]{:S(2)}, u32[]{:S(2)}) %all-to-all-start.4) | async-done | bytes 65568 | tf_op jit(solution)/shard_map/all_to_all | solution.py:12
  158.0 17.9 %while.63 = (s32[]{:T(128)}, f32[1152,256]{1,0:T(8,128)S(1)}, s32[2048]{0:T(1024)S(1)}, s32[2048]{0:T(1024)}, s32[]{:T(128)}, /*index=5*/bf16[1152,256]{1,0:T(8,...) while((s32[]{:T(128)}, f32[1152,256]{1,0:T(8,128)S(1)}, s32[2048]{0:T(1024)S(1)}, ...), condition=%wide.region_7.9_spmd.clone.clone, body=%wide.region_6.8_spmd.clone.clone.sunk | while | flops 606471168 | bytes 2962605 | solution.py:54
  159.5 3.0 convolution_add_fusion.16
  164.0 3.0 convolution_add_fusion.16
  168.5 3.0 convolution_add_fusion.16
  173.0 3.0 convolution_add_fusion.16
  180.4 40.7 %psum.39 = f32[256]{0:T(256)S(1)} all-reduce(f32[256]{0:T(256)S(1)} %copy-done.19), channel_id=1, replica_groups=mesh['dom'=8,'sub'=4] {'dom','sub'}, use_global_device_ids=true, to_apply=%region_13.15 | all-reduce | flops 256 | bytes 2048 | tf_op jit(solution)/shard_map/psum | solution.py:128
  223.5 94.9 %all-reduce.3.cloned.1.call-done = (f32[1,256,256]{1,2,0:T(8,128)}, f32[1,256,256]{1,2,0:T(8,128)}, f32[1,256,256]{1,2,0:T(8,128)}, f32[1,256,256]{1,2,0:T(8,128)}) async-done(((f32[1,256,256]{1,2,0:T(8,128)}, f32[1,256,256]{1,2,0:T(8,128)}, f32[1,256,256]{1,2,0:T(8,128)}, f32[1,256,256]{1,2,0:T(8,128)}), (f32[1,256,256]{1,2,0:T(8,128)}, f32[1,256,256]{1,2,0:T(8,128)}, f32[1,256,256]{1,2,0:T(8,128)}, ...) | async-done | bytes 1048592 | tf_op jit(solution)/shard_map/psum | solution.py:128
  (164 shorter events, 91.9 us)
Async XLA Ops:
  7.2 37.8 %copy-start = (bf16[1024,256]{1,0:T(8,128)(2,1)S(1)}, bf16[1024,256]{1,0:T(8,128)(2,1)}, u32[]{:S(2)}) copy-start(bf16[1024,256]{1,0:T(8,128)(2,1)} %param.23) | copy-start | bytes 1572868
  7.2 14.7 %copy-start.1 = (bf16[1024,256]{1,0:T(8,128)(2,1)S(1)}, bf16[1024,256]{1,0:T(8,128)(2,1)}, u32[]{:S(2)}) copy-start(bf16[1024,256]{1,0:T(8,128)(2,1)} %param.22) | copy-start | bytes 1572868
  7.2 14.7 %copy-start.7 = (bf16[256,256]{1,0:T(8,128)(2,1)S(1)}, bf16[256,256]{1,0:T(8,128)(2,1)}, u32[]{:S(2)}) copy-start(bf16[256,256]{1,0:T(8,128)(2,1)} %param.24) | copy-start | bytes 393220
  12.2 10.9 %copy-start.18 = (s32[1024]{0:T(1024)S(1)}, s32[1024]{0:T(1024)}, u32[]{:S(2)}) copy-start(s32[1024]{0:T(1024)} %param.29) | copy-start | bytes 12292
  12.4 15.5 %copy-start.13 = (pred[32,4]{1,0:T(8,128)(4,1)}, pred[32,4]{1,0:T(8,128)(4,1)S(1)}, u32[]{:S(2)}) copy-start(pred[32,4]{1,0:T(8,128)(4,1)S(1)} %copy.27) | copy-start | bytes 388
  13.1 14.7 %all-to-all-start = ((bf16[32,4,256]{2,1,0:T(4,128)(2,1)}), bf16[32,4,256]{2,1,0:T(4,128)(2,1)S(1)}, u32[]{:S(2)}, u32[]{:S(2)}) async-start(bf16[32,4,256]{2,1,0:T(4,128)(2,1)} %broadcast_select_fusion.2), calls=%async_computation | async-start | bytes 131072 | tf_op jit(solution)/shard_map/all_to_all | solution.py:12
  21.8 6.0 %copy-start.8 = (s32[1,2048]{1,0:T(1,128)S(1)}, s32[1,2048]{1,0:T(1,128)}, u32[]{:S(2)}) copy-start(s32[1,2048]{1,0:T(1,128)} %param.31) | copy-start | bytes 24580
  27.9 17.0 %copy-start.9 = (bf16[256,256]{1,0:T(8,128)(2,1)S(1)}, bf16[256,256]{1,0:T(8,128)(2,1)}, u32[]{:S(2)}) copy-start(bf16[256,256]{1,0:T(8,128)(2,1)} %param.28) | copy-start | bytes 393220
  41.6 11.6 %copy-start.16 = (s32[128]{0:T(128)S(1)}, s32[128]{0:T(128)}, u32[]{:S(2)}) copy-start(s32[128]{0:T(128)} %eq.286) | copy-start | bytes 1540
  42.3 10.8 %all-to-all-start.1 = ((f32[32,4,256]{2,1,0:T(4,128)}), f32[32,4,256]{2,1,0:T(4,128)S(1)}, u32[]{:S(2)}, u32[]{:S(2)}) async-start(f32[32,4,256]{2,1,0:T(4,128)} %reshape.104), calls=%async_computation.1 | async-start | bytes 262144 | tf_op jit(solution)/shard_map/all_to_all | solution.py:20
  45.3 8.5 %copy-start.10 = (bf16[256,256]{1,0:T(8,128)(2,1)S(1)}, bf16[256,256]{1,0:T(8,128)(2,1)}, u32[]{:S(2)}) copy-start(bf16[256,256]{1,0:T(8,128)(2,1)} %param.25) | copy-start | bytes 393220
  54.4 2.1 copy-start.3
  56.5 13.2 %copy-start.2 = (bf16[1024,256]{1,0:T(8,128)(2,1)}, bf16[1024,256]{1,0:T(8,128)(2,1)S(1)}, u32[]{:S(2)}) copy-start(bf16[1024,256]{1,0:T(8,128)(2,1)S(1)} %get-tuple-element.740) | copy-start | bytes 1572868
  56.6 1.5 copy-start.14
  58.9 10.8 %all-to-all-start.2 = ((bf16[32,4,512]{2,1,0:T(4,128)(2,1)}), bf16[32,4,512]{2,1,0:T(4,128)(2,1)S(1)}, u32[]{:S(2)}, u32[]{:S(2)}) async-start(bf16[32,4,512]{2,1,0:T(4,128)(2,1)} %broadcast_select_fusion), calls=%async_computation.2 | async-start | bytes 262144 | tf_op jit(solution)/shard_map/all_to_all | solution.py:12
  125.1 13.9 %all-to-all-start.3 = ((f32[32,4,512]{2,1,0:T(4,128)}), f32[32,4,512]{2,1,0:T(4,128)}, u32[]{:S(2)}, u32[]{:S(2)}) async-start(f32[32,4,512]{2,1,0:T(4,128)} %reshape.107), calls=%async_computation.3 | async-start | bytes 524288 | tf_op jit(solution)/shard_map/all_to_all | solution.py:20
  142.7 1.3 copy-start.20
  142.7 1.3 copy-start.21
  147.1 10.0 %all-to-all-start.4 = ((bf16[32,4,256]{2,1,0:T(4,128)(2,1)}), bf16[32,4,256]{2,1,0:T(4,128)(2,1)S(1)}, u32[]{:S(2)}, u32[]{:S(2)}) async-start(bf16[32,4,256]{2,1,0:T(4,128)(2,1)} %broadcast_select_fusion.1), calls=%async_computation.4 | async-start | bytes 131072 | tf_op jit(solution)/shard_map/all_to_all | solution.py:12
  149.7 8.3 %copy-start.5 = (f32[1152,256]{1,0:T(8,128)S(1)}, f32[1152,256]{1,0:T(8,128)}, u32[]{:S(2)}) copy-start(f32[1152,256]{1,0:T(8,128)} %custom-call.3) | copy-start | bytes 3538948
  158.0 21.3 %copy-start.4 = (bf16[1024,256]{1,0:T(8,128)(2,1)S(1)}, bf16[1024,256]{1,0:T(8,128)(2,1)}, u32[]{:S(2)}) copy-start(bf16[1024,256]{1,0:T(8,128)(2,1)} %copy-done.3) | copy-start | bytes 1572868
  176.7 45.0 %all-to-all-start.5 = ((f32[32,4,256]{2,1,0:T(4,128)}), f32[32,4,256]{2,1,0:T(4,128)S(1)}, u32[]{:S(2)}, u32[]{:S(2)}) async-start(f32[32,4,256]{2,1,0:T(4,128)} %reshape.110), calls=%async_computation.5 | async-start | bytes 262144 | tf_op jit(solution)/shard_map/all_to_all | solution.py:20
  179.3 42.5 %copy-start.17 = (s32[128]{0:T(128)S(1)}, s32[128]{0:T(128)}, u32[]{:S(2)}) copy-start(s32[128]{0:T(128)} %eq.286) | copy-start | bytes 1540
  179.3 139.1 %all-reduce.3.cloned.1.call-start = ((), (), s32[]{:S(2)}) async-start(), calls=%async_computation.6 | async-start | bytes 2097152 | tf_op jit(solution)/shard_map/psum | solution.py:128
  (5 other events, 5.4 us)
Sparse Core Ops, SparseCore 0:
  186.2 132.1 all-reduce.2
where the time goes:
time: 330 us; the launch traced here: 328 us
  waiting for transfers between devices  130 us (39%)
  matrix products  64.2 us (19%)
  blocking collectives  40.7 us (12%)
  local copies, waits for them, and re-layouts  35.9 us (11%)
  starting transfers between devices  21.1 us (6%)
  other arithmetic  20.7 us (6%)
  between operations  14.5 us (4%)
    psum x1, waiting for transfers between devices, shards(): lax.psum((early_self, early_nbr, early_bias, late_self, late_nbr), ('dom'...  94.9 us
    dot_general x20, matrix products, tdot(): lax.dot_general(left, right, (((0,), (0,)), ((), ())), preferred_element_...  54.9 us
    psum x1, blocking collectives, shards(): lax.psum((early_self, early_nbr, early_bias, late_self, late_nbr), ('dom'...  40.7 us
    all_to_all x3, waiting for transfers between devices, to_mirrors(): lax.all_to_all(picked_rows, ('dom', 'sub'), split_axis=0, concat_axis=0,...  19.2 us
    all_to_all x3, waiting for transfers between devices, to_masters(): lax.all_to_all(sectioned_rows, ('dom', 'sub'), split_axis=0, concat_axis=...  16.1 us
    lt x16, other arithmetic, one_block(): jnp.arange(block_rows, dtype=jnp.int32) + offset < live_count  12.7 us
    all_to_all x3, starting transfers between devices, to_mirrors(): lax.all_to_all(picked_rows, ('dom', 'sub'), split_axis=0, concat_axis=0,...  12.4 us
    dynamic_slice x16, local copies, waits for them, and re-layouts, one_block(): into_part = lax.dynamic_slice_in_dim(into_slot, offset, block_rows)  9.1 us
  transfers between devices with their start and end apart: 7, of which 6 were waited for; matrix products, arithmetic and copies ran while one was open for 3% of the time, Pallas kernels for 0%

commit v1 on v0

v1 whole, which is shorter than its diff:
```python
import jax
import jax.numpy as jnp
from jax import lax
from jax.sharding import PartitionSpec as P

AXES = ("dom", "sub")


def tdot(left, right):
    return lax.dot_general(
        left, right, (((0,), (0,)), ((), ())), preferred_element_type=jnp.float32
    )


def dot_transposed(left, right):
    return lax.dot_general(
        left, right, (((1,), (1,)), ((), ())), preferred_element_type=jnp.float32
    )


def dot(left, right):
    return jnp.dot(left, right, preferred_element_type=jnp.float32)


def exchange(rows):
    return lax.all_to_all(rows, AXES, split_axis=0, concat_axis=0, tiled=True)


def shards(
    features,
    cotangent,
    w_self_one,
    w_nbr_one,
    bias_one,
    w_self_two,
    w_nbr_two,
    in_count,
    send_list,
    src_slot,
    dst_slot,
    edge_count,
):
    node_dev, width = features.shape
    devices = lax.axis_size("dom") * lax.axis_size("sub")
    per_peer = send_list.shape[2]
    mirrors = devices * per_peer
    slots = node_dev + mirrors
    edges = src_slot.shape[1]
    core = lax.axis_index("sub") % 2
    swap = [(i, i ^ 1) for i in range(devices)]
    bf16 = jnp.bfloat16
    f32 = jnp.float32

    inverse = (1.0 / jnp.maximum(in_count, 1).astype(f32))[:, None]
    owners = send_list[0].reshape(-1)
    placing = (jnp.arange(node_dev, dtype=jnp.int32)[:, None] == owners[None, :]).astype(bf16)

    scaled = (cotangent.astype(f32) * inverse).astype(bf16)
    table = jnp.concatenate([features, scaled], axis=1)
    picked = tdot(placing, table).astype(bf16)
    mirrored = exchange(picked.reshape(devices, per_peer, 2 * width)).reshape(mirrors, 2 * width)

    live = jnp.arange(edges, dtype=jnp.int32) < edge_count[0]
    slot_ids = jnp.arange(slots, dtype=jnp.int32)[:, None]
    from_hot = (jnp.where(live, src_slot[0], -1)[None, :] == slot_ids).astype(bf16)
    into_hot = (dst_slot[0][None, :] == slot_ids).astype(bf16)
    counts = dot_transposed(into_hot, from_hot).astype(bf16)

    forward = dot(counts[:, :node_dev], features) + dot(counts[:, node_dev:], mirrored[:, :width])
    backward = tdot(counts[:node_dev], scaled) + tdot(counts[node_dev:], mirrored[:, width:])
    partial_sums = jnp.concatenate([forward[node_dev:], backward[node_dev:]], axis=1).astype(bf16)
    returned = exchange(partial_sums.reshape(devices, per_peer, 2 * width)).reshape(
        mirrors, 2 * width
    )
    placed = dot(placing, returned)
    mean_one = ((forward[:node_dev] + placed[:, :width]) * inverse).astype(bf16)
    pulled = (backward[:node_dev] + placed[:, width:]).astype(bf16)

    z_one = dot(features, w_self_one) + dot(mean_one, w_nbr_one) + bias_one
    sigmoid = jax.nn.sigmoid(z_one)
    h_one = (z_one * sigmoid).astype(bf16)
    grad_h_one = dot_transposed(cotangent, w_self_two) + dot_transposed(pulled, w_nbr_two)
    grad_z_one = (grad_h_one * (sigmoid * (1.0 + z_one * (1.0 - sigmoid)))).astype(bf16)
    message_one = (dot_transposed(grad_z_one, w_nbr_one) * inverse).astype(bf16)

    weights = jnp.concatenate(
        [
            tdot(features, grad_z_one),
            tdot(mean_one, grad_z_one),
            tdot(h_one, cotangent),
            tdot(h_one, pulled),
        ],
        axis=0,
    )
    half = weights.shape[0] // 2
    chunk = half // devices
    sent_half = lax.dynamic_slice_in_dim(weights, (1 - core) * half, half).astype(bf16)
    own_half = lax.dynamic_slice_in_dim(weights, core * half, half)
    chip_half = (own_half + lax.ppermute(sent_half, AXES, swap).astype(f32)).astype(bf16)
    bias_sum = jnp.sum(grad_z_one.astype(f32), axis=0, keepdims=True)
    bias_high = bias_sum.astype(bf16)
    bias_low = (bias_sum - bias_high.astype(f32)).astype(bf16)
    bias_rows = jnp.concatenate([bias_high, bias_low, jnp.zeros((2, width), bf16)], axis=0)

    picked = tdot(placing, message_one).astype(bf16)
    payload = jnp.concatenate(
        [
            picked.reshape(devices, per_peer, width),
            jnp.broadcast_to(bias_rows[None], (devices, 4, width)),
            chip_half.reshape(devices, chunk, width),
        ],
        axis=1,
    )
    payload = exchange(payload)
    mirrored = payload[:, :per_peer].reshape(mirrors, width)
    bias_parts = payload[:, per_peer : per_peer + 2].astype(f32)
    chunk_parts = payload[:, per_peer + 4 :].astype(f32)

    norm_factor = f32(node_dev * devices) ** (-0.5)
    grad_bias = jnp.sum(bias_parts, axis=(0, 1)) * norm_factor
    owned = (
        jnp.sum(chunk_parts.reshape(devices // 2, 2, chunk, width), axis=0) * norm_factor
    ).astype(bf16)

    backward = tdot(counts[:node_dev], message_one) + tdot(counts[node_dev:], mirrored)
    payload = jnp.concatenate(
        [
            backward[node_dev:].astype(bf16).reshape(devices, per_peer, width),
            jnp.zeros((devices, 4, width), bf16),
            jnp.broadcast_to(owned[None], (devices // 2, 2, chunk, width)).reshape(
                devices, chunk, width
            ),
        ],
        axis=1,
    )
    payload = exchange(payload)
    returned = payload[:, :per_peer].reshape(mirrors, width)
    mine = payload[:, per_peer + 4 :].reshape(half, width)
    other = lax.ppermute(mine, AXES, swap)
    first = jnp.where(core == 0, mine, other)
    second = jnp.where(core == 0, other, mine)
    grad_weights = (
        jnp.concatenate([first, second], axis=0).astype(f32).reshape(4, width, width)
    )
    grad_features = (
        dot_transposed(grad_z_one, w_self_one) + backward[:node_dev] + dot(placing, returned)
    ).astype(bf16)
    return (grad_features, grad_weights, grad_bias)


def solution(mesh):
    by_device = P(AXES)
    return jax.shard_map(
        shards,
        mesh=mesh,
        in_specs=(
            P(AXES, None),
            P(AXES, None),
            P(),
            P(),
            P(),
            P(),
            P(),
            by_device,
            P(AXES, None, None),
            P(AXES, None),
            P(AXES, None),
            by_device,
        ),
        out_specs=(P(AXES, None), P(), P()),
        check_vma=False,
    )
```

time: 330 us -> 90.1 us (0.27)
  waiting for transfers between devices: 130 us -> 30.3 us
  blocking collectives: 40.7 us -> 0 us
  matrix products: 64.2 us -> 26.1 us
  local copies, waits for them, and re-layouts: 35.9 us -> 5.3 us
  other arithmetic: 20.7 us -> 7.02 us
  between operations: 14.5 us -> 1.74 us
    psum x1 -> x0, waiting for transfers between devices: 94.9 us -> none  [shards(): lax.psum((early_self, early_nbr, early_bias, late_self, late_nbr), ('dom'...]
    dot_general x20 -> x10, matrix products: 54.9 us -> 9.15 us  [tdot(): lax.dot_general(left, right, (((0,), (0,)), ((), ())), preferred_element_...]
    psum x1 -> x0, blocking collectives: 40.7 us -> none  [shards(): lax.psum((early_self, early_nbr, early_bias, late_self, late_nbr), ('dom'...]
    dynamic_slice x32 -> x0, local copies, waits for them, and re-layouts: 18.2 us -> none  [the longest x16 9.1 us: one_block(): into_part = lax.dynamic_slice_in_dim(into_slot, offset, block_rows)]
    lt x16 -> x0, other arithmetic: 12.7 us -> none  [one_block(): jnp.arange(block_rows, dtype=jnp.int32) + offset < live_count]
    dot_general x4 -> x5, matrix products: 2.91 us -> 10.2 us  [dot_transposed(): lax.dot_general(left, right, (((1,), (1,)), ((), ())), preferred_element_...]
    all_to_all x6 -> x4, waiting for transfers between devices: 35.4 us -> 29.5 us  [exchange(): return lax.all_to_all(rows, AXES, split_axis=0, concat_axis=0, tiled=True)]
    select_n x5 -> x2, other arithmetic: 3.73 us -> 0.06 us  [the longest x1 0.05 us: shards(): first = jnp.where(core == 0, mine, other)]
  transfers between devices with their start and end apart: 7 -> 6, of which waited for: 6 -> 5; matrix products, arithmetic and copies ran while one was open for 3% -> 20% of each run, Pallas kernels for 0% -> 0%
where the time goes in v1:
time: 90.1 us; the launch traced here: 89.3 us
  waiting for transfers between devices  30.3 us (34%)
  matrix products  26.1 us (29%)
  starting transfers between devices  18.9 us (21%)
  other arithmetic  7.02 us (8%)
  local copies, waits for them, and re-layouts  5.3 us (6%)
  between operations  1.74 us (2%)
    all_to_all x4, waiting for transfers between devices, exchange(): return lax.all_to_all(rows, AXES, split_axis=0, concat_axis=0, tiled=True)  29.5 us
    all_to_all x4, starting transfers between devices, exchange(): return lax.all_to_all(rows, AXES, split_axis=0, concat_axis=0, tiled=True)  18.5 us
    dot_general x5, matrix products, dot_transposed(): lax.dot_general(left, right, (((1,), (1,)), ((), ())), preferred_element_...  10.2 us
    dot_general x10, matrix products, tdot(): lax.dot_general(left, right, (((0,), (0,)), ((), ())), preferred_element_...  9.15 us
    dot_general x6, matrix products, dot(): return jnp.dot(left, right, preferred_element_type=jnp.float32)  6.76 us
    unnamed x31, local copies, waits for them, and re-layouts  3.33 us
  transfers between devices with their start and end apart: 6, of which 5 were waited for; matrix products, arithmetic and copies ran while one was open for 20% of the time, Pallas kernels for 0%

profile of v1, /device:TPU:0, one launch (start us, length us, event | category | flops | bytes accessed | tf_op | source)
XLA Modules:
  0.0 89.3 jit_solution(15264461388370323438)
XLA Ops:
  1.4 0.8 copy.16
  2.3 1.2 %multiply_convert_fusion.1 = bf16[1024,256]{1,0:T(8,128)(2,1)S(1)} fusion(bf16[1024,256]{1,0:T(8,128)(2,1)} %param.13, f32[1024]{0:T(1024)S(1)} %convert_divide_fusion), kind=kLoop, calls=%fused_computation.40 | loop fusion | flops 786432 | bytes 1052672 | tf_op jit(solution)/shard_map/convert_element_type | solution.py:58
  3.5 1.4 %convolution_convert_fusion = bf16[128,512]{1,0:T(8,128)(2,1)S(1)} fusion(bf16[1024,256]{1,0:T(8,128)(2,1)S(1)} %multiply_convert_fusion.1, bf16[1024,256]{1,0:T(8,128)(2,1)} %param.12, s32[128]{0:T(128)S(1)} %eq.60), kind=kOutput, calls=%fused_computation.26 | convolution fusion | flops 136511488 | bytes 1180160 | tf_op jit(solution)/shard_map/dot_general | solution.py:10
  5.6 7.3 %all-to-all-start = ((bf16[32,4,512]{2,1,0:T(4,128)(2,1)}), bf16[32,4,512]{2,1,0:T(4,128)(2,1)S(1)}, u32[]{:S(2)}, u32[]{:S(2)}) async-start(bf16[32,4,512]{2,1,0:T(4,128)(2,1)} %reshape.90), calls=%async_computation | async-start | bytes 262144 | tf_op jit(solution)/shard_map/all_to_all | solution.py:26
  13.6 7.7 %fusion.1 = bf16[1152,1152]{1,0:T(8,128)(2,1)S(1)} fusion(s32[2048]{0:T(1024)S(1)} %bitcast.48, s32[2048]{0:T(1024)S(1)} %bitcast.51), kind=kOutput, calls=%fused_computation.3 | convolution fusion | flops 5441863680 | bytes 2670592 | tf_op jit(solution)/shard_map/dot_general | solution.py:16
  21.3 0.8 fusion.8
  22.7 1.8 %fusion.4 = f32[1152,256]{1,0:T(8,128)} fusion(bf16[1024,256]{1,0:T(8,128)(2,1)S(1)} %copy-done.2, bf16[1152,1152]{1,0:T(8,128)(2,1)S(1)} %fusion.1), kind=kOutput, calls=%fused_computation.9 | convolution fusion | flops 603979776 | bytes 4063232 | tf_op jit(solution)/shard_map/dot_general | solution.py:22
  24.6 1.3 %fusion.33 = f32[1024,256]{1,0:T(8,128)} fusion(bf16[1024,256]{1,0:T(8,128)(2,1)S(1)} %copy-done.2, bf16[256,256]{1,0:T(8,128)(2,1)S(1)} %copy-done.7), kind=kOutput, calls=%fused_computation.73 | convolution fusion | flops 134217728 | bytes 1703936 | tf_op jit(solution)/shard_map/dot_general | solution.py:22
  25.9 1.3 %convolution_add_fusion.2 = f32[1152,256]{1,0:T(8,128)S(1)} fusion(f32[1152,256]{1,0:T(8,128)S(1)} %fusion.8, bf16[1152,1152]{1,0:T(8,128)(2,1)} %copy-done.9, bf16[128,512]{1,0:T(8,128)(2,1)S(1)} %reshape.91), kind=kOutput, calls=%fused_computation.8 | convolution fusion | flops 75792384 | bytes 2719744 | tf_op jit(solution)/shard_map/dot_general | solution.py:10
  27.3 1.7 %convolution_add_fusion.1 = f32[1152,256]{1,0:T(8,128)S(1)} fusion(f32[1152,256]{1,0:T(8,128)} %fusion.4, bf16[1152,1152]{1,0:T(8,128)(2,1)} %copy-done.9, bf16[128,512]{1,0:T(8,128)(2,1)S(1)} %reshape.91), kind=kOutput, calls=%fused_computation.7 | convolution fusion | flops 75792384 | bytes 2719744 | tf_op jit(solution)/shard_map/dot_general | solution.py:22
  29.8 5.8 %all-to-all-start.1 = ((bf16[32,4,512]{2,1,0:T(4,128)(2,1)}), bf16[32,4,512]{2,1,0:T(4,128)(2,1)S(1)}, u32[]{:S(2)}, u32[]{:S(2)}) async-start(bf16[32,4,512]{2,1,0:T(4,128)(2,1)} %pad_maximum_fusion.4), calls=%async_computation.1 | async-start | bytes 262144 | tf_op jit(solution)/shard_map/all_to_all | solution.py:26
  35.6 1.3 %fusion.32 = f32[1024,256]{1,0:T(8,128)} fusion(bf16[1024,256]{1,0:T(8,128)(2,1)S(1)} %copy-done.1, bf16[256,256]{1,0:T(8,128)(2,1)S(1)} %copy-done.10), kind=kOutput, calls=%fused_computation.72 | convolution fusion | flops 134217728 | bytes 1703936 | tf_op jit(solution)/shard_map/dot_general | solution.py:16
  36.9 6.9 %all-to-all-done.1 = bf16[32,4,512]{2,1,0:T(4,128)(2,1)S(1)} async-done(((bf16[32,4,512]{2,1,0:T(4,128)(2,1)}), bf16[32,4,512]{2,1,0:T(4,128)(2,1)S(1)}, u32[]{:S(2)}, u32[]{:S(2)}) %all-to-all-start.1) | async-done | bytes 131104 | tf_op jit(solution)/shard_map/all_to_all | solution.py:26
  46.0 0.7 copy-done.5
  51.0 0.9 pad_maximum_fusion.2
  51.9 2.8 %all-to-all-start.2 = ((bf16[32,24,256]{2,1,0:T(8,128)(2,1)}), bf16[32,24,256]{2,1,0:T(8,128)(2,1)S(1)}, u32[]{:S(2)}, u32[]{:S(2)}) async-start(bf16[32,24,256]{2,1,0:T(8,128)(2,1)} %pad_maximum_fusion.2), calls=%async_computation.2 | async-start | bytes 786432 | tf_op jit(solution)/shard_map/all_to_all | solution.py:26
  54.7 2.6 %fusion.6 = f32[1152,256]{1,0:T(8,128)S(1)} fusion(bf16[1024,256]{1,0:T(8,128)(2,1)} %copy-done.6, bf16[1152,1152]{1,0:T(8,128)(2,1)} %copy-done.9), kind=kOutput, calls=%fused_computation.11 | convolution fusion | flops 603979776 | bytes 4063232 | tf_op jit(solution)/shard_map/dot_general | solution.py:10
  57.3 10.3 %all-to-all-done.2 = bf16[32,24,256]{2,1,0:T(8,128)(2,1)S(1)} async-done(((bf16[32,24,256]{2,1,0:T(8,128)(2,1)}), bf16[32,24,256]{2,1,0:T(8,128)(2,1)S(1)}, u32[]{:S(2)}, u32[]{:S(2)}) %all-to-all-start.2) | async-done | bytes 393248 | tf_op jit(solution)/shard_map/all_to_all | solution.py:26
  68.3 1.3 %convolution_add_fusion = f32[1152,256]{1,0:T(8,128)S(1)} fusion(f32[1152,256]{1,0:T(8,128)S(1)} %fusion.6, bf16[128,256]{1,0:T(8,128)(2,1)} %reshape.95, bf16[1152,1152]{1,0:T(8,128)(2,1)} %copy-done.9), kind=kOutput, calls=%fused_computation.6 | convolution fusion | flops 75792384 | bytes 2719744 | tf_op jit(solution)/shard_map/dot_general | solution.py:10
  69.8 0.9 %pad_maximum_fusion.3 = bf16[32,24,256]{2,1,0:T(8,128)(2,1)} fusion(bf16[32,16,256]{2,1,0:T(8,128)(2,1)S(1)} %bitcast.45, bf16[32,4,256]{2,1,0:T(4,128)(2,1)S(1)} %reshape.96, bf16[24]{0:T(256)(128)(2,1)S(1)} %pad.3.clone), kind=kLoop, calls=%fused_computation.48 | loop fusion | flops 1179648 | bytes 720944 | tf_op jit(solution)/shard_map/concatenate | solution.py:126
  70.8 2.6 %all-to-all-start.3 = ((bf16[32,24,256]{2,1,0:T(8,128)(2,1)}), bf16[32,24,256]{2,1,0:T(8,128)(2,1)S(1)}, u32[]{:S(2)}, u32[]{:S(2)}) async-start(bf16[32,24,256]{2,1,0:T(8,128)(2,1)} %pad_maximum_fusion.3), calls=%async_computation.3 | async-start | bytes 786432 | tf_op jit(solution)/shard_map/all_to_all | solution.py:26
  74.3 12.2 %all-to-all-done.3 = bf16[32,24,256]{2,1,0:T(8,128)(2,1)S(1)} async-done(((bf16[32,24,256]{2,1,0:T(8,128)(2,1)}), bf16[32,24,256]{2,1,0:T(8,128)(2,1)S(1)}, u32[]{:S(2)}, u32[]{:S(2)}) %all-to-all-start.3) | async-done | bytes 393248 | tf_op jit(solution)/shard_map/all_to_all | solution.py:26
  86.7 1.1 %fusion.13 = bf16[1024,256]{1,0:T(8,128)(2,1)} fusion(f32[1024,256]{1,0:T(8,128)S(1)} %convolution_add_fusion.4, bf16[128,256]{1,0:T(8,128)(2,1)S(1)} %reshape.100, s32[128]{0:T(128)S(1)} %eq.60), kind=kOutput, calls=%fused_computation.23 | convolution fusion | flops 67764224 | bytes 1638912 | tf_op jit(solution)/shard_map/dot_general | solution.py:22
  88.3 1.1 %convert.19 = f32[4,256,256]{2,1,0:T(8,128)} convert(bf16[4,256,256]{2,1,0:T(8,128)(2,1)S(1)} %bitcast.43) | non-fusion elementwise | flops 262144 | bytes 1572864 | tf_op jit(solution)/shard_map/convert_element_type | solution.py:143
  (83 shorter events, 11.8 us)
Async XLA Ops:
  0.6 44.2 %copy-start = (bf16[256,256]{1,0:T(8,128)(2,1)S(1)}, bf16[256,256]{1,0:T(8,128)(2,1)}, u32[]{:S(2)}) copy-start(bf16[256,256]{1,0:T(8,128)(2,1)} %param.15) | copy-start | bytes 393220
  0.6 12.9 %copy-start.11 = (s32[1,2048]{1,0:T(1,128)S(1)}, s32[1,2048]{1,0:T(1,128)}, u32[]{:S(2)}) copy-start(s32[1,2048]{1,0:T(1,128)} %param.21) | copy-start | bytes 24580
  0.7 12.9 %copy-start.13 = (s32[1,2048]{1,0:T(1,128)S(1)}, s32[1,2048]{1,0:T(1,128)}, u32[]{:S(2)}) copy-start(s32[1,2048]{1,0:T(1,128)} %param.22) | copy-start | bytes 24580
  5.6 20.3 %all-to-all-start = ((bf16[32,4,512]{2,1,0:T(4,128)(2,1)}), bf16[32,4,512]{2,1,0:T(4,128)(2,1)S(1)}, u32[]{:S(2)}, u32[]{:S(2)}) async-start(bf16[32,4,512]{2,1,0:T(4,128)(2,1)} %reshape.90), calls=%async_computation | async-start | bytes 262144 | tf_op jit(solution)/shard_map/all_to_all | solution.py:26
  21.3 3.2 %copy-start.9 = (bf16[1152,1152]{1,0:T(8,128)(2,1)}, bf16[1152,1152]{1,0:T(8,128)(2,1)S(1)}, u32[]{:S(2)}) copy-start(bf16[1152,1152]{1,0:T(8,128)(2,1)S(1)} %fusion.1) | copy-start | bytes 7962628
  21.3 1.4 %copy-start.2 = (bf16[1024,256]{1,0:T(8,128)(2,1)S(1)}, bf16[1024,256]{1,0:T(8,128)(2,1)}, u32[]{:S(2)}) copy-start(bf16[1024,256]{1,0:T(8,128)(2,1)} %param.12) | copy-start | bytes 1572868
  22.7 1.9 %copy-start.7 = (bf16[256,256]{1,0:T(8,128)(2,1)S(1)}, bf16[256,256]{1,0:T(8,128)(2,1)}, u32[]{:S(2)}) copy-start(bf16[256,256]{1,0:T(8,128)(2,1)} %param.14) | copy-start | bytes 393220
  27.2 8.4 %copy-start.1 = (bf16[1024,256]{1,0:T(8,128)(2,1)S(1)}, bf16[1024,256]{1,0:T(8,128)(2,1)}, u32[]{:S(2)}) copy-start(bf16[1024,256]{1,0:T(8,128)(2,1)} %param.13) | copy-start | bytes 1572868
  27.2 8.4 %copy-start.10 = (bf16[256,256]{1,0:T(8,128)(2,1)S(1)}, bf16[256,256]{1,0:T(8,128)(2,1)}, u32[]{:S(2)}) copy-start(bf16[256,256]{1,0:T(8,128)(2,1)} %param.17) | copy-start | bytes 393220
  29.8 14.1 %all-to-all-start.1 = ((bf16[32,4,512]{2,1,0:T(4,128)(2,1)}), bf16[32,4,512]{2,1,0:T(4,128)(2,1)S(1)}, u32[]{:S(2)}, u32[]{:S(2)}) async-start(bf16[32,4,512]{2,1,0:T(4,128)(2,1)} %pad_maximum_fusion.4), calls=%async_computation.1 | async-start | bytes 262144 | tf_op jit(solution)/shard_map/all_to_all | solution.py:26
  44.3 1.2 %copy-start.4 = (f32[1024,256]{1,0:T(8,128)S(1)}, f32[1024,256]{1,0:T(8,128)}, u32[]{:S(2)}) copy-start(f32[1024,256]{1,0:T(8,128)} %fusion.33) | copy-start | bytes 3145732
  44.3 1.2 %copy-start.14 = (f32[256]{0:T(256)S(1)}, f32[256]{0:T(256)}, u32[]{:S(2)}) copy-start(f32[256]{0:T(256)} %param.16) | copy-start | bytes 3076
  45.5 1.2 %copy-start.5 = (f32[1024,256]{1,0:T(8,128)S(1)}, f32[1024,256]{1,0:T(8,128)}, u32[]{:S(2)}) copy-start(f32[1024,256]{1,0:T(8,128)} %fusion.32) | copy-start | bytes 3145732
  45.5 1.2 %copy-start.12 = (bf16[256,256]{1,0:T(8,128)(2,1)S(1)}, bf16[256,256]{1,0:T(8,128)(2,1)}, u32[]{:S(2)}) copy-start(bf16[256,256]{1,0:T(8,128)(2,1)} %param.18) | copy-start | bytes 393220
  46.8 1.0 %copy-start.3 = (bf16[1024,256]{1,0:T(8,128)(2,1)S(1)}, bf16[1024,256]{1,0:T(8,128)(2,1)}, u32[]{:S(2)}) copy-start(bf16[1024,256]{1,0:T(8,128)(2,1)} %param.12) | copy-start | bytes 1572868
  49.2 0.8 copy-start.6
  49.3 1.6 %collective-permute-start = (bf16[512,256]{1,0:T(8,128)(2,1)S(1)}, bf16[512,256]{1,0:T(8,128)(2,1)S(1)}, u32[]{:S(2)}, u32[]{:S(2)}) collective-permute-start(bf16[512,256]{1,0:T(8,128)(2,1)S(1)} %dynamic-slice_convert_fusion), channel_id=1, source_target_pairs={{0,1},{1,0},{2,3},{3,2},{4,5},{5,4},{6,7},{7,6},{8,9},{9,8},{10,11... | collective-permute-start | bytes 786440 | tf_op jit(solution)/shard_map/ppermute | solution.py:99
  51.9 15.8 %all-to-all-start.2 = ((bf16[32,24,256]{2,1,0:T(8,128)(2,1)}), bf16[32,24,256]{2,1,0:T(8,128)(2,1)S(1)}, u32[]{:S(2)}, u32[]{:S(2)}) async-start(bf16[32,24,256]{2,1,0:T(8,128)(2,1)} %pad_maximum_fusion.2), calls=%async_computation.2 | async-start | bytes 786432 | tf_op jit(solution)/shard_map/all_to_all | solution.py:26
  68.3 5.7 %copy-start.8 = (bf16[256,256]{1,0:T(8,128)(2,1)S(1)}, bf16[256,256]{1,0:T(8,128)(2,1)}, u32[]{:S(2)}) copy-start(bf16[256,256]{1,0:T(8,128)(2,1)} %param.14) | copy-start | bytes 393220
  70.8 15.8 %all-to-all-start.3 = ((bf16[32,24,256]{2,1,0:T(8,128)(2,1)}), bf16[32,24,256]{2,1,0:T(8,128)(2,1)S(1)}, u32[]{:S(2)}, u32[]{:S(2)}) async-start(bf16[32,24,256]{2,1,0:T(8,128)(2,1)} %pad_maximum_fusion.3), calls=%async_computation.3 | async-start | bytes 786432 | tf_op jit(solution)/shard_map/all_to_all | solution.py:26
  86.6 1.6 %collective-permute-start.1 = (bf16[512,256]{1,0:T(8,128)(2,1)S(1)}, bf16[512,256]{1,0:T(8,128)(2,1)S(1)}, u32[]{:S(2)}, u32[]{:S(2)}) collective-permute-start(bf16[512,256]{1,0:T(8,128)(2,1)S(1)} %bitcast.47), channel_id=1, source_target_pairs={{0,1},{1,0},{2,3},{3,2},{4,5},{5,4},{6,7},{7,6},{8,9},{9,8},{10,11... | collective-permute-start | bytes 786440 | tf_op jit(solution)/shard_map/ppermute | solution.py:139

commit v2 on v1

v2 whole, which is shorter than its diff:
```python
import functools

import jax
import jax.numpy as jnp
from jax import lax
from jax.experimental import pallas as pl
from jax.experimental.pallas import tpu as pltpu
from jax.sharding import PartitionSpec as P

AXES = ("dom", "sub")
BF16 = jnp.bfloat16
F8 = jnp.float8_e4m3fn
F32 = jnp.float32
I32 = jnp.int32
LANES = 128
BLOCK = 256
VMEM_LIMIT = 24 * 2**20


def tdot(left, right):
    return lax.dot_general(left, right, (((0,), (0,)), ((), ())), preferred_element_type=F32)


def dot_transposed(left, right):
    return lax.dot_general(left, right, (((1,), (1,)), ((), ())), preferred_element_type=F32)


def dot(left, right):
    return jnp.dot(left, right, preferred_element_type=F32)


def exchange(rows):
    return lax.all_to_all(rows, AXES, split_axis=0, concat_axis=0, tiled=True)


def run(kernel, name, outs, vmem=(), hbm=(), smem=(), scratch=(), flops=0, moved=0):
    in_place = pl.BlockSpec(memory_space=pltpu.VMEM)
    remote = pl.BlockSpec(memory_space=pltpu.HBM)
    return pl.pallas_call(
        kernel,
        out_shape=tuple(outs),
        in_specs=[pl.BlockSpec(memory_space=pltpu.SMEM)] * len(smem)
        + [remote] * len(hbm)
        + [in_place] * len(vmem),
        out_specs=tuple(remote if out.memory_space == pltpu.HBM else in_place for out in outs),
        scratch_shapes=tuple(scratch),
        compiler_params=pltpu.CompilerParams(vmem_limit_bytes=VMEM_LIMIT),
        cost_estimate=pl.CostEstimate(flops=flops, bytes_accessed=moved, transcendentals=0),
        name=name,
    )(
        *smem,
        *[pltpu.with_memory_space_constraint(arg, pltpu.HBM) for arg in hbm],
        *[pltpu.with_memory_space_constraint(arg, pltpu.VMEM) for arg in vmem],
    )


def staged(*arrays):
    buffers = [pltpu.VMEM(array.shape, array.dtype) for array in arrays]
    return buffers + [pltpu.SemaphoreType.DMA((len(arrays),))]


def start_all(sources, buffers, semaphores):
    copies = [
        pltpu.make_async_copy(source, buffer, semaphores.at[index])
        for index, (source, buffer) in enumerate(zip(sources, buffers))
    ]
    for copy in copies:
        copy.start()
    return copies


def iota(shape, dim):
    return lax.broadcasted_iota(I32, shape, dim)


def one_hot(mask, dtype):
    return jnp.where(mask, 1.0, 0.0).astype(dtype)


def inverse_columns(in_count):
    return (1.0 / jnp.maximum(in_count[...], 1).astype(F32)).T


def send(array, out, semaphore):
    copy = pltpu.make_async_copy(array, out, semaphore)
    copy.start()
    copy.wait()


def pick_rows(
    features_at,
    cotangent_at,
    in_count_at,
    sent_at,
    payload,
    scaled,
    picking,
    features,
    cotangent,
    in_count,
    sent,
    semaphores,
    rows_out,
    out_semaphore,
):
    node_dev, width = features.shape
    per_peer, devices = sent.shape
    mirrors = devices * per_peer
    copies = start_all(
        [sent_at, in_count_at, cotangent_at, features_at],
        [sent, in_count, cotangent, features],
        semaphores,
    )
    copies[0].wait()
    spread_out = one_hot(
        iota((mirrors, devices), 0) // per_peer == iota((mirrors, devices), 1), BF16
    )
    high = dot_transposed(spread_out, (sent[...] >> 5).astype(F32).astype(BF16))
    low = dot_transposed(spread_out, (sent[...] & 31).astype(F32).astype(BF16))
    within = iota((mirrors, per_peer), 0) % per_peer == iota((mirrors, per_peer), 1)
    owner = jnp.sum(jnp.where(within, high * 32.0 + low, 0.0), axis=1, keepdims=True).astype(I32)
    picks = one_hot(iota((mirrors, node_dev), 1) == owner, BF16)
    picking[...] = picks
    copies[1].wait()
    columns = inverse_columns(in_count)
    copies[2].wait()
    for block in range(node_dev // LANES):
        rows = pl.ds(block * LANES, LANES)
        scaled[rows, :] = (
            cotangent[rows, :].astype(F32) * columns[:, block : block + 1]
        ).astype(BF16)
    back = dot(picks, scaled[...])
    copies[3].wait()
    front = dot(picks, features[...])
    rows_out[...] = (
        jnp.concatenate([front, back], axis=1)
        .reshape(devices, per_peer, 2 * width)
        .astype(BF16)
    )
    send(rows_out, payload, out_semaphore)


def count_edges(
    edge_count,
    sources_at,
    targets_at,
    features_at,
    scaled,
    counts_out,
    mirror_out,
    partial_out,
    sources,
    targets,
    features,
    semaphores,
    from_hot,
    into_hot,
    counts,
    out_semaphores,
):
    node_dev, width = features.shape
    slots, edges = into_hot.shape
    copies = start_all(
        [sources_at, targets_at, features_at], [sources, targets, features], semaphores
    )
    copies[0].wait()
    edge_ids = iota(sources.shape, 0) * LANES + iota(sources.shape, 1)
    source_columns = jnp.where(edge_ids < edge_count[0], sources[...], -1).T
    lane_ids = iota((LANES, slots), 1)
    for block in range(edges // LANES):
        from_hot[pl.ds(block * LANES, LANES), :] = one_hot(
            lane_ids == source_columns[:, block : block + 1], F8
        )
    copies[1].wait()
    row_ids = iota((LANES, LANES), 0)
    sends = []
    for start in range(0, slots, BLOCK):
        size = min(BLOCK, slots - start)
        for block in range(edges // LANES):
            target_row = targets[block : block + 1, :]
            for part in range(start, start + size, LANES):
                into_hot[pl.ds(part, LANES), pl.ds(block * LANES, LANES)] = one_hot(
                    row_ids + part == target_row, F8
                )
        rows = pl.ds(start, size)
        counts[rows, :] = dot(into_hot[rows, :], from_hot[...]).astype(BF16)
        copy = pltpu.make_async_copy(
            counts.at[rows], counts_out.at[rows], out_semaphores.at[start // BLOCK]
        )
        copy.start()
        sends.append(copy)
    copies[2].wait()
    mirror_out[...] = counts[node_dev:, node_dev:]
    partial_out[:, :width] = dot(counts[node_dev:, :node_dev], features[...])
    partial_out[:, width:] = tdot(counts[:node_dev, node_dev:], scaled[...])
    for copy in sends:
        copy.wait()


def mirror_sums(partial_in, mirror_counts, mirrored, payload, rows_out, out_semaphore):
    width = partial_in.shape[1] // 2
    received = mirrored[...]
    front = partial_in[:, :width] + dot(mirror_counts[...], received[:, :width])
    back = partial_in[:, width:] + tdot(mirror_counts[...], received[:, width:])
    rows_out[...] = (
        jnp.concatenate([front, back], axis=1).reshape(rows_out.shape).astype(BF16)
    )
    send(rows_out, payload, out_semaphore)


def local_sums(
    counts_at, features_at, scaled, mirrored, forward, backward, counts, features, semaphores
):
    node_dev, width = features.shape
    slots = counts.shape[0]
    blocks = [(start, min(BLOCK, slots - start)) for start in range(0, slots, BLOCK)]
    feature_copy = pltpu.make_async_copy(features_at, features, semaphores.at[len(blocks)])
    feature_copy.start()
    copies = []
    for index, (start, size) in enumerate(blocks):
        rows = pl.ds(start, size)
        copy = pltpu.make_async_copy(counts_at.at[rows], counts.at[rows], semaphores.at[index])
        copy.start()
        copies.append(copy)
    feature_copy.wait()
    for (start, size), copy in zip(blocks, copies):
        copy.wait()
        if start < node_dev:
            rows = pl.ds(start, size)
            forward[rows, :] = dot(counts[rows, :node_dev], features[...]) + dot(
                counts[rows, node_dev:], mirrored[:, :width]
            )
    for start in range(0, node_dev, BLOCK):
        rows = pl.ds(start, BLOCK)
        backward[rows, :] = tdot(counts[:node_dev, rows], scaled[...]) + tdot(
            counts[node_dev:, rows], mirrored[:, width:]
        )


def middle(
    core,
    features_at,
    cotangent_at,
    in_count_at,
    forward,
    backward,
    returned,
    picking,
    w_self_one,
    w_nbr_one,
    bias_one,
    w_self_two,
    w_nbr_two,
    grad_z,
    sent_half,
    own_half,
    bias_rows,
    features,
    cotangent,
    in_count,
    semaphores,
    mean_one,
    h_one,
    pulled,
):
    node_dev, width = features.shape
    copies = start_all(
        [in_count_at, features_at, cotangent_at], [in_count, features, cotangent], semaphores
    )
    copies[0].wait()
    columns = inverse_columns(in_count)
    for start in range(0, node_dev, BLOCK):
        rows = pl.ds(start, BLOCK)
        placed = tdot(picking[:, rows], returned[...])
        inverse = jnp.concatenate(
            [columns[:, b : b + 1] for b in range(start // LANES, (start + BLOCK) // LANES)],
            axis=0,
        )
        mean_one[rows, :] = ((forward[rows, :] + placed[:, :width]) * inverse).astype(BF16)
        pulled[rows, :] = (backward[rows, :] + placed[:, width:]).astype(BF16)
    copies[1].wait()
    copies[2].wait()
    bias_total = jnp.zeros((1, width), F32)
    for start in range(0, node_dev, BLOCK):
        rows = pl.ds(start, BLOCK)
        z_one = (
            dot(features[rows, :], w_self_one[...])
            + dot(mean_one[rows, :], w_nbr_one[...])
            + bias_one[...]
        )
        sigmoid = 1.0 / (1.0 + jnp.exp(-z_one))
        grad_h = dot_transposed(cotangent[rows, :], w_self_two[...]) + dot_transposed(
            pulled[rows, :], w_nbr_two[...]
        )
        grad = (grad_h * (sigmoid * (1.0 + z_one * (1.0 - sigmoid)))).astype(BF16)
        h_one[rows, :] = (z_one * sigmoid).astype(BF16)
        grad_z[rows, :] = grad
        bias_total += jnp.sum(grad.astype(F32), axis=0, keepdims=True)
    bias_high = bias_total.astype(BF16)
    bias_rows[0:1, :] = bias_high
    bias_rows[1:2, :] = (bias_total - bias_high.astype(F32)).astype(BF16)
    bias_rows[2:, :] = jnp.zeros((bias_rows.shape[0] - 2, width), BF16)

    def early():
        return tdot(features[...], grad_z[...]), tdot(mean_one[...], grad_z[...])

    def late():
        return tdot(h_one[...], cotangent[...]), tdot(h_one[...], pulled[...])

    for parity, (sent, owned) in enumerate(((late, early), (early, late))):

        @pl.when(core[0] == parity)
        def _(sent=sent, owned=owned):
            top, bottom = sent()
            sent_half[:width, :] = top.astype(BF16)
            sent_half[width:, :] = bottom.astype(BF16)
            top, bottom = owned()
            own_half[:width, :] = top
            own_half[width:, :] = bottom


def messages(in_count, grad_z, w_nbr_one, picking, message_one, picked):
    node_dev, width = grad_z.shape
    columns = inverse_columns(in_count)
    for start in range(0, node_dev, BLOCK):
        rows = pl.ds(start, BLOCK)
        inverse = jnp.concatenate(
            [columns[:, b : b + 1] for b in range(start // LANES, (start + BLOCK) // LANES)],
            axis=0,
        )
        message_one[rows, :] = (
            dot_transposed(grad_z[rows, :], w_nbr_one[...]) * inverse
        ).astype(BF16)
    picked[...] = dot(picking[...], message_one[...])


def join_first(own_half, other_half, picked, bias_rows, payload, rows_out, out_semaphore):
    devices, _, width = rows_out.shape
    per_peer = picked.shape[0] // devices
    chunk = own_half.shape[0] // devices
    chip_half = own_half[...] + other_half[...].astype(F32)
    rows_out[:, :chunk, :] = chip_half.reshape(devices, chunk, width).astype(BF16)
    rows_out[:, chunk : chunk + per_peer, :] = (
        picked[...].reshape(devices, per_peer, width).astype(BF16)
    )
    rows_out[:, chunk + per_peer :, :] = jnp.broadcast_to(
        bias_rows[:4, :][None], (devices, 4, width)
    )
    send(rows_out, payload, out_semaphore)


def local_back(
    counts_at, message_one, grad_z, w_self_one, mirror_out, local_out, counts, semaphore
):
    node_dev, width = grad_z.shape
    copy = pltpu.make_async_copy(counts_at.at[pl.ds(0, node_dev)], counts, semaphore)
    copy.start()
    for start in range(0, node_dev, BLOCK):
        rows = pl.ds(start, BLOCK)
        local_out[rows, :] = dot_transposed(grad_z[rows, :], w_self_one[...])
    copy.wait()
    mirror_out[...] = tdot(counts[:, node_dev:], message_one[...])
    for start in range(0, node_dev, BLOCK):
        rows = pl.ds(start, BLOCK)
        local_out[rows, :] += tdot(counts[:, rows], message_one[...])


def join_second(
    chunk, norm_factor, received, mirror_partial, mirror_counts, payload, mirrored_out, bias_out, rows_out, out_semaphore
):
    devices, _, width = rows_out.shape
    mirrors = mirror_partial.shape[0]
    per_peer = mirrors // devices
    owned = (
        jnp.sum(
            received[:, :chunk, :].astype(F32).reshape(devices // 2, 2, chunk, width), axis=0
        )
        * norm_factor
    )
    mirrored = (
        received[:, chunk : chunk + per_peer, :].astype(F32).reshape(mirrors, width).astype(BF16)
    )
    mirrored_out[...] = mirrored
    partial_sums = mirror_partial[...] + tdot(mirror_counts[...], mirrored)
    rows_out[:, :chunk, :] = (
        jnp.broadcast_to(owned[None], (devices // 2, 2, chunk, width))
        .reshape(devices, chunk, width)
        .astype(BF16)
    )
    rows_out[:, chunk : chunk + per_peer, :] = partial_sums.reshape(
        devices, per_peer, width
    ).astype(BF16)
    rows_out[:, chunk + per_peer :, :] = jnp.zeros((devices, 4, width), BF16)
    copy = pltpu.make_async_copy(rows_out, payload, out_semaphore)
    copy.start()
    bias_out[...] = (
        jnp.sum(
            received[:, chunk + per_peer : chunk + per_peer + 2, :].astype(F32),
            axis=(0, 1),
            keepdims=True,
        ).reshape(1, width)
        * norm_factor
    )
    copy.wait()


def shards(
    features,
    cotangent,
    w_self_one,
    w_nbr_one,
    bias_one,
    w_self_two,
    w_nbr_two,
    in_count,
    send_list,
    src_slot,
    dst_slot,
    edge_count,
):
    node_dev, width = features.shape
    devices = lax.axis_size("dom") * lax.axis_size("sub")
    per_peer = send_list.shape[2]
    mirrors = devices * per_peer
    slots = node_dev + mirrors
    edges = src_slot.shape[1]
    core = lax.axis_index("sub") % 2
    swap = [(i, i ^ 1) for i in range(devices)]
    in_count = in_count.reshape(-1, LANES)
    sent = send_list[0].T
    sources = src_slot.reshape(-1, LANES)
    targets = dst_slot.reshape(-1, LANES)
    blocks = -(-slots // BLOCK)

    payload_shape = (devices, per_peer, 2 * width)
    payload, scaled, picking = run(
        pick_rows,
        "pick_rows",
        [
            pltpu.HBM(payload_shape, BF16),
            pltpu.VMEM((node_dev, width), BF16),
            pltpu.VMEM((mirrors, node_dev), BF16),
        ],
        hbm=[features, cotangent, in_count, sent],
        scratch=staged(features, cotangent, in_count, sent)
        + [pltpu.VMEM(payload_shape, BF16), pltpu.SemaphoreType.DMA],
        flops=4 * mirrors * node_dev * width,
    )
    mirrored = exchange(payload).reshape(mirrors, 2 * width)

    counts, mirror_counts, partial_sums = run(
        count_edges,
        "count_edges",
        [
            pltpu.HBM((slots, slots), BF16),
            pltpu.VMEM((mirrors, mirrors), BF16),
            pltpu.VMEM((mirrors, 2 * width), F32),
        ],
        smem=[edge_count],
        hbm=[sources, targets, features],
        vmem=[scaled],
        scratch=staged(sources, targets, features)
        + [
            pltpu.VMEM((edges, slots), F8),
            pltpu.VMEM((slots, edges), F8),
            pltpu.VMEM((slots, slots), BF16),
            pltpu.SemaphoreType.DMA((blocks,)),
        ],
        flops=2 * slots * edges * slots,
    )
    (payload,) = run(
        mirror_sums,
        "mirror_sums",
        [pltpu.HBM(payload_shape, BF16)],
        vmem=[partial_sums, mirror_counts, mirrored],
        scratch=[pltpu.VMEM(payload_shape, BF16), pltpu.SemaphoreType.DMA],
        flops=4 * mirrors * mirrors * width,
    )
    returned = exchange(payload).reshape(mirrors, 2 * width)
    forward, backward = run(
        local_sums,
        "local_sums",
        [pltpu.VMEM((node_dev, width), F32)] * 2,
        hbm=[counts, features],
        vmem=[scaled, mirrored],
        scratch=[
            pltpu.VMEM((slots, slots), BF16),
            pltpu.VMEM((node_dev, width), BF16),
            pltpu.SemaphoreType.DMA((blocks + 1,)),
        ],
        flops=4 * node_dev * slots * width,
    )

    half = 2 * width
    chunk = half // devices
    grad_z_one, sent_half, own_half, bias_rows = run(
        middle,
        "middle",
        [
            pltpu.VMEM((node_dev, width), BF16),
            pltpu.VMEM((half, width), BF16),
            pltpu.VMEM((half, width), F32),
            pltpu.VMEM((16, width), BF16),
        ],
        smem=[core.reshape(1)],
        hbm=[features, cotangent, in_count],
        vmem=[
            forward,
            backward,
            returned,
            picking,
            w_self_one,
            w_nbr_one,
            bias_one.reshape(1, -1),
            w_self_two,
            w_nbr_two,
        ],
        scratch=staged(features, cotangent, in_count)
        + [pltpu.VMEM((node_dev, width), BF16)] * 3,
        flops=24 * node_dev * width * width,
    )
    other_half = lax.ppermute(sent_half, AXES, swap)
    message_one, picked = run(
        messages,
        "messages",
        [pltpu.VMEM((node_dev, width), BF16), pltpu.VMEM((mirrors, width), F32)],
        vmem=[in_count, grad_z_one, w_nbr_one, picking],
        flops=2 * node_dev * width * width,
    )

    payload_shape = (devices, chunk + per_peer + 4, width)
    (payload,) = run(
        join_first,
        "join_first",
        [pltpu.HBM(payload_shape, BF16)],
        vmem=[own_half, other_half, picked, bias_rows],
        scratch=[pltpu.VMEM(payload_shape, BF16), pltpu.SemaphoreType.DMA],
    )
    received = exchange(payload)
    mirror_back, local_grad = run(
        local_back,
        "local_back",
        [pltpu.VMEM((mirrors, width), F32), pltpu.VMEM((node_dev, width), F32)],
        hbm=[counts],
        vmem=[message_one, grad_z_one, w_self_one],
        scratch=[pltpu.VMEM((node_dev, slots), BF16), pltpu.SemaphoreType.DMA],
        flops=2 * node_dev * (slots + width) * width,
    )
    norm_factor = float(node_dev * devices) ** -0.5
    payload, mirrored, grad_bias = run(
        functools.partial(join_second, chunk, norm_factor),
        "join_second",
        [
            pltpu.HBM(payload_shape, BF16),
            pltpu.VMEM((mirrors, width), BF16),
            pltpu.VMEM((1, width), F32),
        ],
        vmem=[received, mirror_back, mirror_counts],
        scratch=[pltpu.VMEM(payload_shape, BF16), pltpu.SemaphoreType.DMA],
    )
    received = exchange(payload)
    local_grad = local_grad + tdot(counts[node_dev:, :node_dev], mirrored)
    returned = received[:, chunk : chunk + per_peer].reshape(mirrors, width)
    mine = received[:, :chunk].reshape(half, width)
    other = lax.ppermute(mine, AXES, swap)
    first = jnp.where(core == 0, mine, other)
    second = jnp.where(core == 0, other, mine)
    grad_weights = jnp.concatenate([first, second], axis=0).astype(F32).reshape(4, width, width)
    grad_features = (local_grad + tdot(picking, returned)).astype(BF16)
    return (grad_features, grad_weights, grad_bias.reshape(width))


def solution(mesh):
    by_device = P(AXES)
    return jax.shard_map(
        shards,
        mesh=mesh,
        in_specs=(
            P(AXES, None),
            P(AXES, None),
            P(),
            P(),
            P(),
            P(),
            P(),
            by_device,
            P(AXES, None, None),
            P(AXES, None),
            P(AXES, None),
            by_device,
        ),
        out_specs=(P(AXES, None), P(), P()),
        check_vma=False,
    )
```

time: 90.1 us -> 74.7 us (0.83)
  matrix products: 26.1 us -> 2.39 us
  Pallas kernels: 0 us -> 21.1 us
  other arithmetic: 7.02 us -> 1.15 us
  waiting for transfers between devices: 30.3 us -> 27.8 us
  local copies, waits for them, and re-layouts: 5.3 us -> 2.92 us
  starting transfers between devices: 18.9 us -> 17.3 us
    pallas_call x0 -> x9, Pallas kernels: none -> 21.1 us  [run(): pl.pallas_call(kernel, out_shape=tuple(outs), in_specs=[pl.BlockSpec(memo...]
    dot_general x11 -> x0, matrix products: 17 us -> none  [the longest x5 10.2 us: dot_transposed(): lax.dot_general(left, right, (((1,), (1,)), ((), ())), preferred_element_...]
    dot_general x10 -> x2, matrix products: 9.15 us -> 2.39 us  [tdot(): lax.dot_general(left, right, (((0,), (0,)), ((), ())), preferred_element_...]
    all_to_all x4, waiting for transfers between devices: 29.5 us -> 26.7 us  [exchange(): return lax.all_to_all(rows, AXES, split_axis=0, concat_axis=0, tiled=True)]
    concatenate x6 -> x1, other arithmetic: 2.68 us -> 0.04 us  [shards(): jnp.concatenate([first, second], axis=0).astype(F32)]
    convert_element_type x7 -> x1, other arithmetic: 2.87 us -> 1.06 us  [shards(): jnp.concatenate([first, second], axis=0).astype(F32)]
    all_to_all x4, starting transfers between devices: 18.5 us -> 16.9 us  [exchange(): return lax.all_to_all(rows, AXES, split_axis=0, concat_axis=0, tiled=True)]
    reshape x7 -> x3, local copies, waits for them, and re-layouts: 1.48 us -> 0.09 us  [the longest x1 0.04 us: shards(): mirrored = exchange(payload).reshape(mirrors, 2 * width)]
  transfers between devices with their start and end apart: 6 -> 6, of which waited for: 5 -> 6; matrix products, arithmetic and copies ran while one was open for 20% -> 4% of each run, Pallas kernels for 0% -> 18%
where the time goes in v2:
time: 74.7 us; the launch traced here: 74.1 us
  waiting for transfers between devices  27.8 us (37%)
  Pallas kernels  21.1 us (28%)
  starting transfers between devices  17.3 us (23%)
  local copies, waits for them, and re-layouts  2.92 us (4%)
  matrix products  2.39 us (3%)
  between operations  1.54 us (2%)
  other arithmetic  1.15 us (2%)
    all_to_all x4, waiting for transfers between devices, exchange(): return lax.all_to_all(rows, AXES, split_axis=0, concat_axis=0, tiled=True)  26.7 us
    pallas_call x9, Pallas kernels, run(): pl.pallas_call(kernel, out_shape=tuple(outs), in_specs=[pl.BlockSpec(memo...  21.1 us
    all_to_all x4, starting transfers between devices, exchange(): return lax.all_to_all(rows, AXES, split_axis=0, concat_axis=0, tiled=True)  16.9 us
    unnamed x17, local copies, waits for them, and re-layouts  2.78 us
    dot_general x2, matrix products, tdot(): lax.dot_general(left, right, (((0,), (0,)), ((), ())), preferred_element_...  2.39 us
  transfers between devices with their start and end apart: 6, of which 6 were waited for; matrix products, arithmetic and copies ran while one was open for 4% of the time, Pallas kernels for 18%

profile of v2, /device:TPU:0, one launch (start us, length us, event | category | flops | bytes accessed | tf_op | source)
XLA Modules:
  0.0 74.1 jit_solution(5881349751583104119)
XLA Ops:
  0.6 2.4 %pick_rows.1 = (bf16[32,4,512]{2,1,0:T(4,128)(2,1)}, bf16[1024,256]{1,0:T(8,128)(2,1)S(1)}, bf16[128,1024]{1,0:T(8,128)(2,1)S(1)}) custom-call(bf16[1024,256]{1,0:T(8,128)(2,1)} %features_at.7, bf16[1024,256]{1,0:T(8,128)(2,1)} %cotangent_at.3, s32[8,128]{1,0:T(8,128)} %bitcast.18, s32[4,32]{1,0:T(4,128)} %bitcast.24), custom_call_target="tpu_custom_call" | custom-call | flops 134217728 | tf_op jit(solution)/shard_map/pick_rows/pallas_call | solution.py:39
  3.1 7.3 %all-to-all-start = ((bf16[32,4,512]{2,1,0:T(4,128)(2,1)}), bf16[32,4,512]{2,1,0:T(4,128)(2,1)S(1)}, u32[]{:S(2)}, u32[]{:S(2)}) async-start(bf16[32,4,512]{2,1,0:T(4,128)(2,1)} %get-tuple-element.24), calls=%async_computation | async-start | bytes 262144 | tf_op jit(solution)/shard_map/all_to_all | solution.py:33
  11.0 6.0 %count_edges.1 = (bf16[1152,1152]{1,0:T(8,128)(2,1)}, bf16[128,128]{1,0:T(8,128)(2,1)S(1)}, f32[128,512]{1,0:T(8,128)S(1)}) custom-call(s32[1]{0:T(128)S(6)} %copy.16.edge_count, s32[16,128]{1,0:T(8,128)} %bitcast.25, s32[16,128]{1,0:T(8,128)} %bitcast.26, bf16[1024,256]{1,0:T(8,128)(2,1)} %features_at.7, bf16[1024,256]{1,0:T(8,128)(2,1)S(1)} %get-tuple-element.22.scaled), custom_call_target="tpu_custom_call" | custom-call | flops 5435817984 | tf_op jit(solution)/shard_map/count_edges/pallas_call | solution.py:39
  17.0 1.6 %all-to-all-done = bf16[32,4,512]{2,1,0:T(4,128)(2,1)S(1)} async-done(((bf16[32,4,512]{2,1,0:T(4,128)(2,1)}), bf16[32,4,512]{2,1,0:T(4,128)(2,1)S(1)}, u32[]{:S(2)}, u32[]{:S(2)}) %all-to-all-start) | async-done | bytes 131104 | tf_op jit(solution)/shard_map/all_to_all | solution.py:33
  18.7 0.9 %mirror_sums.1 = bf16[32,4,512]{2,1,0:T(4,128)(2,1)} custom-call(f32[128,512]{1,0:T(8,128)S(1)} %get-tuple-element.27.partial_in, bf16[128,128]{1,0:T(8,128)(2,1)S(1)} %get-tuple-element.28.mirror_counts, bf16[128,512]{1,0:T(8,128)(2,1)S(1)} %reshape.44.mirrored), custom_call_target="tpu_custom_call" | custom-call | flops 16777216 | tf_op jit(solution)/shard_map/mirror_sums/pallas_call | solution.py:39
  19.6 4.3 %all-to-all-start.1 = ((bf16[32,4,512]{2,1,0:T(4,128)(2,1)}), bf16[32,4,512]{2,1,0:T(4,128)(2,1)S(1)}, u32[]{:S(2)}, u32[]{:S(2)}) async-start(bf16[32,4,512]{2,1,0:T(4,128)(2,1)} %mirror_sums.1), calls=%async_computation.1 | async-start | bytes 262144 | tf_op jit(solution)/shard_map/all_to_all | solution.py:33
  23.9 4.0 %local_sums.1 = (f32[1024,256]{1,0:T(8,128)S(1)}, f32[1024,256]{1,0:T(8,128)S(1)}) custom-call(bf16[1152,1152]{1,0:T(8,128)(2,1)} %get-tuple-element.23.counts_at, bf16[1024,256]{1,0:T(8,128)(2,1)} %features_at.7, bf16[1024,256]{1,0:T(8,128)(2,1)S(1)} %get-tuple-element.22.scaled, bf16[128,512]{1,0:T(8,128)(2,1)S(1)} %reshape.44.mirrored), custom_call_target="tpu_custom_call" | custom-call | flops 1207959552 | tf_op jit(solution)/shard_map/local_sums/pallas_call | solution.py:39
  28.0 1.0 %copy-done.6 = f32[1024,256]{1,0:T(8,128)} copy-done((f32[1024,256]{1,0:T(8,128)}, f32[1024,256]{1,0:T(8,128)S(1)}, u32[]{:S(2)}) %copy-start.6) | copy-done | bytes 1048600
  28.9 3.2 %all-to-all-done.1 = bf16[32,4,512]{2,1,0:T(4,128)(2,1)S(1)} async-done(((bf16[32,4,512]{2,1,0:T(4,128)(2,1)}), bf16[32,4,512]{2,1,0:T(4,128)(2,1)S(1)}, u32[]{:S(2)}, u32[]{:S(2)}) %all-to-all-start.1) | async-done | bytes 131104 | tf_op jit(solution)/shard_map/all_to_all | solution.py:33
  32.2 1.2 %copy-done.7 = f32[1024,256]{1,0:T(8,128)S(1)} copy-done((f32[1024,256]{1,0:T(8,128)S(1)}, f32[1024,256]{1,0:T(8,128)}, u32[]{:S(2)}) %copy-start.7) | copy-done | bytes 1048600
  33.4 2.8 %middle.1 = (bf16[1024,256]{1,0:T(8,128)(2,1)S(1)}, bf16[512,256]{1,0:T(8,128)(2,1)S(1)}, f32[512,256]{1,0:T(8,128)S(1)}, bf16[16,256]{1,0:T(8,128)(2,1)S(1)}) custom-call(s32[1]{0:T(128)} %bitcast.5.core, bf16[1024,256]{1,0:T(8,128)(2,1)} %features_at.7, bf16[1024,256]{1,0:T(8,128)(2,1)} %cotangent_at.3, s32[8,128]{1,0:T(8,128)} %bitcast.19, ...), custom_call_target="tpu_custom_call" | custom-call | flops 1610612736 | tf_op jit(solution)/shard_map/middle/pallas_call | solution.py:39
  36.6 0.6 messages.1
  37.2 0.7 collective-permute-done.other_half
  37.9 0.8 %join_first.1 = bf16[32,24,256]{2,1,0:T(8,128)(2,1)} custom-call(f32[512,256]{1,0:T(8,128)S(1)} %get-tuple-element.33.own_half, bf16[512,256]{1,0:T(8,128)(2,1)S(1)} %collective-permute-done.other_half, f32[128,256]{1,0:T(8,128)S(1)} %get-tuple-element.35.picked, bf16[16,256]{1,0:T(8,128)(2,1)S(1)} %get-tuple-element.36.bias_rows), custom_call_target="tpu_custom_call" | custom-call | tf_op jit(solution)/shard_map/join_first/pallas_call | solution.py:39
  38.7 2.6 %all-to-all-start.2 = ((bf16[32,24,256]{2,1,0:T(8,128)(2,1)}), bf16[32,24,256]{2,1,0:T(8,128)(2,1)S(1)}, u32[]{:S(2)}, u32[]{:S(2)}) async-start(bf16[32,24,256]{2,1,0:T(8,128)(2,1)} %join_first.1), calls=%async_computation.2 | async-start | bytes 786432 | tf_op jit(solution)/shard_map/all_to_all | solution.py:33
  41.3 2.5 %local_back.1 = (f32[128,256]{1,0:T(8,128)S(1)}, f32[1024,256]{1,0:T(8,128)S(1)}) custom-call(bf16[1152,1152]{1,0:T(8,128)(2,1)} %get-tuple-element.23.counts_at, bf16[1024,256]{1,0:T(8,128)(2,1)S(1)} %get-tuple-element.31.message_one, bf16[1024,256]{1,0:T(8,128)(2,1)S(1)} %get-tuple-element.30.grad_z, bf16[256,256]{1,0:T(8,128)(2,1)S(1)} %copy-done.1), custom_call_target="tpu_custom_call" | custom-call | flops 738197504 | tf_op jit(solution)/shard_map/local_back/pallas_call | solution.py:39
  43.9 10.6 %all-to-all-done.2.received = bf16[32,24,256]{2,1,0:T(8,128)(2,1)S(1)} async-done(((bf16[32,24,256]{2,1,0:T(8,128)(2,1)}), bf16[32,24,256]{2,1,0:T(8,128)(2,1)S(1)}, u32[]{:S(2)}, u32[]{:S(2)}) %all-to-all-start.2) | async-done | bytes 393248 | tf_op jit(solution)/shard_map/all_to_all | solution.py:33
  54.5 1.0 %join_second.1 = (bf16[32,24,256]{2,1,0:T(8,128)(2,1)}, bf16[128,256]{1,0:T(8,128)(2,1)S(1)}, f32[1,256]{1,0:T(1,128)S(1)}) custom-call(bf16[32,24,256]{2,1,0:T(8,128)(2,1)S(1)} %all-to-all-done.2.received, f32[128,256]{1,0:T(8,128)S(1)} %get-tuple-element.37.mirror_partial, bf16[128,128]{1,0:T(8,128)(2,1)S(1)} %get-tuple-element.28.mirror_counts), custom_call_target="tpu_custom_call" | custom-call | tf_op jit(solution)/shard_map/join_second/pallas_call | solution.py:39
  55.5 2.6 %all-to-all-start.3 = ((bf16[32,24,256]{2,1,0:T(8,128)(2,1)}), bf16[32,24,256]{2,1,0:T(8,128)(2,1)S(1)}, u32[]{:S(2)}, u32[]{:S(2)}) async-start(bf16[32,24,256]{2,1,0:T(8,128)(2,1)} %get-tuple-element.39), calls=%async_computation.3 | async-start | bytes 786432 | tf_op jit(solution)/shard_map/all_to_all | solution.py:33
  58.1 0.6 copy.15
  58.7 1.3 %convolution_add_fusion.1 = f32[1024,256]{1,0:T(8,128)S(1)} fusion(f32[1024,256]{1,0:T(8,128)S(1)} %get-tuple-element.32, bf16[128,256]{1,0:T(8,128)(2,1)S(1)} %get-tuple-element.38, bf16[1152,1152]{1,0:T(8,128)(2,1)} %get-tuple-element.23.counts_at), kind=kOutput, calls=%fused_computation.1 | convolution fusion | flops 67371008 | bytes 2424832 | tf_op jit(solution)/shard_map/dot_general | solution.py:21
  60.0 11.3 %all-to-all-done.3 = bf16[32,24,256]{2,1,0:T(8,128)(2,1)S(1)} async-done(((bf16[32,24,256]{2,1,0:T(8,128)(2,1)}), bf16[32,24,256]{2,1,0:T(8,128)(2,1)S(1)}, u32[]{:S(2)}, u32[]{:S(2)}) %all-to-all-start.3) | async-done | bytes 393248 | tf_op jit(solution)/shard_map/all_to_all | solution.py:33
  71.5 1.1 %fusion = bf16[1024,256]{1,0:T(8,128)(2,1)} fusion(f32[1024,256]{1,0:T(8,128)S(1)} %convolution_add_fusion.1, bf16[128,1024]{1,0:T(8,128)(2,1)S(1)} %get-tuple-element.29.picking, bf16[128,256]{1,0:T(8,128)(2,1)S(1)} %reshape.47), kind=kOutput, calls=%fused_computation.2 | convolution fusion | flops 67633152 | bytes 1900544 | tf_op jit(solution)/shard_map/dot_general | solution.py:21
  73.1 1.1 %convert.1 = f32[4,256,256]{2,1,0:T(8,128)} convert(bf16[4,256,256]{2,1,0:T(8,128)(2,1)S(1)} %bitcast.22) | non-fusion elementwise | flops 262144 | bytes 1572864 | tf_op jit(solution)/shard_map/convert_element_type | solution.py:568
  (24 shorter events, 1.1 us)
Async XLA Ops:
  3.1 15.5 %all-to-all-start = ((bf16[32,4,512]{2,1,0:T(4,128)(2,1)}), bf16[32,4,512]{2,1,0:T(4,128)(2,1)S(1)}, u32[]{:S(2)}, u32[]{:S(2)}) async-start(bf16[32,4,512]{2,1,0:T(4,128)(2,1)} %get-tuple-element.24), calls=%async_computation | async-start | bytes 262144 | tf_op jit(solution)/shard_map/all_to_all | solution.py:33
  19.5 12.6 %copy-start = (bf16[256,256]{1,0:T(8,128)(2,1)S(1)}, bf16[256,256]{1,0:T(8,128)(2,1)}, u32[]{:S(2)}) copy-start(bf16[256,256]{1,0:T(8,128)(2,1)} %w_nbr_one.3) | copy-start | bytes 393220
  19.5 12.6 %copy-start.1 = (bf16[256,256]{1,0:T(8,128)(2,1)S(1)}, bf16[256,256]{1,0:T(8,128)(2,1)}, u32[]{:S(2)}) copy-start(bf16[256,256]{1,0:T(8,128)(2,1)} %w_self_one.3) | copy-start | bytes 393220
  19.6 12.6 %copy-start.3 = (bf16[256,256]{1,0:T(8,128)(2,1)S(1)}, bf16[256,256]{1,0:T(8,128)(2,1)}, u32[]{:S(2)}) copy-start(bf16[256,256]{1,0:T(8,128)(2,1)} %w_self_two.1) | copy-start | bytes 393220
  19.6 12.6 %copy-start.4 = (bf16[256,256]{1,0:T(8,128)(2,1)S(1)}, bf16[256,256]{1,0:T(8,128)(2,1)}, u32[]{:S(2)}) copy-start(bf16[256,256]{1,0:T(8,128)(2,1)} %w_nbr_two.1) | copy-start | bytes 393220
  19.6 12.6 %copy-start.5 = (f32[256]{0:T(256)S(1)}, f32[256]{0:T(256)}, u32[]{:S(2)}) copy-start(f32[256]{0:T(256)} %param.16) | copy-start | bytes 3076
  19.6 12.5 %all-to-all-start.1 = ((bf16[32,4,512]{2,1,0:T(4,128)(2,1)}), bf16[32,4,512]{2,1,0:T(4,128)(2,1)S(1)}, u32[]{:S(2)}, u32[]{:S(2)}) async-start(bf16[32,4,512]{2,1,0:T(4,128)(2,1)} %mirror_sums.1), calls=%async_computation.1 | async-start | bytes 262144 | tf_op jit(solution)/shard_map/all_to_all | solution.py:33
  27.9 1.0 %copy-start.6 = (f32[1024,256]{1,0:T(8,128)}, f32[1024,256]{1,0:T(8,128)S(1)}, u32[]{:S(2)}) copy-start(f32[1024,256]{1,0:T(8,128)S(1)} %get-tuple-element.26.backward) | copy-start | bytes 3145732
  32.2 1.2 %copy-start.7 = (f32[1024,256]{1,0:T(8,128)S(1)}, f32[1024,256]{1,0:T(8,128)}, u32[]{:S(2)}) copy-start(f32[1024,256]{1,0:T(8,128)} %copy-done.6) | copy-start | bytes 3145732
  33.4 3.1 %copy-start.2 = (s32[1024]{0:T(1024)S(1)}, s32[1024]{0:T(1024)}, u32[]{:S(2)}) copy-start(s32[1024]{0:T(1024)} %param.19) | copy-start | bytes 12292
  36.3 1.6 %collective-permute-start = (bf16[512,256]{1,0:T(8,128)(2,1)S(1)}, bf16[512,256]{1,0:T(8,128)(2,1)S(1)}, u32[]{:S(2)}, u32[]{:S(2)}) collective-permute-start(bf16[512,256]{1,0:T(8,128)(2,1)S(1)} %get-tuple-element.34), channel_id=1, source_target_pairs={{0,1},{1,0},{2,3},{3,2},{4,5},{5,4},{6,7},{7,6},{8,9},{9,8},{10,11... | collective-permute-start | bytes 786440 | tf_op jit(solution)/shard_map/ppermute | solution.py:522
  38.7 15.8 %all-to-all-start.2 = ((bf16[32,24,256]{2,1,0:T(8,128)(2,1)}), bf16[32,24,256]{2,1,0:T(8,128)(2,1)S(1)}, u32[]{:S(2)}, u32[]{:S(2)}) async-start(bf16[32,24,256]{2,1,0:T(8,128)(2,1)} %join_first.1), calls=%async_computation.2 | async-start | bytes 786432 | tf_op jit(solution)/shard_map/all_to_all | solution.py:33
  55.5 15.8 %all-to-all-start.3 = ((bf16[32,24,256]{2,1,0:T(8,128)(2,1)}), bf16[32,24,256]{2,1,0:T(8,128)(2,1)S(1)}, u32[]{:S(2)}, u32[]{:S(2)}) async-start(bf16[32,24,256]{2,1,0:T(8,128)(2,1)} %get-tuple-element.39), calls=%async_computation.3 | async-start | bytes 786432 | tf_op jit(solution)/shard_map/all_to_all | solution.py:33
  71.4 1.6 %collective-permute-start.1 = (bf16[512,256]{1,0:T(8,128)(2,1)S(1)}, bf16[512,256]{1,0:T(8,128)(2,1)S(1)}, u32[]{:S(2)}, u32[]{:S(2)}) collective-permute-start(bf16[512,256]{1,0:T(8,128)(2,1)S(1)} %bitcast.23), channel_id=1, source_target_pairs={{0,1},{1,0},{2,3},{3,2},{4,5},{5,4},{6,7},{7,6},{8,9},{9,8},{10,11... | collective-permute-start | bytes 786440 | tf_op jit(solution)/shard_map/ppermute | solution.py:565

commit v3 on v2

v3 whole, which is shorter than its diff:
```python
import functools

import jax
import jax.numpy as jnp
from jax import lax
from jax.experimental import pallas as pl
from jax.experimental.pallas import tpu as pltpu
from jax.sharding import PartitionSpec as P

AXES = ("dom", "sub")
BF16 = jnp.bfloat16
F8 = jnp.float8_e4m3fn
F32 = jnp.float32
I32 = jnp.int32
I16 = jnp.int16
LANES = 128
BLOCK = 256
VMEM_LIMIT = 24 * 2**20


def tdot(left, right):
    return lax.dot_general(left, right, (((0,), (0,)), ((), ())), preferred_element_type=F32)


def dot_transposed(left, right):
    return lax.dot_general(left, right, (((1,), (1,)), ((), ())), preferred_element_type=F32)


def dot(left, right):
    return jnp.dot(left, right, preferred_element_type=F32)


def exchange(rows):
    return lax.all_to_all(rows, AXES, split_axis=0, concat_axis=0, tiled=True)


def run(kernel, name, outs, vmem=(), hbm=(), smem=(), scratch=(), flops=0, moved=0, aliases=None):
    in_place = pl.BlockSpec(memory_space=pltpu.VMEM)
    remote = pl.BlockSpec(memory_space=pltpu.HBM)
    return pl.pallas_call(
        kernel,
        out_shape=tuple(outs),
        in_specs=[pl.BlockSpec(memory_space=pltpu.SMEM)] * len(smem)
        + [remote] * len(hbm)
        + [in_place] * len(vmem),
        out_specs=tuple(remote if out.memory_space == pltpu.HBM else in_place for out in outs),
        scratch_shapes=tuple(scratch),
        compiler_params=pltpu.CompilerParams(vmem_limit_bytes=VMEM_LIMIT),
        cost_estimate=pl.CostEstimate(flops=flops, bytes_accessed=moved, transcendentals=0),
        input_output_aliases=aliases or {},
        name=name,
    )(
        *smem,
        *[pltpu.with_memory_space_constraint(arg, pltpu.HBM) for arg in hbm],
        *[pltpu.with_memory_space_constraint(arg, pltpu.VMEM) for arg in vmem],
    )


def staged_for(count, *arrays):
    buffers = [pltpu.VMEM(array.shape, array.dtype) for array in arrays]
    return buffers + [pltpu.SemaphoreType.DMA((count,))]


def start_all(sources, buffers, semaphores):
    copies = [
        pltpu.make_async_copy(source, buffer, semaphores.at[index])
        for index, (source, buffer) in enumerate(zip(sources, buffers))
    ]
    for copy in copies:
        copy.start()
    return copies


def iota(shape, dim, dtype=I32):
    return lax.broadcasted_iota(dtype, shape, dim)


def one_hot(mask, dtype):
    return jnp.where(mask, 1.0, 0.0).astype(dtype)


def edge_hot(mask):
    return jnp.where(mask, jnp.ones(mask.shape, BF16), jnp.zeros(mask.shape, BF16)).astype(F8)


def by_peer(rows, devices):
    return rows.reshape(devices, rows.shape[0] // devices, rows.shape[1]).astype(BF16)


def by_row(parts):
    return parts.astype(F32).reshape(parts.shape[0] * parts.shape[1], parts.shape[2])


def inverse_columns(in_count):
    return (1.0 / jnp.maximum(in_count[...], 1).astype(F32)).T


def send(array, out, semaphore):
    copy = pltpu.make_async_copy(array, out, semaphore)
    copy.start()
    copy.wait()


def pick_rows(
    edge_count,
    features_at,
    cotangent_at,
    in_count_at,
    sent_at,
    sources_at,
    targets_at,
    payload,
    scaled,
    picking,
    source_columns,
    targets,
    features,
    cotangent,
    in_count,
    sent,
    sources,
    semaphores,
    rows_out,
    out_semaphore,
):
    node_dev, width = features.shape
    per_peer, devices = sent.shape
    mirrors = devices * per_peer
    copies = start_all(
        [sent_at, in_count_at, cotangent_at, features_at, sources_at, targets_at],
        [sent, in_count, cotangent, features, sources, targets],
        semaphores,
    )
    copies[0].wait()
    spread_out = one_hot(
        iota((mirrors, devices), 0) // per_peer == iota((mirrors, devices), 1), BF16
    )
    high = dot_transposed(spread_out, (sent[...] >> 5).astype(F32).astype(BF16))
    low = dot_transposed(spread_out, (sent[...] & 31).astype(F32).astype(BF16))
    within = iota((mirrors, per_peer), 0) % per_peer == iota((mirrors, per_peer), 1)
    owner = jnp.sum(jnp.where(within, high * 32.0 + low, 0.0), axis=1, keepdims=True).astype(I32)
    picked = iota((mirrors, node_dev), 1) == owner
    picks = one_hot(picked, BF16)
    picking[...] = picks
    copies[1].wait()
    inverse_rows = 1.0 / jnp.maximum(in_count[...], 1).astype(F32)
    owner_inverse = jnp.zeros((mirrors, LANES), F32)
    for block in range(node_dev // LANES):
        lanes = slice(block * LANES, (block + 1) * LANES)
        owner_inverse += jnp.where(picked[:, lanes], inverse_rows[block : block + 1, :], 0.0)
    owner_inverse = jnp.sum(owner_inverse, axis=1, keepdims=True)
    copies[2].wait()
    back = dot(picks, cotangent[...]) * owner_inverse
    rows_out[:, :, width:] = by_peer(back, devices)
    copies[3].wait()
    rows_out[:, :, :width] = by_peer(dot(picks, features[...]), devices)
    out_copy = pltpu.make_async_copy(rows_out, payload, out_semaphore)
    out_copy.start()
    columns = inverse_rows.T
    for block in range(node_dev // LANES):
        rows = pl.ds(block * LANES, LANES)
        scaled[rows, :] = (
            cotangent[rows, :].astype(F32) * columns[:, block : block + 1]
        ).astype(BF16)
    copies[4].wait()
    edge_ids = iota(sources.shape, 0) * LANES + iota(sources.shape, 1)
    source_columns[...] = jnp.where(edge_ids < edge_count[0], sources[...], -1).T
    copies[5].wait()
    out_copy.wait()


def count_edges(
    features_at,
    scaled,
    source_columns,
    targets,
    counts_out,
    mirror_out,
    partial_out,
    features,
    semaphore,
    from_hot,
    into_hot,
    counts,
    out_semaphores,
):
    node_dev, width = features.shape
    slots, edges = into_hot.shape
    feature_copy = pltpu.make_async_copy(features_at, features, semaphore)
    feature_copy.start()
    lane_ids = iota((LANES, slots), 1, I16)
    for block in range(edges // LANES):
        column = jnp.broadcast_to(source_columns[:, block : block + 1], (LANES, LANES)).astype(I16)
        column = jnp.concatenate([column] * (slots // LANES), axis=1)
        from_hot[pl.ds(block * LANES, LANES), :] = edge_hot(lane_ids == column)
    row_ids = iota((LANES, LANES), 0, I16)
    target_rows = targets[...].astype(I16)
    sends = []
    for start in range(0, slots, BLOCK):
        size = min(BLOCK, slots - start)
        for block in range(edges // LANES):
            target_row = target_rows[block : block + 1, :]
            for part in range(start, start + size, LANES):
                into_hot[pl.ds(part, LANES), pl.ds(block * LANES, LANES)] = edge_hot(
                    row_ids + jnp.int16(part) == target_row
                )
        rows = pl.ds(start, size)
        counts[rows, :] = dot(into_hot[rows, :], from_hot[...]).astype(BF16)
        copy = pltpu.make_async_copy(
            counts.at[rows], counts_out.at[rows], out_semaphores.at[start // BLOCK]
        )
        copy.start()
        sends.append(copy)
    feature_copy.wait()
    mirror_out[...] = counts[node_dev:, node_dev:]
    partial_out[:, :width] = dot(counts[node_dev:, :node_dev], features[...])
    partial_out[:, width:] = tdot(counts[:node_dev, node_dev:], scaled[...])
    for copy in sends:
        copy.wait()


def mirror_sums(partial_in, mirror_counts, mirrored, payload, rows_out, out_semaphore):
    devices, _, columns = rows_out.shape
    width = columns // 2
    received = mirrored[...]
    front = partial_in[:, :width] + dot(mirror_counts[...], received[:, :width])
    back = partial_in[:, width:] + tdot(mirror_counts[...], received[:, width:])
    rows_out[:, :, :width] = by_peer(front, devices)
    rows_out[:, :, width:] = by_peer(back, devices)
    send(rows_out, payload, out_semaphore)


def local_sums(
    counts_at, features_at, scaled, mirrored, forward, backward, counts, features, semaphores
):
    node_dev, width = features.shape
    slots = counts.shape[0]
    blocks = [(start, min(BLOCK, slots - start)) for start in range(0, slots, BLOCK)]
    feature_copy = pltpu.make_async_copy(features_at, features, semaphores.at[len(blocks)])
    feature_copy.start()
    copies = []
    for index, (start, size) in enumerate(blocks):
        rows = pl.ds(start, size)
        copy = pltpu.make_async_copy(counts_at.at[rows], counts.at[rows], semaphores.at[index])
        copy.start()
        copies.append(copy)
    feature_copy.wait()
    for (start, size), copy in zip(blocks, copies):
        copy.wait()
        if start < node_dev:
            rows = pl.ds(start, size)
            forward[rows, :] = dot(counts[rows, :node_dev], features[...]) + dot(
                counts[rows, node_dev:], mirrored[:, :width]
            )
    for start in range(0, node_dev, BLOCK):
        rows = pl.ds(start, BLOCK)
        backward[rows, :] = tdot(counts[:node_dev, rows], scaled[...]) + tdot(
            counts[node_dev:, rows], mirrored[:, width:]
        )


def middle(
    core,
    in_count_at,
    w_nbr_one_at,
    w_self_one_at,
    bias_one_at,
    features_at,
    w_nbr_two_at,
    w_self_two_at,
    cotangent_at,
    forward,
    backward,
    returned,
    picking,
    grad_z,
    sent_half,
    own_half,
    bias_rows,
    in_count,
    w_nbr_one,
    w_self_one,
    bias_one,
    features,
    w_nbr_two,
    w_self_two,
    cotangent,
    semaphores,
    mean_one,
    h_one,
    pulled,
    slope,
):
    node_dev, width = features.shape
    copies = start_all(
        [
            in_count_at,
            w_nbr_one_at,
            w_self_one_at,
            bias_one_at,
            features_at,
            w_nbr_two_at,
            w_self_two_at,
            cotangent_at,
        ],
        [in_count, w_nbr_one, w_self_one, bias_one, features, w_nbr_two, w_self_two, cotangent],
        semaphores,
    )
    blocks = [pl.ds(start, BLOCK) for start in range(0, node_dev, BLOCK)]
    copies[0].wait()
    columns = inverse_columns(in_count)
    for index, rows in enumerate(blocks):
        placed = tdot(picking[:, rows], returned[...])
        first = index * BLOCK // LANES
        inverse = jnp.concatenate(
            [columns[:, b : b + 1] for b in range(first, first + BLOCK // LANES)], axis=0
        )
        mean_one[rows, :] = ((forward[rows, :] + placed[:, :width]) * inverse).astype(BF16)
        pulled[rows, :] = (backward[rows, :] + placed[:, width:]).astype(BF16)
    for copy in copies[1:5]:
        copy.wait()
    for rows in blocks:
        z_one = (
            dot(features[rows, :], w_self_one[...])
            + dot(mean_one[rows, :], w_nbr_one[...])
            + bias_one[...]
        )
        sigmoid = 1.0 / (1.0 + jnp.exp(-z_one))
        h_one[rows, :] = (z_one * sigmoid).astype(BF16)
        slope[rows, :] = sigmoid * (1.0 + z_one * (1.0 - sigmoid))
    for copy in copies[5:]:
        copy.wait()
    bias_total = jnp.zeros((1, width), F32)
    for rows in blocks:
        grad_h = dot_transposed(cotangent[rows, :], w_self_two[...]) + dot_transposed(
            pulled[rows, :], w_nbr_two[...]
        )
        grad = (grad_h * slope[rows, :]).astype(BF16)
        grad_z[rows, :] = grad
        bias_total += jnp.sum(grad.astype(F32), axis=0, keepdims=True)
    bias_high = bias_total.astype(BF16).astype(F32)
    bias_low = bias_total - bias_high
    for row, part in enumerate((bias_high, bias_low)):
        for block in range(width // LANES):
            bias_rows[row * (width // LANES) + block : row * (width // LANES) + block + 1, :] = (
                part[:, block * LANES : (block + 1) * LANES]
            )

    def early():
        return tdot(features[...], grad_z[...]), tdot(mean_one[...], grad_z[...])

    def late():
        return tdot(h_one[...], cotangent[...]), tdot(h_one[...], pulled[...])

    for parity, (sent, owned) in enumerate(((late, early), (early, late))):

        @pl.when(core[0] == parity)
        def _(sent=sent, owned=owned):
            top, bottom = sent()
            sent_half[:width, :] = top.astype(BF16)
            sent_half[width:, :] = bottom.astype(BF16)
            top, bottom = owned()
            own_half[:width, :] = top
            own_half[width:, :] = bottom


def messages(in_count, grad_z, w_nbr_one, picking, message_one, picked):
    node_dev, width = grad_z.shape
    columns = inverse_columns(in_count)
    for start in range(0, node_dev, BLOCK):
        rows = pl.ds(start, BLOCK)
        inverse = jnp.concatenate(
            [columns[:, b : b + 1] for b in range(start // LANES, (start + BLOCK) // LANES)],
            axis=0,
        )
        message_one[rows, :] = (
            dot_transposed(grad_z[rows, :], w_nbr_one[...]) * inverse
        ).astype(BF16)
    picked[...] = dot(picking[...], message_one[...])


def join_first(own_half, other_half, picked, bias_rows, payload, rows_out, out_semaphore):
    devices, per_peer, _ = rows_out.shape
    mirrors, width = picked.shape
    groups = own_half.shape[0] // mirrors
    rows_out[:, :, :width] = by_peer(picked[...], devices)
    for group in range(groups):
        rows = pl.ds(group * mirrors, mirrors)
        rows_out[:, :, (group + 1) * width : (group + 2) * width] = by_peer(
            own_half[rows, :] + other_half[rows, :].astype(F32), devices
        )
    rows_out[:, :, (groups + 1) * width :] = jnp.broadcast_to(
        bias_rows[...][None], (devices, per_peer, LANES)
    ).astype(BF16)
    send(rows_out, payload, out_semaphore)


def local_back(
    counts_at,
    message_one,
    grad_z,
    w_self_one,
    mirror_out,
    local_out,
    mirror_rows,
    counts,
    semaphores,
):
    node_dev, width = grad_z.shape
    copies = [
        pltpu.make_async_copy(counts_at.at[pl.ds(0, node_dev)], counts, semaphores.at[0]),
        pltpu.make_async_copy(
            counts_at.at[pl.ds(node_dev, mirror_rows.shape[0])], mirror_rows, semaphores.at[1]
        ),
    ]
    for copy in copies:
        copy.start()
    for start in range(0, node_dev, BLOCK):
        rows = pl.ds(start, BLOCK)
        local_out[rows, :] = dot_transposed(grad_z[rows, :], w_self_one[...])
    copies[0].wait()
    mirror_out[...] = tdot(counts[:, node_dev:], message_one[...])
    for start in range(0, node_dev, BLOCK):
        rows = pl.ds(start, BLOCK)
        local_out[rows, :] += tdot(counts[:, rows], message_one[...])
    copies[1].wait()


def join_second(
    norm_factor,
    received,
    mirror_partial,
    mirror_counts,
    payload,
    mirrored_out,
    bias_out,
    bias_total,
    semaphore,
):
    devices, per_peer, _ = payload.shape
    mirrors, width = mirror_partial.shape
    groups = payload.shape[2] // width - 1
    mirrored = by_row(received[:, :, :width]).astype(BF16)
    mirrored_out[...] = mirrored
    partial_sums = mirror_partial[...] + tdot(mirror_counts[...], mirrored)
    payload[:, :, :width] = by_peer(partial_sums, devices)
    for group in range(groups):
        lanes = slice((group + 1) * width, (group + 2) * width)
        owned = (
            jnp.sum(
                received[:, :, lanes].astype(F32).reshape(devices // 2, 2, per_peer, width), axis=0
            )
            * norm_factor
        ).astype(BF16)
        payload[:, :, lanes] = jnp.broadcast_to(
            owned[None], (devices // 2, 2, per_peer, width)
        ).reshape(devices, per_peer, width)
    sums = (
        jnp.sum(received[:, :, (groups + 1) * width :].astype(F32), axis=0) * norm_factor
    )
    parts = width // LANES
    for block in range(parts):
        bias_total[:, block * LANES : (block + 1) * LANES] = (
            sums[block : block + 1, :] + sums[parts + block : parts + block + 1, :]
        )
    send(bias_total, bias_out, semaphore)


def finish(
    core,
    received,
    mirrored,
    picking,
    mirror_rows,
    local_grad,
    features_at,
    weights_at,
    features_out,
    weights_out,
    semaphores,
):
    devices, per_peer, _ = received.shape
    node_dev, width = local_grad.shape
    mirrors = picking.shape[0]
    half = weights_out.shape[0]
    for group in range(half // mirrors):
        weights_out[pl.ds(group * mirrors, mirrors), :] = by_row(
            received[:, :, (group + 1) * width : (group + 2) * width]
        )
    mine = pl.multiple_of(core[0] * half, half)
    weights_copy = pltpu.make_async_copy(
        weights_out, weights_at.at[pl.ds(mine, half)], semaphores.at[0]
    )
    weights_copy.start()
    returned = by_row(received[:, :, :width]).astype(BF16)
    for start in range(0, node_dev, BLOCK):
        rows = pl.ds(start, BLOCK)
        features_out[rows, :] = (
            local_grad[rows, :]
            + tdot(picking[:, rows], returned)
            + tdot(mirror_rows[:, rows], mirrored[...])
        ).astype(BF16)
    features_copy = pltpu.make_async_copy(features_out, features_at, semaphores.at[1])
    features_copy.start()
    weights_copy.wait()
    features_copy.wait()


def finish_other(core, weights_in, received, weights_at, weights_out, semaphore):
    half, width = weights_out.shape
    devices, per_peer, columns = received.shape
    mirrors = devices * per_peer
    for group in range(half // mirrors):
        weights_out[pl.ds(group * mirrors, mirrors), :] = by_row(
            received[:, :, (group + 1) * width : (group + 2) * width]
        )
    other = pl.multiple_of((1 - core[0]) * half, half)
    send(weights_out, weights_at.at[pl.ds(other, half)], semaphore)


def shards(
    features,
    cotangent,
    w_self_one,
    w_nbr_one,
    bias_one,
    w_self_two,
    w_nbr_two,
    in_count,
    send_list,
    src_slot,
    dst_slot,
    edge_count,
):
    node_dev, width = features.shape
    devices = lax.axis_size("dom") * lax.axis_size("sub")
    per_peer = send_list.shape[2]
    mirrors = devices * per_peer
    slots = node_dev + mirrors
    edges = src_slot.shape[1]
    core = lax.axis_index("sub") % 2
    swap = [(i, i ^ 1) for i in range(devices)]
    in_count = in_count.reshape(-1, LANES)
    sent = send_list[0].T
    sources = src_slot.reshape(-1, LANES)
    targets = dst_slot.reshape(-1, LANES)
    blocks = -(-slots // BLOCK)

    payload_shape = (devices, per_peer, 2 * width)
    payload, scaled, picking, source_columns, targets = run(
        pick_rows,
        "pick_rows",
        [
            pltpu.HBM(payload_shape, BF16),
            pltpu.VMEM((node_dev, width), BF16),
            pltpu.VMEM((mirrors, node_dev), BF16),
            pltpu.VMEM((LANES, edges // LANES), I32),
            pltpu.VMEM(targets.shape, I32),
        ],
        smem=[edge_count],
        hbm=[features, cotangent, in_count, sent, sources, targets],
        scratch=staged_for(6, features, cotangent, in_count, sent, sources)
        + [pltpu.VMEM(payload_shape, BF16), pltpu.SemaphoreType.DMA],
        flops=4 * mirrors * node_dev * width,
    )
    mirrored = exchange(payload).reshape(mirrors, 2 * width)

    counts, mirror_counts, partial_sums = run(
        count_edges,
        "count_edges",
        [
            pltpu.HBM((slots, slots), BF16),
            pltpu.VMEM((mirrors, mirrors), BF16),
            pltpu.VMEM((mirrors, 2 * width), F32),
        ],
        hbm=[features],
        vmem=[scaled, source_columns, targets],
        scratch=[
            pltpu.VMEM((node_dev, width), BF16),
            pltpu.SemaphoreType.DMA,
            pltpu.VMEM((edges, slots), F8),
            pltpu.VMEM((slots, edges), F8),
            pltpu.VMEM((slots, slots), BF16),
            pltpu.SemaphoreType.DMA((blocks,)),
        ],
        flops=2 * slots * edges * slots,
    )
    (payload,) = run(
        mirror_sums,
        "mirror_sums",
        [pltpu.HBM(payload_shape, BF16)],
        vmem=[partial_sums, mirror_counts, mirrored],
        scratch=[pltpu.VMEM(payload_shape, BF16), pltpu.SemaphoreType.DMA],
        flops=4 * mirrors * mirrors * width,
    )
    returned = exchange(payload).reshape(mirrors, 2 * width)
    forward, backward = run(
        local_sums,
        "local_sums",
        [pltpu.VMEM((node_dev, width), F32)] * 2,
        hbm=[counts, features],
        vmem=[scaled, mirrored],
        scratch=[
            pltpu.VMEM((slots, slots), BF16),
            pltpu.VMEM((node_dev, width), BF16),
            pltpu.SemaphoreType.DMA((blocks + 1,)),
        ],
        flops=4 * node_dev * slots * width,
    )

    half = 2 * width
    loaded = [
        in_count,
        w_nbr_one,
        w_self_one,
        bias_one.reshape(1, -1),
        features,
        w_nbr_two,
        w_self_two,
        cotangent,
    ]
    grad_z_one, sent_half, own_half, bias_rows = run(
        middle,
        "middle",
        [
            pltpu.VMEM((node_dev, width), BF16),
            pltpu.VMEM((half, width), BF16),
            pltpu.VMEM((half, width), F32),
            pltpu.VMEM((2 * width // LANES, LANES), F32),
        ],
        smem=[core.reshape(1)],
        hbm=loaded,
        vmem=[forward, backward, returned, picking],
        scratch=staged_for(len(loaded), *loaded)
        + [pltpu.VMEM((node_dev, width), BF16)] * 3
        + [pltpu.VMEM((node_dev, width), F32)],
        flops=24 * node_dev * width * width,
    )
    other_half = lax.ppermute(sent_half, AXES, swap)
    message_one, picked = run(
        messages,
        "messages",
        [pltpu.VMEM((node_dev, width), BF16), pltpu.VMEM((mirrors, width), F32)],
        vmem=[in_count, grad_z_one, w_nbr_one, picking],
        flops=2 * node_dev * width * width,
    )

    columns = width * (half // mirrors + 1)
    payload_shape = (devices, per_peer, columns + LANES)
    (payload,) = run(
        join_first,
        "join_first",
        [pltpu.HBM(payload_shape, BF16)],
        vmem=[own_half, other_half, picked, bias_rows],
        scratch=[pltpu.VMEM(payload_shape, BF16), pltpu.SemaphoreType.DMA],
    )
    received = exchange(payload)
    mirror_back, local_grad, mirror_rows = run(
        local_back,
        "local_back",
        [
            pltpu.VMEM((mirrors, width), F32),
            pltpu.VMEM((node_dev, width), F32),
            pltpu.VMEM((mirrors, slots), BF16),
        ],
        hbm=[counts],
        vmem=[message_one, grad_z_one, w_self_one],
        scratch=[pltpu.VMEM((node_dev, slots), BF16), pltpu.SemaphoreType.DMA((2,))],
        flops=2 * node_dev * (slots + width) * width,
    )
    norm_factor = float(node_dev * devices) ** -0.5
    payload, mirrored, grad_bias = run(
        functools.partial(join_second, norm_factor),
        "join_second",
        [
            pltpu.VMEM((devices, per_peer, columns), BF16),
            pltpu.VMEM((mirrors, width), BF16),
            pltpu.HBM((1, width), F32),
        ],
        vmem=[received, mirror_back, mirror_counts],
        scratch=[pltpu.VMEM((1, width), F32), pltpu.SemaphoreType.DMA],
    )
    received = exchange(payload)
    other = lax.ppermute(received, AXES, swap)
    grad_features, grad_weights = run(
        finish,
        "finish",
        [pltpu.HBM((node_dev, width), BF16), pltpu.HBM((2 * half, width), F32)],
        smem=[core.reshape(1)],
        vmem=[received, mirrored, picking, mirror_rows, local_grad],
        scratch=[
            pltpu.VMEM((node_dev, width), BF16),
            pltpu.VMEM((half, width), F32),
            pltpu.SemaphoreType.DMA((2,)),
        ],
        flops=6 * node_dev * mirrors * width,
    )
    (grad_weights,) = run(
        finish_other,
        "finish_other",
        [pltpu.HBM((2 * half, width), F32)],
        smem=[core.reshape(1)],
        hbm=[grad_weights],
        vmem=[other],
        scratch=[pltpu.VMEM((half, width), F32), pltpu.SemaphoreType.DMA],
        aliases={1: 0},
    )
    return (
        grad_features,
        grad_weights.reshape(4, width, width),
        grad_bias.reshape(width),
    )


def solution(mesh):
    by_device = P(AXES)
    return jax.shard_map(
        shards,
        mesh=mesh,
        in_specs=(
            P(AXES, None),
            P(AXES, None),
            P(),
            P(),
            P(),
            P(),
            P(),
            by_device,
            P(AXES, None, None),
            P(AXES, None),
            P(AXES, None),
            by_device,
        ),
        out_specs=(P(AXES, None), P(), P()),
        check_vma=False,
    )
```

time: 74.7 us -> 71.4 us (0.956)
  blocking collectives: 0 us -> 14.3 us
  waiting for transfers between devices: 27.8 us -> 18.2 us
  starting transfers between devices: 17.3 us -> 12.8 us
  matrix products: 2.39 us -> 0 us
  other arithmetic: 1.15 us -> 0 us
  Pallas kernels: 21.1 us -> 21.9 us
    all_to_all x0 -> x1, blocking collectives: none -> 14.3 us  [exchange(): return lax.all_to_all(rows, AXES, split_axis=0, concat_axis=0, tiled=True)]
    all_to_all x4 -> x3, waiting for transfers between devices: 26.7 us -> 17.3 us  [exchange(): return lax.all_to_all(rows, AXES, split_axis=0, concat_axis=0, tiled=True)]
    all_to_all x4 -> x3, starting transfers between devices: 16.9 us -> 12.5 us  [exchange(): return lax.all_to_all(rows, AXES, split_axis=0, concat_axis=0, tiled=True)]
    dot_general x2 -> x0, matrix products: 2.39 us -> none  [tdot(): lax.dot_general(left, right, (((0,), (0,)), ((), ())), preferred_element_...]
    convert_element_type x1 -> x0, other arithmetic: 1.06 us -> none  [shards(): jnp.concatenate([first, second], axis=0).astype(F32)]
    pallas_call x9 -> x11, Pallas kernels: 21.1 us -> 21.9 us  [run(): pl.pallas_call(kernel, out_shape=tuple(outs), in_specs=[pl.BlockSpec(memo...]
    unnamed x17 -> x10, local copies, waits for them, and re-layouts: 2.78 us -> 2.2 us
  transfers between devices with their start and end apart: 6 -> 5, of which waited for: 6 -> 5; matrix products, arithmetic and copies ran while one was open for 4% -> 0% of each run, Pallas kernels for 18% -> 18%
where the time goes in v3:
time: 71.4 us; the launch traced here: 70.9 us
  Pallas kernels  21.9 us (31%)
  waiting for transfers between devices  18.2 us (25%)
  blocking collectives  14.3 us (20%)
  starting transfers between devices  12.8 us (18%)
  local copies, waits for them, and re-layouts  2.27 us (3%)
  between operations  1.43 us (2%)
    pallas_call x11, Pallas kernels, run(): pl.pallas_call(kernel, out_shape=tuple(outs), in_specs=[pl.BlockSpec(memo...  21.9 us
    all_to_all x3, waiting for transfers between devices, exchange(): return lax.all_to_all(rows, AXES, split_axis=0, concat_axis=0, tiled=True)  17.3 us
    all_to_all x1, blocking collectives, exchange(): return lax.all_to_all(rows, AXES, split_axis=0, concat_axis=0, tiled=True)  14.3 us
    all_to_all x3, starting transfers between devices, exchange(): return lax.all_to_all(rows, AXES, split_axis=0, concat_axis=0, tiled=True)  12.5 us
    unnamed x10, local copies, waits for them, and re-layouts  2.2 us
  transfers between devices with their start and end apart: 5, of which 5 were waited for; matrix products, arithmetic and copies ran while one was open for 0% of the time, Pallas kernels for 18%

profile of v3, /device:TPU:0, one launch (start us, length us, event | category | flops | bytes accessed | tf_op | source)
XLA Modules:
  0.0 70.9 jit_solution(13092959084022818179)
XLA Ops:
  1.3 2.4 %pick_rows.1 = (bf16[32,4,512]{2,1,0:T(4,128)(2,1)}, bf16[1024,256]{1,0:T(8,128)(2,1)S(1)}, bf16[128,1024]{1,0:T(8,128)(2,1)S(1)}, s32[128,16]{1,0:T(8,128)S(1)}, s32[16,128]{1,0:T(8,128)S(1)}) custom-call(s32[1]{0:T(128)S(6)} %copy.17.edge_count, bf16[1024,256]{1,0:T(8,128)(2,1)} %features_at.7, bf16[1024,256]{1,0:T(8,128)(2,1)} %cotangent_at.3, ...), custom_call_target="tpu_custom_call" | custom-call | flops 134217728 | tf_op jit(solution)/shard_map/pick_rows/pallas_call | solution.py:40
  3.7 7.3 %all-to-all-start = ((bf16[32,4,512]{2,1,0:T(4,128)(2,1)}), bf16[32,4,512]{2,1,0:T(4,128)(2,1)S(1)}, u32[]{:S(2)}, u32[]{:S(2)}) async-start(bf16[32,4,512]{2,1,0:T(4,128)(2,1)} %get-tuple-element.31), calls=%async_computation | async-start | bytes 262144 | tf_op jit(solution)/shard_map/all_to_all | solution.py:34
  11.0 4.1 %count_edges.1 = (bf16[1152,1152]{1,0:T(8,128)(2,1)}, bf16[128,128]{1,0:T(8,128)(2,1)S(1)}, f32[128,512]{1,0:T(8,128)S(1)}) custom-call(bf16[1024,256]{1,0:T(8,128)(2,1)} %features_at.7, bf16[1024,256]{1,0:T(8,128)(2,1)S(1)} %get-tuple-element.27.scaled, s32[128,16]{1,0:T(8,128)S(1)} %get-tuple-element.28.source_columns, s32[16,128]{1,0:T(8,128)S(1)} %get-tuple-element.29.targets), custom_call_target="tpu_custom_call" | custom-call | flops 5435817984 | tf_op jit(solution)/shard_map/count_edges/pallas_call | solution.py:40
  15.1 4.2 %all-to-all-done = bf16[32,4,512]{2,1,0:T(4,128)(2,1)S(1)} async-done(((bf16[32,4,512]{2,1,0:T(4,128)(2,1)}), bf16[32,4,512]{2,1,0:T(4,128)(2,1)S(1)}, u32[]{:S(2)}, u32[]{:S(2)}) %all-to-all-start) | async-done | bytes 131104 | tf_op jit(solution)/shard_map/all_to_all | solution.py:34
  19.3 0.9 %mirror_sums.1 = bf16[32,4,512]{2,1,0:T(4,128)(2,1)} custom-call(f32[128,512]{1,0:T(8,128)S(1)} %get-tuple-element.34.partial_in, bf16[128,128]{1,0:T(8,128)(2,1)S(1)} %get-tuple-element.35.mirror_counts, bf16[128,512]{1,0:T(8,128)(2,1)S(1)} %reshape.40.mirrored), custom_call_target="tpu_custom_call" | custom-call | flops 16777216 | tf_op jit(solution)/shard_map/mirror_sums/pallas_call | solution.py:40
  20.2 2.6 %all-to-all-start.1 = ((bf16[32,4,512]{2,1,0:T(4,128)(2,1)}), bf16[32,4,512]{2,1,0:T(4,128)(2,1)S(1)}, u32[]{:S(2)}, u32[]{:S(2)}) async-start(bf16[32,4,512]{2,1,0:T(4,128)(2,1)} %mirror_sums.1), calls=%async_computation.1 | async-start | bytes 262144 | tf_op jit(solution)/shard_map/all_to_all | solution.py:34
  22.8 4.0 %local_sums.1 = (f32[1024,256]{1,0:T(8,128)S(1)}, f32[1024,256]{1,0:T(8,128)S(1)}) custom-call(bf16[1152,1152]{1,0:T(8,128)(2,1)} %get-tuple-element.30.counts_at, bf16[1024,256]{1,0:T(8,128)(2,1)} %features_at.7, bf16[1024,256]{1,0:T(8,128)(2,1)S(1)} %get-tuple-element.27.scaled, bf16[128,512]{1,0:T(8,128)(2,1)S(1)} %reshape.40.mirrored), custom_call_target="tpu_custom_call" | custom-call | flops 1207959552 | tf_op jit(solution)/shard_map/local_sums/pallas_call | solution.py:40
  26.8 0.0 copy-start.3
  26.8 1.0 %copy-done.3 = f32[1024,256]{1,0:T(8,128)} copy-done((f32[1024,256]{1,0:T(8,128)}, f32[1024,256]{1,0:T(8,128)S(1)}, u32[]{:S(2)}) %copy-start.3) | copy-done | bytes 1048600
  27.8 3.2 %all-to-all-done.1 = bf16[32,4,512]{2,1,0:T(4,128)(2,1)S(1)} async-done(((bf16[32,4,512]{2,1,0:T(4,128)(2,1)}), bf16[32,4,512]{2,1,0:T(4,128)(2,1)S(1)}, u32[]{:S(2)}, u32[]{:S(2)}) %all-to-all-start.1) | async-done | bytes 131104 | tf_op jit(solution)/shard_map/all_to_all | solution.py:34
  31.1 1.2 %copy-done.4 = f32[1024,256]{1,0:T(8,128)S(1)} copy-done((f32[1024,256]{1,0:T(8,128)S(1)}, f32[1024,256]{1,0:T(8,128)}, u32[]{:S(2)}) %copy-start.4) | copy-done | bytes 1048600
  32.3 3.3 %middle.1 = (bf16[1024,256]{1,0:T(8,128)(2,1)S(1)}, bf16[512,256]{1,0:T(8,128)(2,1)S(1)}, f32[512,256]{1,0:T(8,128)S(1)}, f32[4,128]{1,0:T(4,128)S(1)}) custom-call(s32[1]{0:T(128)} %bitcast.core, s32[8,128]{1,0:T(8,128)} %bitcast.11, bf16[256,256]{1,0:T(8,128)(2,1)} %w_nbr_one.1, bf16[256,256]{1,0:T(8,128)(2,1)} %w_self_one.1, f32[1,256]{1,0:T(1,128)} %bitcast.17, ...), custom_call_target="tpu_custom_call" | custom-call | flops 1610612736 | tf_op jit(solution)/shard_map/middle/pallas_call | solution.py:40
  35.6 0.3 collective-permute-start
  35.9 0.6 messages.1
  36.5 0.7 collective-permute-done.other_half
  37.2 0.9 %join_first.1 = bf16[32,4,1408]{2,1,0:T(4,128)(2,1)} custom-call(f32[512,256]{1,0:T(8,128)S(1)} %get-tuple-element.37.own_half, bf16[512,256]{1,0:T(8,128)(2,1)S(1)} %collective-permute-done.other_half, f32[128,256]{1,0:T(8,128)S(1)} %get-tuple-element.40.picked, f32[4,128]{1,0:T(4,128)S(1)} %get-tuple-element.41.bias_rows), custom_call_target="tpu_custom_call" | custom-call | tf_op jit(solution)/shard_map/join_first/pallas_call | solution.py:40
  38.1 2.6 %all-to-all-start.2 = ((bf16[32,4,1408]{2,1,0:T(4,128)(2,1)}), bf16[32,4,1408]{2,1,0:T(4,128)(2,1)S(1)}, u32[]{:S(2)}, u32[]{:S(2)}) async-start(bf16[32,4,1408]{2,1,0:T(4,128)(2,1)} %join_first.1), calls=%async_computation.2 | async-start | bytes 720896 | tf_op jit(solution)/shard_map/all_to_all | solution.py:34
  40.7 2.6 %local_back.1 = (f32[128,256]{1,0:T(8,128)S(1)}, f32[1024,256]{1,0:T(8,128)S(1)}, bf16[128,1152]{1,0:T(8,128)(2,1)S(1)}) custom-call(bf16[1152,1152]{1,0:T(8,128)(2,1)} %get-tuple-element.30.counts_at, bf16[1024,256]{1,0:T(8,128)(2,1)S(1)} %get-tuple-element.42.message_one, bf16[1024,256]{1,0:T(8,128)(2,1)S(1)} %get-tuple-element.39.grad_z, ...), custom_call_target="tpu_custom_call" | custom-call | flops 738197504 | tf_op jit(solution)/shard_map/local_back/pallas_call | solution.py:40
  43.3 10.0 %all-to-all-done.2.received = bf16[32,4,1408]{2,1,0:T(4,128)(2,1)S(1)} async-done(((bf16[32,4,1408]{2,1,0:T(4,128)(2,1)}), bf16[32,4,1408]{2,1,0:T(4,128)(2,1)S(1)}, u32[]{:S(2)}, u32[]{:S(2)}) %all-to-all-start.2) | async-done | bytes 360480 | tf_op jit(solution)/shard_map/all_to_all | solution.py:34
  53.3 0.9 %join_second.1 = (bf16[32,4,1280]{2,1,0:T(4,128)(2,1)S(1)}, bf16[128,256]{1,0:T(8,128)(2,1)S(1)}, f32[1,256]{1,0:T(1,128)}) custom-call(bf16[32,4,1408]{2,1,0:T(4,128)(2,1)S(1)} %all-to-all-done.2.received, f32[128,256]{1,0:T(8,128)S(1)} %get-tuple-element.43.mirror_partial, bf16[128,128]{1,0:T(8,128)(2,1)S(1)} %get-tuple-element.35.mirror_counts), custom_call_target="tpu_custom_call" | custom-call | tf_op jit(solution)/shard_map/join_second/pallas_call | solution.py:40
  54.2 14.3 %all_to_all.20.received = bf16[32,4,1280]{2,1,0:T(4,128)(2,1)S(1)} all-to-all(bf16[32,4,1280]{2,1,0:T(4,128)(2,1)S(1)} %get-tuple-element.44), channel_id=1, replica_groups=mesh['dom'=8,'sub'=4] {'dom','sub'}, dimensions={0} | all-to-all | bytes 655360 | tf_op jit(solution)/shard_map/all_to_all | solution.py:34
  68.5 1.4 %finish.1 = (bf16[1024,256]{1,0:T(8,128)(2,1)}, f32[1024,256]{1,0:T(8,128)}) custom-call(s32[1]{0:T(128)} %bitcast.core, bf16[32,4,1280]{2,1,0:T(4,128)(2,1)S(1)} %all_to_all.20.received, bf16[128,256]{1,0:T(8,128)(2,1)S(1)} %get-tuple-element.45.mirrored, bf16[128,1024]{1,0:T(8,128)(2,1)S(1)} %get-tuple-element.36.picking, ...), custom_call_target="tpu_custom_call" | custom-call | flops 201326592 | tf_op jit(solution)/shard_map/finish/pallas_call | solution.py:40
  69.9 0.2 collective-permute-done.1.received
  70.1 0.8 %finish_other.1 = f32[1024,256]{1,0:T(8,128)} custom-call(s32[1]{0:T(128)} %bitcast.core, f32[1024,256]{1,0:T(8,128)} %get-tuple-element.49.weights_in, bf16[32,4,1280]{2,1,0:T(4,128)(2,1)S(1)} %collective-permute-done.1.received), custom_call_target="tpu_custom_call", output_to_operand_aliasing={{}: (1, {})} | custom-call | tf_op jit(solution)/shard_map/finish_other/pallas_call | solution.py:40
  (10 shorter events, 0.1 us)
Async XLA Ops:
  3.7 15.5 %all-to-all-start = ((bf16[32,4,512]{2,1,0:T(4,128)(2,1)}), bf16[32,4,512]{2,1,0:T(4,128)(2,1)S(1)}, u32[]{:S(2)}, u32[]{:S(2)}) async-start(bf16[32,4,512]{2,1,0:T(4,128)(2,1)} %get-tuple-element.31), calls=%async_computation | async-start | bytes 262144 | tf_op jit(solution)/shard_map/all_to_all | solution.py:34
  20.2 10.8 %all-to-all-start.1 = ((bf16[32,4,512]{2,1,0:T(4,128)(2,1)}), bf16[32,4,512]{2,1,0:T(4,128)(2,1)S(1)}, u32[]{:S(2)}, u32[]{:S(2)}) async-start(bf16[32,4,512]{2,1,0:T(4,128)(2,1)} %mirror_sums.1), calls=%async_computation.1 | async-start | bytes 262144 | tf_op jit(solution)/shard_map/all_to_all | solution.py:34
  26.8 1.0 %copy-start.3 = (f32[1024,256]{1,0:T(8,128)}, f32[1024,256]{1,0:T(8,128)S(1)}, u32[]{:S(2)}) copy-start(f32[1024,256]{1,0:T(8,128)S(1)} %get-tuple-element.33.backward) | copy-start | bytes 3145732
  31.0 1.2 %copy-start.4 = (f32[1024,256]{1,0:T(8,128)S(1)}, f32[1024,256]{1,0:T(8,128)}, u32[]{:S(2)}) copy-start(f32[1024,256]{1,0:T(8,128)} %copy-done.3) | copy-start | bytes 3145732
  32.3 3.6 %copy-start = (bf16[256,256]{1,0:T(8,128)(2,1)S(1)}, bf16[256,256]{1,0:T(8,128)(2,1)}, u32[]{:S(2)}) copy-start(bf16[256,256]{1,0:T(8,128)(2,1)} %w_nbr_one.1) | copy-start | bytes 393220
  32.3 3.6 %copy-start.2 = (s32[1024]{0:T(1024)S(1)}, s32[1024]{0:T(1024)}, u32[]{:S(2)}) copy-start(s32[1024]{0:T(1024)} %param.19) | copy-start | bytes 12292
  35.6 5.1 %copy-start.1 = (bf16[256,256]{1,0:T(8,128)(2,1)S(1)}, bf16[256,256]{1,0:T(8,128)(2,1)}, u32[]{:S(2)}) copy-start(bf16[256,256]{1,0:T(8,128)(2,1)} %w_self_one.1) | copy-start | bytes 393220
  35.6 1.6 %collective-permute-start = (bf16[512,256]{1,0:T(8,128)(2,1)S(1)}, bf16[512,256]{1,0:T(8,128)(2,1)S(1)}, u32[]{:S(2)}, u32[]{:S(2)}) collective-permute-start(bf16[512,256]{1,0:T(8,128)(2,1)S(1)} %get-tuple-element.38), channel_id=1, source_target_pairs={{0,1},{1,0},{2,3},{3,2},{4,5},{5,4},{6,7},{7,6},{8,9},{9,8},{10,11... | collective-permute-start | bytes 786440 | tf_op jit(solution)/shard_map/ppermute | solution.py:639
  38.1 15.2 %all-to-all-start.2 = ((bf16[32,4,1408]{2,1,0:T(4,128)(2,1)}), bf16[32,4,1408]{2,1,0:T(4,128)(2,1)S(1)}, u32[]{:S(2)}, u32[]{:S(2)}) async-start(bf16[32,4,1408]{2,1,0:T(4,128)(2,1)} %join_first.1), calls=%async_computation.2 | async-start | bytes 720896 | tf_op jit(solution)/shard_map/all_to_all | solution.py:34
  68.5 1.6 %collective-permute-start.1 = (bf16[32,4,1280]{2,1,0:T(4,128)(2,1)S(1)}, bf16[32,4,1280]{2,1,0:T(4,128)(2,1)S(1)}, u32[]{:S(2)}, u32[]{:S(2)}) collective-permute-start(bf16[32,4,1280]{2,1,0:T(4,128)(2,1)S(1)} %all_to_all.20.received), channel_id=1, source_target_pairs={{0,1},{1,0},{2,3},{3,2},{4,5},{5,4},{6,7},{7,6},{8,9},{9,8},{10,11... | collective-permute-start | bytes 983048 | tf_op jit(solution)/shard_map/ppermute | solution.py:684

commit v4 on v3

--- a/solution.py
+++ b/solution.py
@@ -110,7 +110,6 @@
     sources_at,
     targets_at,
     payload,
-    scaled,
     picking,
     source_columns,
     targets,
@@ -156,12 +155,6 @@
     rows_out[:, :, :width] = by_peer(dot(picks, features[...]), devices)
     out_copy = pltpu.make_async_copy(rows_out, payload, out_semaphore)
     out_copy.start()
-    columns = inverse_rows.T
-    for block in range(node_dev // LANES):
-        rows = pl.ds(block * LANES, LANES)
-        scaled[rows, :] = (
-            cotangent[rows, :].astype(F32) * columns[:, block : block + 1]
-        ).astype(BF16)
     copies[4].wait()
     edge_ids = iota(sources.shape, 0) * LANES + iota(sources.shape, 1)
     source_columns[...] = jnp.where(edge_ids < edge_count[0], sources[...], -1).T
@@ -171,14 +164,19 @@
 
 def count_edges(
     features_at,
-    scaled,
+    cotangent_at,
+    in_count_at,
     source_columns,
     targets,
     counts_out,
+    scaled_out,
     mirror_out,
     partial_out,
     features,
-    semaphore,
+    cotangent,
+    in_count,
+    semaphores,
+    scaled,
     from_hot,
     into_hot,
     counts,
@@ -186,8 +184,9 @@
 ):
     node_dev, width = features.shape
     slots, edges = into_hot.shape
-    feature_copy = pltpu.make_async_copy(features_at, features, semaphore)
-    feature_copy.start()
+    loads = start_all(
+        [features_at, cotangent_at, in_count_at], [features, cotangent, in_count], semaphores
+    )
     lane_ids = iota((LANES, slots), 1, I16)
     for block in range(edges // LANES):
         column = jnp.broadcast_to(source_columns[:, block : block + 1], (LANES, LANES)).astype(I16)
@@ -211,7 +210,17 @@
         )
         copy.start()
         sends.append(copy)
-    feature_copy.wait()
+    for copy in loads:
+        copy.wait()
+    columns = inverse_columns(in_count)
+    for index, start in enumerate(range(0, node_dev, BLOCK)):
+        rows = pl.ds(start, BLOCK)
+        scaled[rows, :] = (
+            cotangent[rows, :].astype(F32) * block_inverse(columns, index)
+        ).astype(BF16)
+    copy = pltpu.make_async_copy(scaled, scaled_out, out_semaphores.at[len(sends)])
+    copy.start()
+    sends.append(copy)
     mirror_out[...] = counts[node_dev:, node_dev:]
     partial_out[:, :width] = dot(counts[node_dev:, :node_dev], features[...])
     partial_out[:, width:] = tdot(counts[:node_dev, node_dev:], scaled[...])
@@ -231,20 +240,53 @@
 
 
 def local_sums(
-    counts_at, features_at, scaled, mirrored, forward, backward, counts, features, semaphores
+    counts_at,
+    features_at,
+    w_nbr_one_at,
+    w_self_one_at,
+    bias_one_at,
+    in_count_at,
+    scaled_at,
+    mirrored,
+    forward,
+    features,
+    w_nbr_one,
+    w_self_one,
+    bias_one,
+    in_count,
+    backward_at,
+    counts,
+    scaled,
+    backward,
+    block_semaphores,
+    out_semaphores,
+    semaphores,
 ):
     node_dev, width = features.shape
     slots = counts.shape[0]
     blocks = [(start, min(BLOCK, slots - start)) for start in range(0, slots, BLOCK)]
-    feature_copy = pltpu.make_async_copy(features_at, features, semaphores.at[len(blocks)])
-    feature_copy.start()
+    loads = start_all([features_at], [features], semaphores)
     copies = []
     for index, (start, size) in enumerate(blocks):
         rows = pl.ds(start, size)
-        copy = pltpu.make_async_copy(counts_at.at[rows], counts.at[rows], semaphores.at[index])
+        copy = pltpu.make_async_copy(
+            counts_at.at[rows], counts.at[rows], block_semaphores.at[index]
+        )
         copy.start()
         copies.append(copy)
-    feature_copy.wait()
+    for index, (source, buffer) in enumerate(
+        (
+            (scaled_at, scaled),
+            (w_nbr_one_at, w_nbr_one),
+            (w_self_one_at, w_self_one),
+            (bias_one_at, bias_one),
+            (in_count_at, in_count),
+        )
+    ):
+        copy = pltpu.make_async_copy(source, buffer, semaphores.at[index + 1])
+        copy.start()
+        loads.append(copy)
+    loads[0].wait()
     for (start, size), copy in zip(blocks, copies):
         copy.wait()
         if start < node_dev:
@@ -252,88 +294,82 @@
             forward[rows, :] = dot(counts[rows, :node_dev], features[...]) + dot(
                 counts[rows, node_dev:], mirrored[:, :width]
             )
-    for start in range(0, node_dev, BLOCK):
+    loads[1].wait()
+    sends = []
+    for index, start in enumerate(range(0, node_dev, BLOCK)):
         rows = pl.ds(start, BLOCK)
         backward[rows, :] = tdot(counts[:node_dev, rows], scaled[...]) + tdot(
             counts[node_dev:, rows], mirrored[:, width:]
         )
+        copy = pltpu.make_async_copy(
+            backward.at[rows], backward_at.at[rows], out_semaphores.at[index]
+        )
+        copy.start()
+        sends.append(copy)
+    for copy in loads[2:] + sends:
+        copy.wait()
+
+
+def block_inverse(columns, index):
+    first = index * BLOCK // LANES
+    return jnp.concatenate(
+        [columns[:, b : b + 1] for b in range(first, first + BLOCK // LANES)], axis=0
+    )
 
 
 def middle(
     core,
-    in_count_at,
-    w_nbr_one_at,
-    w_self_one_at,
-    bias_one_at,
-    features_at,
     w_nbr_two_at,
     w_self_two_at,
     cotangent_at,
+    backward_at,
     forward,
-    backward,
     returned,
     picking,
-    grad_z,
-    sent_half,
-    own_half,
-    bias_rows,
-    in_count,
+    features,
     w_nbr_one,
     w_self_one,
     bias_one,
-    features,
-    w_nbr_two,
-    w_self_two,
-    cotangent,
-    semaphores,
+    in_count,
+    grad_z,
+    sent_half,
+    bias_rows,
     mean_one,
     h_one,
     pulled,
+    cotangent,
+    w_nbr_two,
+    w_self_two,
+    backward,
+    semaphores,
     slope,
 ):
     node_dev, width = features.shape
     copies = start_all(
-        [
-            in_count_at,
-            w_nbr_one_at,
-            w_self_one_at,
-            bias_one_at,
-            features_at,
-            w_nbr_two_at,
-            w_self_two_at,
-            cotangent_at,
-        ],
-        [in_count, w_nbr_one, w_self_one, bias_one, features, w_nbr_two, w_self_two, cotangent],
+        [backward_at, w_nbr_two_at, w_self_two_at, cotangent_at],
+        [backward, w_nbr_two, w_self_two, cotangent],
         semaphores,
     )
     blocks = [pl.ds(start, BLOCK) for start in range(0, node_dev, BLOCK)]
-    copies[0].wait()
     columns = inverse_columns(in_count)
     for index, rows in enumerate(blocks):
-        placed = tdot(picking[:, rows], returned[...])
-        first = index * BLOCK // LANES
-        inverse = jnp.concatenate(
-            [columns[:, b : b + 1] for b in range(first, first + BLOCK // LANES)], axis=0
-        )
-        mean_one[rows, :] = ((forward[rows, :] + placed[:, :width]) * inverse).astype(BF16)
-        pulled[rows, :] = (backward[rows, :] + placed[:, width:]).astype(BF16)
-    for copy in copies[1:5]:
-        copy.wait()
-    for rows in blocks:
+        placed = tdot(picking[:, rows], returned[:, :width])
+        mean = ((forward[rows, :] + placed) * block_inverse(columns, index)).astype(BF16)
+        mean_one[rows, :] = mean
         z_one = (
-            dot(features[rows, :], w_self_one[...])
-            + dot(mean_one[rows, :], w_nbr_one[...])
-            + bias_one[...]
+            dot(features[rows, :], w_self_one[...]) + dot(mean, w_nbr_one[...]) + bias_one[...]
         )
         sigmoid = 1.0 / (1.0 + jnp.exp(-z_one))
         h_one[rows, :] = (z_one * sigmoid).astype(BF16)
         slope[rows, :] = sigmoid * (1.0 + z_one * (1.0 - sigmoid))
-    for copy in copies[5:]:
+    for copy in copies:
         copy.wait()
     bias_total = jnp.zeros((1, width), F32)
     for rows in blocks:
+        pull = (backward[rows, :] + tdot(picking[:, rows], returned[:, width:])).astype(BF16)
+        pulled[rows, :] = pull
         grad_h = dot_transposed(cotangent[rows, :], w_self_two[...]) + dot_transposed(
-            pulled[rows, :], w_nbr_two[...]
+            pull, w_nbr_two[...]
         )
         grad = (grad_h * slope[rows, :]).astype(BF16)
         grad_z[rows, :] = grad
@@ -346,37 +382,50 @@
                 part[:, block * LANES : (block + 1) * LANES]
             )
 
-    def early():
-        return tdot(features[...], grad_z[...]), tdot(mean_one[...], grad_z[...])
-
-    def late():
-        return tdot(h_one[...], cotangent[...]), tdot(h_one[...], pulled[...])
-
-    for parity, (sent, owned) in enumerate(((late, early), (early, late))):
-
-        @pl.when(core[0] == parity)
-        def _(sent=sent, owned=owned):
-            top, bottom = sent()
-            sent_half[:width, :] = top.astype(BF16)
-            sent_half[width:, :] = bottom.astype(BF16)
-            top, bottom = owned()
-            own_half[:width, :] = top
-            own_half[width:, :] = bottom
-
-
-def messages(in_count, grad_z, w_nbr_one, picking, message_one, picked):
+    @pl.when(core[0] == 0)
+    def _():
+        sent_half[:width, :] = tdot(h_one[...], cotangent[...]).astype(BF16)
+        sent_half[width:, :] = tdot(h_one[...], pulled[...]).astype(BF16)
+
+    @pl.when(core[0] == 1)
+    def _():
+        sent_half[:width, :] = tdot(features[...], grad_z[...]).astype(BF16)
+        sent_half[width:, :] = tdot(mean_one[...], grad_z[...]).astype(BF16)
+
+
+def messages(
+    core,
+    in_count,
+    grad_z,
+    w_nbr_one,
+    picking,
+    features,
+    mean_one,
+    h_one,
+    cotangent,
+    pulled,
+    message_one,
+    picked,
+    own_half,
+):
     node_dev, width = grad_z.shape
     columns = inverse_columns(in_count)
-    for start in range(0, node_dev, BLOCK):
+    for index, start in enumerate(range(0, node_dev, BLOCK)):
         rows = pl.ds(start, BLOCK)
-        inverse = jnp.concatenate(
-            [columns[:, b : b + 1] for b in range(start // LANES, (start + BLOCK) // LANES)],
-            axis=0,
-        )
         message_one[rows, :] = (
-            dot_transposed(grad_z[rows, :], w_nbr_one[...]) * inverse
+            dot_transposed(grad_z[rows, :], w_nbr_one[...]) * block_inverse(columns, index)
         ).astype(BF16)
     picked[...] = dot(picking[...], message_one[...])
+
+    @pl.when(core[0] == 0)
+    def _():
+        own_half[:width, :] = tdot(features[...], grad_z[...])
+        own_half[width:, :] = tdot(mean_one[...], grad_z[...])
+
+    @pl.when(core[0] == 1)
+    def _():
+        own_half[:width, :] = tdot(h_one[...], cotangent[...])
+        own_half[width:, :] = tdot(h_one[...], pulled[...])
 
 
 def join_first(own_half, other_half, picked, bias_rows, payload, rows_out, out_semaphore):
@@ -433,9 +482,7 @@
     mirror_counts,
     payload,
     mirrored_out,
-    bias_out,
     bias_total,
-    semaphore,
 ):
     devices, per_peer, _ = payload.shape
     mirrors, width = mirror_partial.shape
@@ -463,7 +510,6 @@
         bias_total[:, block * LANES : (block + 1) * LANES] = (
             sums[block : block + 1, :] + sums[parts + block : parts + block + 1, :]
         )
-    send(bias_total, bias_out, semaphore)
 
 
 def finish(
@@ -473,8 +519,10 @@
     picking,
     mirror_rows,
     local_grad,
+    bias_total,
     features_at,
     weights_at,
+    bias_at,
     features_out,
     weights_out,
     semaphores,
@@ -492,6 +540,8 @@
         weights_out, weights_at.at[pl.ds(mine, half)], semaphores.at[0]
     )
     weights_copy.start()
+    bias_copy = pltpu.make_async_copy(bias_total, bias_at, semaphores.at[2])
+    bias_copy.start()
     returned = by_row(received[:, :, :width]).astype(BF16)
     for start in range(0, node_dev, BLOCK):
         rows = pl.ds(start, BLOCK)
@@ -503,6 +553,7 @@
     features_copy = pltpu.make_async_copy(features_out, features_at, semaphores.at[1])
     features_copy.start()
     weights_copy.wait()
+    bias_copy.wait()
     features_copy.wait()
 
 
@@ -547,12 +598,11 @@
     blocks = -(-slots // BLOCK)
 
     payload_shape = (devices, per_peer, 2 * width)
-    payload, scaled, picking, source_columns, targets = run(
+    payload, picking, source_columns, targets = run(
         pick_rows,
         "pick_rows",
         [
             pltpu.HBM(payload_shape, BF16),
-            pltpu.VMEM((node_dev, width), BF16),
             pltpu.VMEM((mirrors, node_dev), BF16),
             pltpu.VMEM((LANES, edges // LANES), I32),
             pltpu.VMEM(targets.shape, I32),
@@ -565,23 +615,26 @@
     )
     mirrored = exchange(payload).reshape(mirrors, 2 * width)
 
-    counts, mirror_counts, partial_sums = run(
+    rows_bf16 = pltpu.VMEM((node_dev, width), BF16)
+    rows_f32 = pltpu.VMEM((node_dev, width), F32)
+    counts, scaled, mirror_counts, partial_sums = run(
         count_edges,
         "count_edges",
         [
             pltpu.HBM((slots, slots), BF16),
+            pltpu.HBM((node_dev, width), BF16),
             pltpu.VMEM((mirrors, mirrors), BF16),
             pltpu.VMEM((mirrors, 2 * width), F32),
         ],
-        hbm=[features],
-        vmem=[scaled, source_columns, targets],
-        scratch=[
-            pltpu.VMEM((node_dev, width), BF16),
-            pltpu.SemaphoreType.DMA,
+        hbm=[features, cotangent, in_count],
+        vmem=[source_columns, targets],
+        scratch=staged_for(3, features, cotangent, in_count)
+        + [
+            rows_bf16,
             pltpu.VMEM((edges, slots), F8),
             pltpu.VMEM((slots, edges), F8),
             pltpu.VMEM((slots, slots), BF16),
-            pltpu.SemaphoreType.DMA((blocks,)),
+            pltpu.SemaphoreType.DMA((blocks + 1,)),
         ],
         flops=2 * slots * edges * slots,
     )
@@ -594,55 +647,78 @@
         flops=4 * mirrors * mirrors * width,
     )
     returned = exchange(payload).reshape(mirrors, 2 * width)
-    forward, backward = run(
+    weight = pltpu.VMEM((width, width), BF16)
+    forward, features_in, w_nbr_in, w_self_in, bias_in, in_count_in, backward = run(
         local_sums,
         "local_sums",
-        [pltpu.VMEM((node_dev, width), F32)] * 2,
-        hbm=[counts, features],
-        vmem=[scaled, mirrored],
+        [
+            rows_f32,
+            rows_bf16,
+            weight,
+            weight,
+            pltpu.VMEM((1, width), F32),
+            pltpu.VMEM(in_count.shape, I32),
+            pltpu.HBM((node_dev, width), F32),
+        ],
+        hbm=[counts, features, w_nbr_one, w_self_one, bias_one.reshape(1, -1), in_count, scaled],
+        vmem=[mirrored],
         scratch=[
             pltpu.VMEM((slots, slots), BF16),
-            pltpu.VMEM((node_dev, width), BF16),
-            pltpu.SemaphoreType.DMA((blocks + 1,)),
+            rows_bf16,
+            rows_f32,
+            pltpu.SemaphoreType.DMA((blocks,)),
+            pltpu.SemaphoreType.DMA((node_dev // BLOCK,)),
+            pltpu.SemaphoreType.DMA((6,)),
         ],
         flops=4 * node_dev * slots * width,
     )
 
     half = 2 * width
-    loaded = [
-        in_count,
-        w_nbr_one,
-        w_self_one,
-        bias_one.reshape(1, -1),
-        features,
-        w_nbr_two,
-        w_self_two,
-        cotangent,
-    ]
-    grad_z_one, sent_half, own_half, bias_rows = run(
+    grad_z_one, sent_half, bias_rows, mean_one, h_one, pulled, cotangent_in = run(
         middle,
         "middle",
         [
-            pltpu.VMEM((node_dev, width), BF16),
+            rows_bf16,
             pltpu.VMEM((half, width), BF16),
-            pltpu.VMEM((half, width), F32),
             pltpu.VMEM((2 * width // LANES, LANES), F32),
+            rows_bf16,
+            rows_bf16,
+            rows_bf16,
+            rows_bf16,
         ],
         smem=[core.reshape(1)],
-        hbm=loaded,
-        vmem=[forward, backward, returned, picking],
-        scratch=staged_for(len(loaded), *loaded)
-        + [pltpu.VMEM((node_dev, width), BF16)] * 3
-        + [pltpu.VMEM((node_dev, width), F32)],
-        flops=24 * node_dev * width * width,
+        hbm=[w_nbr_two, w_self_two, cotangent, backward],
+        vmem=[
+            forward,
+            returned,
+            picking,
+            features_in,
+            w_nbr_in,
+            w_self_in,
+            bias_in,
+            in_count_in,
+        ],
+        scratch=[weight, weight, rows_f32, pltpu.SemaphoreType.DMA((4,)), rows_f32],
+        flops=20 * node_dev * width * width,
     )
     other_half = lax.ppermute(sent_half, AXES, swap)
-    message_one, picked = run(
+    message_one, picked, own_half = run(
         messages,
         "messages",
-        [pltpu.VMEM((node_dev, width), BF16), pltpu.VMEM((mirrors, width), F32)],
-        vmem=[in_count, grad_z_one, w_nbr_one, picking],
-        flops=2 * node_dev * width * width,
+        [rows_bf16, pltpu.VMEM((mirrors, width), F32), pltpu.VMEM((half, width), F32)],
+        smem=[core.reshape(1)],
+        vmem=[
+            in_count_in,
+            grad_z_one,
+            w_nbr_in,
+            picking,
+            features_in,
+            mean_one,
+            h_one,
+            cotangent_in,
+            pulled,
+        ],
+        flops=6 * node_dev * width * width,
     )
 
     columns = width * (half // mirrors + 1)
@@ -664,34 +740,37 @@
             pltpu.VMEM((mirrors, slots), BF16),
         ],
         hbm=[counts],
-        vmem=[message_one, grad_z_one, w_self_one],
+        vmem=[message_one, grad_z_one, w_self_in],
         scratch=[pltpu.VMEM((node_dev, slots), BF16), pltpu.SemaphoreType.DMA((2,))],
         flops=2 * node_dev * (slots + width) * width,
     )
     norm_factor = float(node_dev * devices) ** -0.5
-    payload, mirrored, grad_bias = run(
+    payload, mirrored, bias_total = run(
         functools.partial(join_second, norm_factor),
         "join_second",
         [
             pltpu.VMEM((devices, per_peer, columns), BF16),
             pltpu.VMEM((mirrors, width), BF16),
-            pltpu.HBM((1, width), F32),
+            pltpu.VMEM((1, width), F32),
         ],
         vmem=[received, mirror_back, mirror_counts],
-        scratch=[pltpu.VMEM((1, width), F32), pltpu.SemaphoreType.DMA],
     )
     received = exchange(payload)
     other = lax.ppermute(received, AXES, swap)
-    grad_features, grad_weights = run(
+    grad_features, grad_weights, grad_bias = run(
         finish,
         "finish",
-        [pltpu.HBM((node_dev, width), BF16), pltpu.HBM((2 * half, width), F32)],
+        [
+            pltpu.HBM((node_dev, width), BF16),
+            pltpu.HBM((2 * half, width), F32),
+            pltpu.HBM((1, width), F32),
+        ],
         smem=[core.reshape(1)],
-        vmem=[received, mirrored, picking, mirror_rows, local_grad],
+        vmem=[received, mirrored, picking, mirror_rows, local_grad, bias_total],
         scratch=[
             pltpu.VMEM((node_dev, width), BF16),
             pltpu.VMEM((half, width), F32),
-            pltpu.SemaphoreType.DMA((2,)),
+            pltpu.SemaphoreType.DMA((3,)),
         ],
         flops=6 * node_dev * mirrors * width,
     )

time: 71.4 us -> 69.3 us (0.971)
  local copies, waits for them, and re-layouts: 2.27 us -> 0.07 us
  Pallas kernels: 21.9 us -> 23.1 us
  waiting for transfers between devices: 18.2 us -> 17.3 us
    unnamed x10 -> x0, local copies, waits for them, and re-layouts: 2.2 us -> none
    pallas_call x11, Pallas kernels: 21.9 us -> 23.1 us  [run(): pl.pallas_call(kernel, out_shape=tuple(outs), in_specs=[pl.BlockSpec(memo...]
  transfers between devices with their start and end apart: 5 -> 5, of which waited for: 5 -> 5; matrix products, arithmetic and copies ran while one was open for 0% -> 0% of each run, Pallas kernels for 18% -> 21%
where the time goes in v4:
time: 69.3 us; the launch traced here: 68.9 us
  Pallas kernels  23.1 us (33%)
  waiting for transfers between devices  17.3 us (25%)
  blocking collectives  14.3 us (21%)
  starting transfers between devices  12.8 us (18%)
  between operations  1.39 us (2%)
    pallas_call x11, Pallas kernels, run(): pl.pallas_call(kernel, out_shape=tuple(outs), in_specs=[pl.BlockSpec(memo...  23.1 us
    all_to_all x3, waiting for transfers between devices, exchange(): return lax.all_to_all(rows, AXES, split_axis=0, concat_axis=0, tiled=True)  16.9 us
    all_to_all x1, blocking collectives, exchange(): return lax.all_to_all(rows, AXES, split_axis=0, concat_axis=0, tiled=True)  14.3 us
    all_to_all x3, starting transfers between devices, exchange(): return lax.all_to_all(rows, AXES, split_axis=0, concat_axis=0, tiled=True)  12.5 us
  transfers between devices with their start and end apart: 5, of which 5 were waited for; matrix products, arithmetic and copies ran while one was open for 0% of the time, Pallas kernels for 21%

profile of v4, /device:TPU:0, one launch (start us, length us, event | category | flops | bytes accessed | tf_op | source)
XLA Modules:
  0.0 68.9 jit_solution(15052149207398550705)
XLA Ops:
  1.3 2.4 %pick_rows.1 = (bf16[32,4,512]{2,1,0:T(4,128)(2,1)}, bf16[128,1024]{1,0:T(8,128)(2,1)S(1)}, s32[128,16]{1,0:T(8,128)S(1)}, s32[16,128]{1,0:T(8,128)S(1)}) custom-call(s32[1]{0:T(128)S(6)} %copy.17.edge_count, bf16[1024,256]{1,0:T(8,128)(2,1)} %features_at.5, bf16[1024,256]{1,0:T(8,128)(2,1)} %cotangent_at.5, s32[8,128]{1,0:T(8,128)} %bitcast.13, ...), custom_call_target="tpu_custom_call" | custom-call | flops 134217728 | tf_op jit(solution)/shard_map/pick_rows/pallas_call | solution.py:40
  3.7 7.3 %all-to-all-start = ((bf16[32,4,512]{2,1,0:T(4,128)(2,1)}), bf16[32,4,512]{2,1,0:T(4,128)(2,1)S(1)}, u32[]{:S(2)}, u32[]{:S(2)}) async-start(bf16[32,4,512]{2,1,0:T(4,128)(2,1)} %get-tuple-element.41), calls=%async_computation | async-start | bytes 262144 | tf_op jit(solution)/shard_map/all_to_all | solution.py:34
  11.0 4.6 %count_edges.1 = (bf16[1152,1152]{1,0:T(8,128)(2,1)}, bf16[1024,256]{1,0:T(8,128)(2,1)}, bf16[128,128]{1,0:T(8,128)(2,1)S(1)}, f32[128,512]{1,0:T(8,128)S(1)}) custom-call(bf16[1024,256]{1,0:T(8,128)(2,1)} %features_at.5, bf16[1024,256]{1,0:T(8,128)(2,1)} %cotangent_at.5, s32[8,128]{1,0:T(8,128)} %bitcast.14, ...), custom_call_target="tpu_custom_call" | custom-call | flops 5435817984 | tf_op jit(solution)/shard_map/count_edges/pallas_call | solution.py:40
  15.6 3.7 %all-to-all-done = bf16[32,4,512]{2,1,0:T(4,128)(2,1)S(1)} async-done(((bf16[32,4,512]{2,1,0:T(4,128)(2,1)}), bf16[32,4,512]{2,1,0:T(4,128)(2,1)S(1)}, u32[]{:S(2)}, u32[]{:S(2)}) %all-to-all-start) | async-done | bytes 131104 | tf_op jit(solution)/shard_map/all_to_all | solution.py:34
  19.3 0.9 %mirror_sums.1 = bf16[32,4,512]{2,1,0:T(4,128)(2,1)} custom-call(f32[128,512]{1,0:T(8,128)S(1)} %get-tuple-element.45.partial_in, bf16[128,128]{1,0:T(8,128)(2,1)S(1)} %get-tuple-element.46.mirror_counts, bf16[128,512]{1,0:T(8,128)(2,1)S(1)} %reshape.41.mirrored), custom_call_target="tpu_custom_call" | custom-call | flops 16777216 | tf_op jit(solution)/shard_map/mirror_sums/pallas_call | solution.py:40
  20.1 2.6 %all-to-all-start.1 = ((bf16[32,4,512]{2,1,0:T(4,128)(2,1)}), bf16[32,4,512]{2,1,0:T(4,128)(2,1)S(1)}, u32[]{:S(2)}, u32[]{:S(2)}) async-start(bf16[32,4,512]{2,1,0:T(4,128)(2,1)} %mirror_sums.1), calls=%async_computation.1 | async-start | bytes 262144 | tf_op jit(solution)/shard_map/all_to_all | solution.py:34
  22.7 4.9 %local_sums.1 = (f32[1024,256]{1,0:T(8,128)S(1)}, bf16[1024,256]{1,0:T(8,128)(2,1)S(1)}, bf16[256,256]{1,0:T(8,128)(2,1)S(1)}, bf16[256,256]{1,0:T(8,128)(2,1)S(...) custom-call(bf16[1152,1152]{1,0:T(8,128)(2,1)} %get-tuple-element.39.counts_at, ...), custom_call_target="tpu_custom_call" | custom-call | flops 1207959552 | tf_op jit(solution)/shard_map/local_sums/pallas_call | solution.py:40
  27.7 3.3 %all-to-all-done.1 = bf16[32,4,512]{2,1,0:T(4,128)(2,1)S(1)} async-done(((bf16[32,4,512]{2,1,0:T(4,128)(2,1)}), bf16[32,4,512]{2,1,0:T(4,128)(2,1)S(1)}, u32[]{:S(2)}, u32[]{:S(2)}) %all-to-all-start.1) | async-done | bytes 131104 | tf_op jit(solution)/shard_map/all_to_all | solution.py:34
  31.0 3.3 %middle.1 = (bf16[1024,256]{1,0:T(8,128)(2,1)S(1)}, bf16[512,256]{1,0:T(8,128)(2,1)S(1)}, f32[4,128]{1,0:T(4,128)S(1)}, bf16[1024,256]{1,0:T(8,128)(2,1)S(1)}, b...) custom-call(s32[1]{0:T(128)} %bitcast.core, ...), custom_call_target="tpu_custom_call" | custom-call | flops 1342177280 | tf_op jit(solution)/shard_map/middle/pallas_call | solution.py:40
  34.3 0.3 collective-permute-start
  34.6 1.0 %messages.1 = (bf16[1024,256]{1,0:T(8,128)(2,1)S(1)}, f32[128,256]{1,0:T(8,128)S(1)}, f32[512,256]{1,0:T(8,128)S(1)}) custom-call(s32[1]{0:T(128)} %bitcast.core, s32[8,128]{1,0:T(8,128)S(1)} %get-tuple-element.42.in_count, bf16[1024,256]{1,0:T(8,128)(2,1)S(1)} %get-tuple-element.52.grad_z, bf16[256,256]{1,0:T(8,128)(2,1)S(1)} %get-tuple-element.49.w_nbr_one, ...), custom_call_target="tpu_custom_call" | custom-call | flops 402653184 | tf_op jit(solution)/shard_map/messages/pallas_call | solution.py:40
  35.6 0.3 collective-permute-done.other_half
  35.9 0.9 %join_first.1 = bf16[32,4,1408]{2,1,0:T(4,128)(2,1)} custom-call(f32[512,256]{1,0:T(8,128)S(1)} %get-tuple-element.57.own_half, bf16[512,256]{1,0:T(8,128)(2,1)S(1)} %collective-permute-done.other_half, f32[128,256]{1,0:T(8,128)S(1)} %get-tuple-element.59.picked, f32[4,128]{1,0:T(4,128)S(1)} %get-tuple-element.60.bias_rows), custom_call_target="tpu_custom_call" | custom-call | tf_op jit(solution)/shard_map/join_first/pallas_call | solution.py:40
  36.7 2.6 %all-to-all-start.2 = ((bf16[32,4,1408]{2,1,0:T(4,128)(2,1)}), bf16[32,4,1408]{2,1,0:T(4,128)(2,1)S(1)}, u32[]{:S(2)}, u32[]{:S(2)}) async-start(bf16[32,4,1408]{2,1,0:T(4,128)(2,1)} %join_first.1), calls=%async_computation.2 | async-start | bytes 720896 | tf_op jit(solution)/shard_map/all_to_all | solution.py:34
  39.4 2.6 %local_back.1 = (f32[128,256]{1,0:T(8,128)S(1)}, f32[1024,256]{1,0:T(8,128)S(1)}, bf16[128,1152]{1,0:T(8,128)(2,1)S(1)}) custom-call(bf16[1152,1152]{1,0:T(8,128)(2,1)} %get-tuple-element.39.counts_at, bf16[1024,256]{1,0:T(8,128)(2,1)S(1)} %get-tuple-element.61.message_one, bf16[1024,256]{1,0:T(8,128)(2,1)S(1)} %get-tuple-element.52.grad_z, ...), custom_call_target="tpu_custom_call" | custom-call | flops 738197504 | tf_op jit(solution)/shard_map/local_back/pallas_call | solution.py:40
  42.0 9.9 %all-to-all-done.2.received = bf16[32,4,1408]{2,1,0:T(4,128)(2,1)S(1)} async-done(((bf16[32,4,1408]{2,1,0:T(4,128)(2,1)}), bf16[32,4,1408]{2,1,0:T(4,128)(2,1)S(1)}, u32[]{:S(2)}, u32[]{:S(2)}) %all-to-all-start.2) | async-done | bytes 360480 | tf_op jit(solution)/shard_map/all_to_all | solution.py:34
  51.9 0.3 join_second.1
  52.2 14.3 %all_to_all.20.received = bf16[32,4,1280]{2,1,0:T(4,128)(2,1)S(1)} all-to-all(bf16[32,4,1280]{2,1,0:T(4,128)(2,1)S(1)} %get-tuple-element.63), channel_id=1, replica_groups=mesh['dom'=8,'sub'=4] {'dom','sub'}, dimensions={0} | all-to-all | bytes 655360 | tf_op jit(solution)/shard_map/all_to_all | solution.py:34
  66.5 0.0 collective-permute-start.1
  66.5 1.5 %finish.1 = (bf16[1024,256]{1,0:T(8,128)(2,1)}, f32[1024,256]{1,0:T(8,128)}, f32[1,256]{1,0:T(1,128)}) custom-call(s32[1]{0:T(128)} %bitcast.core, bf16[32,4,1280]{2,1,0:T(4,128)(2,1)S(1)} %all_to_all.20.received, bf16[128,256]{1,0:T(8,128)(2,1)S(1)} %get-tuple-element.64.mirrored, bf16[128,1024]{1,0:T(8,128)(2,1)S(1)} %get-tuple-element.47.picking, ...), custom_call_target="tpu_custom_call" | custom-call | flops 201326592 | tf_op jit(solution)/shard_map/finish/pallas_call | solution.py:40
  67.9 0.2 collective-permute-done.1.received
  68.1 0.8 %finish_other.1 = f32[1024,256]{1,0:T(8,128)} custom-call(s32[1]{0:T(128)} %bitcast.core, f32[1024,256]{1,0:T(8,128)} %get-tuple-element.69.weights_in, bf16[32,4,1280]{2,1,0:T(4,128)(2,1)S(1)} %collective-permute-done.1.received), custom_call_target="tpu_custom_call", output_to_operand_aliasing={{}: (1, {})} | custom-call | tf_op jit(solution)/shard_map/finish_other/pallas_call | solution.py:40
  (2 shorter events, 0.1 us)
Async XLA Ops:
  3.7 15.5 %all-to-all-start = ((bf16[32,4,512]{2,1,0:T(4,128)(2,1)}), bf16[32,4,512]{2,1,0:T(4,128)(2,1)S(1)}, u32[]{:S(2)}, u32[]{:S(2)}) async-start(bf16[32,4,512]{2,1,0:T(4,128)(2,1)} %get-tuple-element.41), calls=%async_computation | async-start | bytes 262144 | tf_op jit(solution)/shard_map/all_to_all | solution.py:34
  20.1 10.8 %all-to-all-start.1 = ((bf16[32,4,512]{2,1,0:T(4,128)(2,1)}), bf16[32,4,512]{2,1,0:T(4,128)(2,1)S(1)}, u32[]{:S(2)}, u32[]{:S(2)}) async-start(bf16[32,4,512]{2,1,0:T(4,128)(2,1)} %mirror_sums.1), calls=%async_computation.1 | async-start | bytes 262144 | tf_op jit(solution)/shard_map/all_to_all | solution.py:34
  34.3 1.6 %collective-permute-start = (bf16[512,256]{1,0:T(8,128)(2,1)S(1)}, bf16[512,256]{1,0:T(8,128)(2,1)S(1)}, u32[]{:S(2)}, u32[]{:S(2)}) collective-permute-start(bf16[512,256]{1,0:T(8,128)(2,1)S(1)} %get-tuple-element.58), channel_id=1, source_target_pairs={{0,1},{1,0},{2,3},{3,2},{4,5},{5,4},{6,7},{7,6},{8,9},{9,8},{10,11... | collective-permute-start | bytes 786440 | tf_op jit(solution)/shard_map/ppermute | solution.py:704
  36.7 15.2 %all-to-all-start.2 = ((bf16[32,4,1408]{2,1,0:T(4,128)(2,1)}), bf16[32,4,1408]{2,1,0:T(4,128)(2,1)S(1)}, u32[]{:S(2)}, u32[]{:S(2)}) async-start(bf16[32,4,1408]{2,1,0:T(4,128)(2,1)} %join_first.1), calls=%async_computation.2 | async-start | bytes 720896 | tf_op jit(solution)/shard_map/all_to_all | solution.py:34
  66.5 1.6 %collective-permute-start.1 = (bf16[32,4,1280]{2,1,0:T(4,128)(2,1)S(1)}, bf16[32,4,1280]{2,1,0:T(4,128)(2,1)S(1)}, u32[]{:S(2)}, u32[]{:S(2)}) collective-permute-start(bf16[32,4,1280]{2,1,0:T(4,128)(2,1)S(1)} %all_to_all.20.received), channel_id=1, source_target_pairs={{0,1},{1,0},{2,3},{3,2},{4,5},{5,4},{6,7},{7,6},{8,9},{9,8},{10,11... | collective-permute-start | bytes 983048 | tf_op jit(solution)/shard_map/ppermute | solution.py:759

commit v5 on v4

--- a/solution.py
+++ b/solution.py
@@ -15,6 +15,7 @@
 I16 = jnp.int16
 LANES = 128
 BLOCK = 256
+ROWS = 512
 VMEM_LIMIT = 24 * 2**20
 
 
@@ -110,6 +111,7 @@
     sources_at,
     targets_at,
     payload,
+    scaled,
     picking,
     source_columns,
     targets,
@@ -155,6 +157,12 @@
     rows_out[:, :, :width] = by_peer(dot(picks, features[...]), devices)
     out_copy = pltpu.make_async_copy(rows_out, payload, out_semaphore)
     out_copy.start()
+    columns = inverse_rows.T
+    for block in range(node_dev // LANES):
+        rows = pl.ds(block * LANES, LANES)
+        scaled[rows, :] = (
+            cotangent[rows, :].astype(F32) * columns[:, block : block + 1]
+        ).astype(BF16)
     copies[4].wait()
     edge_ids = iota(sources.shape, 0) * LANES + iota(sources.shape, 1)
     source_columns[...] = jnp.where(edge_ids < edge_count[0], sources[...], -1).T
@@ -164,8 +172,7 @@
 
 def count_edges(
     features_at,
-    cotangent_at,
-    in_count_at,
+    scaled,
     source_columns,
     targets,
     counts_out,
@@ -173,10 +180,7 @@
     mirror_out,
     partial_out,
     features,
-    cotangent,
-    in_count,
-    semaphores,
-    scaled,
+    semaphore,
     from_hot,
     into_hot,
     counts,
@@ -184,9 +188,14 @@
 ):
     node_dev, width = features.shape
     slots, edges = into_hot.shape
-    loads = start_all(
-        [features_at, cotangent_at, in_count_at], [features, cotangent, in_count], semaphores
-    )
+    feature_copy = pltpu.make_async_copy(features_at, features, semaphore)
+    feature_copy.start()
+    sends = [
+        pltpu.make_async_copy(
+            scaled, scaled_out, out_semaphores.at[out_semaphores.shape[0] - 1]
+        )
+    ]
+    sends[0].start()
     lane_ids = iota((LANES, slots), 1, I16)
     for block in range(edges // LANES):
         column = jnp.broadcast_to(source_columns[:, block : block + 1], (LANES, LANES)).astype(I16)
@@ -194,7 +203,6 @@
         from_hot[pl.ds(block * LANES, LANES), :] = edge_hot(lane_ids == column)
     row_ids = iota((LANES, LANES), 0, I16)
     target_rows = targets[...].astype(I16)
-    sends = []
     for start in range(0, slots, BLOCK):
         size = min(BLOCK, slots - start)
         for block in range(edges // LANES):
@@ -210,17 +218,7 @@
         )
         copy.start()
         sends.append(copy)
-    for copy in loads:
-        copy.wait()
-    columns = inverse_columns(in_count)
-    for index, start in enumerate(range(0, node_dev, BLOCK)):
-        rows = pl.ds(start, BLOCK)
-        scaled[rows, :] = (
-            cotangent[rows, :].astype(F32) * block_inverse(columns, index)
-        ).astype(BF16)
-    copy = pltpu.make_async_copy(scaled, scaled_out, out_semaphores.at[len(sends)])
-    copy.start()
-    sends.append(copy)
+    feature_copy.wait()
     mirror_out[...] = counts[node_dev:, node_dev:]
     partial_out[:, :width] = dot(counts[node_dev:, :node_dev], features[...])
     partial_out[:, width:] = tdot(counts[:node_dev, node_dev:], scaled[...])
@@ -242,18 +240,10 @@
 def local_sums(
     counts_at,
     features_at,
-    w_nbr_one_at,
-    w_self_one_at,
-    bias_one_at,
-    in_count_at,
     scaled_at,
     mirrored,
     forward,
     features,
-    w_nbr_one,
-    w_self_one,
-    bias_one,
-    in_count,
     backward_at,
     counts,
     scaled,
@@ -265,7 +255,7 @@
     node_dev, width = features.shape
     slots = counts.shape[0]
     blocks = [(start, min(BLOCK, slots - start)) for start in range(0, slots, BLOCK)]
-    loads = start_all([features_at], [features], semaphores)
+    loads = start_all([scaled_at], [scaled], semaphores)
     copies = []
     for index, (start, size) in enumerate(blocks):
         rows = pl.ds(start, size)
@@ -274,27 +264,10 @@
         )
         copy.start()
         copies.append(copy)
-    for index, (source, buffer) in enumerate(
-        (
-            (scaled_at, scaled),
-            (w_nbr_one_at, w_nbr_one),
-            (w_self_one_at, w_self_one),
-            (bias_one_at, bias_one),
-            (in_count_at, in_count),
-        )
-    ):
-        copy = pltpu.make_async_copy(source, buffer, semaphores.at[index + 1])
-        copy.start()
-        loads.append(copy)
-    loads[0].wait()
-    for (start, size), copy in zip(blocks, copies):
+    loads.append(pltpu.make_async_copy(features_at, features, semaphores.at[1]))
+    loads[1].start()
+    for copy in [loads[0]] + copies:
         copy.wait()
-        if start < node_dev:
-            rows = pl.ds(start, size)
-            forward[rows, :] = dot(counts[rows, :node_dev], features[...]) + dot(
-                counts[rows, node_dev:], mirrored[:, :width]
-            )
-    loads[1].wait()
     sends = []
     for index, start in enumerate(range(0, node_dev, BLOCK)):
         rows = pl.ds(start, BLOCK)
@@ -306,21 +279,26 @@
         )
         copy.start()
         sends.append(copy)
-    for copy in loads[2:] + sends:
+    for copy in loads[1:]:
         copy.wait()
-
-
-def block_inverse(columns, index):
-    first = index * BLOCK // LANES
+    for start in range(0, node_dev, BLOCK):
+        rows = pl.ds(start, BLOCK)
+        forward[rows, :] = dot(counts[rows, :node_dev], features[...]) + dot(
+            counts[rows, node_dev:], mirrored[:, :width]
+        )
+    for copy in sends:
+        copy.wait()
+
+
+def block_inverse(columns, index, size=BLOCK):
+    first = index * size // LANES
     return jnp.concatenate(
-        [columns[:, b : b + 1] for b in range(first, first + BLOCK // LANES)], axis=0
+        [columns[:, b : b + 1] for b in range(first, first + size // LANES)], axis=0
     )
 
 
 def middle(
     core,
-    w_nbr_two_at,
-    w_self_two_at,
     cotangent_at,
     backward_at,
     forward,
@@ -330,6 +308,8 @@
     w_nbr_one,
     w_self_one,
     bias_one,
+    w_nbr_two,
+    w_self_two,
     in_count,
     grad_z,
     sent_half,
@@ -338,23 +318,21 @@
     h_one,
     pulled,
     cotangent,
-    w_nbr_two,
-    w_self_two,
     backward,
     semaphores,
     slope,
 ):
     node_dev, width = features.shape
+    blocks = [pl.ds(start, ROWS) for start in range(0, node_dev, ROWS)]
     copies = start_all(
-        [backward_at, w_nbr_two_at, w_self_two_at, cotangent_at],
-        [backward, w_nbr_two, w_self_two, cotangent],
+        [backward_at, cotangent_at],
+        [backward, cotangent],
         semaphores,
     )
-    blocks = [pl.ds(start, BLOCK) for start in range(0, node_dev, BLOCK)]
     columns = inverse_columns(in_count)
     for index, rows in enumerate(blocks):
         placed = tdot(picking[:, rows], returned[:, :width])
-        mean = ((forward[rows, :] + placed) * block_inverse(columns, index)).astype(BF16)
+        mean = ((forward[rows, :] + placed) * block_inverse(columns, index, ROWS)).astype(BF16)
         mean_one[rows, :] = mean
         z_one = (
             dot(features[rows, :], w_self_one[...]) + dot(mean, w_nbr_one[...]) + bias_one[...]
@@ -598,11 +576,12 @@
     blocks = -(-slots // BLOCK)
 
     payload_shape = (devices, per_peer, 2 * width)
-    payload, picking, source_columns, targets = run(
+    payload, scaled, picking, source_columns, targets = run(
         pick_rows,
         "pick_rows",
         [
             pltpu.HBM(payload_shape, BF16),
+            pltpu.VMEM((node_dev, width), BF16),
             pltpu.VMEM((mirrors, node_dev), BF16),
             pltpu.VMEM((LANES, edges // LANES), I32),
             pltpu.VMEM(targets.shape, I32),
@@ -626,11 +605,11 @@
             pltpu.VMEM((mirrors, mirrors), BF16),
             pltpu.VMEM((mirrors, 2 * width), F32),
         ],
-        hbm=[features, cotangent, in_count],
-        vmem=[source_columns, targets],
-        scratch=staged_for(3, features, cotangent, in_count)
-        + [
+        hbm=[features],
+        vmem=[scaled, source_columns, targets],
+        scratch=[
             rows_bf16,
+            pltpu.SemaphoreType.DMA,
             pltpu.VMEM((edges, slots), F8),
             pltpu.VMEM((slots, edges), F8),
             pltpu.VMEM((slots, slots), BF16),
@@ -647,20 +626,11 @@
         flops=4 * mirrors * mirrors * width,
     )
     returned = exchange(payload).reshape(mirrors, 2 * width)
-    weight = pltpu.VMEM((width, width), BF16)
-    forward, features_in, w_nbr_in, w_self_in, bias_in, in_count_in, backward = run(
+    forward, features_in, backward = run(
         local_sums,
         "local_sums",
-        [
-            rows_f32,
-            rows_bf16,
-            weight,
-            weight,
-            pltpu.VMEM((1, width), F32),
-            pltpu.VMEM(in_count.shape, I32),
-            pltpu.HBM((node_dev, width), F32),
-        ],
-        hbm=[counts, features, w_nbr_one, w_self_one, bias_one.reshape(1, -1), in_count, scaled],
+        [rows_f32, rows_bf16, pltpu.HBM((node_dev, width), F32)],
+        hbm=[counts, features, scaled],
         vmem=[mirrored],
         scratch=[
             pltpu.VMEM((slots, slots), BF16),
@@ -668,7 +638,7 @@
             rows_f32,
             pltpu.SemaphoreType.DMA((blocks,)),
             pltpu.SemaphoreType.DMA((node_dev // BLOCK,)),
-            pltpu.SemaphoreType.DMA((6,)),
+            pltpu.SemaphoreType.DMA((2,)),
         ],
         flops=4 * node_dev * slots * width,
     )
@@ -687,18 +657,24 @@
             rows_bf16,
         ],
         smem=[core.reshape(1)],
-        hbm=[w_nbr_two, w_self_two, cotangent, backward],
+        hbm=[cotangent, backward],
         vmem=[
             forward,
             returned,
             picking,
             features_in,
-            w_nbr_in,
-            w_self_in,
-            bias_in,
-            in_count_in,
-        ],
-        scratch=[weight, weight, rows_f32, pltpu.SemaphoreType.DMA((4,)), rows_f32],
+            w_nbr_one,
+            w_self_one,
+            bias_one.reshape(1, -1),
+            w_nbr_two,
+            w_self_two,
+            in_count,
+        ],
+        scratch=[
+            rows_f32,
+            pltpu.SemaphoreType.DMA((2,)),
+            rows_f32,
+        ],
         flops=20 * node_dev * width * width,
     )
     other_half = lax.ppermute(sent_half, AXES, swap)
@@ -708,9 +684,9 @@
         [rows_bf16, pltpu.VMEM((mirrors, width), F32), pltpu.VMEM((half, width), F32)],
         smem=[core.reshape(1)],
         vmem=[
-            in_count_in,
+            in_count,
             grad_z_one,
-            w_nbr_in,
+            w_nbr_one,
             picking,
             features_in,
             mean_one,
@@ -740,7 +716,7 @@
             pltpu.VMEM((mirrors, slots), BF16),
         ],
         hbm=[counts],
-        vmem=[message_one, grad_z_one, w_self_in],
+        vmem=[message_one, grad_z_one, w_self_one],
         scratch=[pltpu.VMEM((node_dev, slots), BF16), pltpu.SemaphoreType.DMA((2,))],
         flops=2 * node_dev * (slots + width) * width,
     )

time: 69.3 us -> 69 us (level)
  Pallas kernels: 23.1 us -> 20.8 us
  waiting for transfers between devices: 17.3 us -> 19 us
    pallas_call x11, Pallas kernels: 23.1 us -> 20.8 us  [run(): pl.pallas_call(kernel, out_shape=tuple(outs), in_specs=[pl.BlockSpec(memo...]
    all_to_all x3, waiting for transfers between devices: 16.9 us -> 18.6 us  [exchange(): return lax.all_to_all(rows, AXES, split_axis=0, concat_axis=0, tiled=True)]
  transfers between devices with their start and end apart: 5 -> 5, of which waited for: 5 -> 5; matrix products, arithmetic and copies ran while one was open for 0% -> 0% of each run, Pallas kernels for 21% -> 19%
where the time goes in v5:
time: 69 us; the launch traced here: 68.6 us
  Pallas kernels  20.8 us (30%)
  waiting for transfers between devices  19 us (28%)
  blocking collectives  14.2 us (21%)
  starting transfers between devices  12.9 us (19%)
  between operations  1.49 us (2%)
    pallas_call x11, Pallas kernels, run(): pl.pallas_call(kernel, out_shape=tuple(outs), in_specs=[pl.BlockSpec(memo...  20.8 us
    all_to_all x3, waiting for transfers between devices, exchange(): return lax.all_to_all(rows, AXES, split_axis=0, concat_axis=0, tiled=True)  18.6 us
    all_to_all x1, blocking collectives, exchange(): return lax.all_to_all(rows, AXES, split_axis=0, concat_axis=0, tiled=True)  14.2 us
    all_to_all x3, starting transfers between devices, exchange(): return lax.all_to_all(rows, AXES, split_axis=0, concat_axis=0, tiled=True)  12.6 us
  transfers between devices with their start and end apart: 5, of which 5 were waited for; matrix products, arithmetic and copies ran while one was open for 0% of the time, Pallas kernels for 19%

profile of v5, /device:TPU:0, one launch (start us, length us, event | category | flops | bytes accessed | tf_op | source)
XLA Modules:
  0.0 68.6 jit_solution(2683215499856856014)
XLA Ops:
  1.3 2.4 %pick_rows.1 = (bf16[32,4,512]{2,1,0:T(4,128)(2,1)}, bf16[1024,256]{1,0:T(8,128)(2,1)S(1)}, bf16[128,1024]{1,0:T(8,128)(2,1)S(1)}, s32[128,16]{1,0:T(8,128)S(1)}, s32[16,128]{1,0:T(8,128)S(1)}) custom-call(s32[1]{0:T(128)S(6)} %copy.17.edge_count, bf16[1024,256]{1,0:T(8,128)(2,1)} %features_at.5, bf16[1024,256]{1,0:T(8,128)(2,1)} %cotangent_at.3, ...), custom_call_target="tpu_custom_call" | custom-call | flops 134217728 | tf_op jit(solution)/shard_map/pick_rows/pallas_call | solution.py:41
  3.7 7.3 %all-to-all-start = ((bf16[32,4,512]{2,1,0:T(4,128)(2,1)}), bf16[32,4,512]{2,1,0:T(4,128)(2,1)S(1)}, u32[]{:S(2)}, u32[]{:S(2)}) async-start(bf16[32,4,512]{2,1,0:T(4,128)(2,1)} %get-tuple-element.39), calls=%async_computation | async-start | bytes 262144 | tf_op jit(solution)/shard_map/all_to_all | solution.py:35
  11.0 4.1 %count_edges.1 = (bf16[1152,1152]{1,0:T(8,128)(2,1)}, bf16[1024,256]{1,0:T(8,128)(2,1)}, bf16[128,128]{1,0:T(8,128)(2,1)S(1)}, f32[128,512]{1,0:T(8,128)S(1)}) custom-call(bf16[1024,256]{1,0:T(8,128)(2,1)} %features_at.5, bf16[1024,256]{1,0:T(8,128)(2,1)S(1)} %get-tuple-element.34.scaled, s32[128,16]{1,0:T(8,128)S(1)} %get-tuple-element.35.source_columns, ...), custom_call_target="tpu_custom_call" | custom-call | flops 5435817984 | tf_op jit(solution)/shard_map/count_edges/pallas_call | solution.py:41
  15.1 4.2 %all-to-all-done = bf16[32,4,512]{2,1,0:T(4,128)(2,1)S(1)} async-done(((bf16[32,4,512]{2,1,0:T(4,128)(2,1)}), bf16[32,4,512]{2,1,0:T(4,128)(2,1)S(1)}, u32[]{:S(2)}, u32[]{:S(2)}) %all-to-all-start) | async-done | bytes 131104 | tf_op jit(solution)/shard_map/all_to_all | solution.py:35
  19.3 0.9 %mirror_sums.1 = bf16[32,4,512]{2,1,0:T(4,128)(2,1)} custom-call(f32[128,512]{1,0:T(8,128)S(1)} %get-tuple-element.42.partial_in, bf16[128,128]{1,0:T(8,128)(2,1)S(1)} %get-tuple-element.43.mirror_counts, bf16[128,512]{1,0:T(8,128)(2,1)S(1)} %reshape.40.mirrored), custom_call_target="tpu_custom_call" | custom-call | flops 16777216 | tf_op jit(solution)/shard_map/mirror_sums/pallas_call | solution.py:41
  20.2 0.0 copy-start
  20.2 0.0 copy-start.1
  20.2 0.0 copy-start.3
  20.2 2.7 %all-to-all-start.1 = ((bf16[32,4,512]{2,1,0:T(4,128)(2,1)}), bf16[32,4,512]{2,1,0:T(4,128)(2,1)S(1)}, u32[]{:S(2)}, u32[]{:S(2)}) async-start(bf16[32,4,512]{2,1,0:T(4,128)(2,1)} %mirror_sums.1), calls=%async_computation.1 | async-start | bytes 262144 | tf_op jit(solution)/shard_map/all_to_all | solution.py:35
  23.0 3.7 %local_sums.1 = (f32[1024,256]{1,0:T(8,128)S(1)}, bf16[1024,256]{1,0:T(8,128)(2,1)S(1)}, f32[1024,256]{1,0:T(8,128)}) custom-call(bf16[1152,1152]{1,0:T(8,128)(2,1)} %get-tuple-element.37.counts_at, bf16[1024,256]{1,0:T(8,128)(2,1)} %features_at.5, bf16[1024,256]{1,0:T(8,128)(2,1)} %get-tuple-element.38.scaled_at, bf16[128,512]{1,0:T(8,128)(2,1)S(1)} %reshape.40.mirrored), custom_call_target="tpu_custom_call" | custom-call | flops 1207959552 | tf_op jit(solution)/shard_map/local_sums/pallas_call | solution.py:41
  26.7 4.5 %all-to-all-done.1 = bf16[32,4,512]{2,1,0:T(4,128)(2,1)S(1)} async-done(((bf16[32,4,512]{2,1,0:T(4,128)(2,1)}), bf16[32,4,512]{2,1,0:T(4,128)(2,1)S(1)}, u32[]{:S(2)}, u32[]{:S(2)}) %all-to-all-start.1) | async-done | bytes 131104 | tf_op jit(solution)/shard_map/all_to_all | solution.py:35
  31.3 2.7 %middle.1 = (bf16[1024,256]{1,0:T(8,128)(2,1)S(1)}, bf16[512,256]{1,0:T(8,128)(2,1)S(1)}, f32[4,128]{1,0:T(4,128)S(1)}, bf16[1024,256]{1,0:T(8,128)(2,1)S(1)}, b...) custom-call(s32[1]{0:T(128)} %bitcast.core, ...), custom_call_target="tpu_custom_call" | custom-call | flops 1342177280 | tf_op jit(solution)/shard_map/middle/pallas_call | solution.py:41
  33.9 0.3 collective-permute-start
  34.2 1.0 %messages.1 = (bf16[1024,256]{1,0:T(8,128)(2,1)S(1)}, f32[128,256]{1,0:T(8,128)S(1)}, f32[512,256]{1,0:T(8,128)S(1)}) custom-call(s32[1]{0:T(128)} %bitcast.core, s32[8,128]{1,0:T(8,128)S(1)} %bitcast.12, bf16[1024,256]{1,0:T(8,128)(2,1)S(1)} %get-tuple-element.46.grad_z, bf16[256,256]{1,0:T(8,128)(2,1)S(1)} %copy-done, ...), custom_call_target="tpu_custom_call" | custom-call | flops 402653184 | tf_op jit(solution)/shard_map/messages/pallas_call | solution.py:41
  35.3 0.2 collective-permute-done.other_half
  35.5 0.9 %join_first.1 = bf16[32,4,1408]{2,1,0:T(4,128)(2,1)} custom-call(f32[512,256]{1,0:T(8,128)S(1)} %get-tuple-element.51.own_half, bf16[512,256]{1,0:T(8,128)(2,1)S(1)} %collective-permute-done.other_half, f32[128,256]{1,0:T(8,128)S(1)} %get-tuple-element.53.picked, f32[4,128]{1,0:T(4,128)S(1)} %get-tuple-element.54.bias_rows), custom_call_target="tpu_custom_call" | custom-call | tf_op jit(solution)/shard_map/join_first/pallas_call | solution.py:41
  36.4 2.6 %all-to-all-start.2 = ((bf16[32,4,1408]{2,1,0:T(4,128)(2,1)}), bf16[32,4,1408]{2,1,0:T(4,128)(2,1)S(1)}, u32[]{:S(2)}, u32[]{:S(2)}) async-start(bf16[32,4,1408]{2,1,0:T(4,128)(2,1)} %join_first.1), calls=%async_computation.2 | async-start | bytes 720896 | tf_op jit(solution)/shard_map/all_to_all | solution.py:35
  39.0 2.7 %local_back.1 = (f32[128,256]{1,0:T(8,128)S(1)}, f32[1024,256]{1,0:T(8,128)S(1)}, bf16[128,1152]{1,0:T(8,128)(2,1)S(1)}) custom-call(bf16[1152,1152]{1,0:T(8,128)(2,1)} %get-tuple-element.37.counts_at, bf16[1024,256]{1,0:T(8,128)(2,1)S(1)} %get-tuple-element.55.message_one, bf16[1024,256]{1,0:T(8,128)(2,1)S(1)} %get-tuple-element.46.grad_z, ...), custom_call_target="tpu_custom_call" | custom-call | flops 738197504 | tf_op jit(solution)/shard_map/local_back/pallas_call | solution.py:41
  41.7 9.9 %all-to-all-done.2.received = bf16[32,4,1408]{2,1,0:T(4,128)(2,1)S(1)} async-done(((bf16[32,4,1408]{2,1,0:T(4,128)(2,1)}), bf16[32,4,1408]{2,1,0:T(4,128)(2,1)S(1)}, u32[]{:S(2)}, u32[]{:S(2)}) %all-to-all-start.2) | async-done | bytes 360480 | tf_op jit(solution)/shard_map/all_to_all | solution.py:35
  51.6 0.3 join_second.1
  51.9 14.2 %all_to_all.20.received = bf16[32,4,1280]{2,1,0:T(4,128)(2,1)S(1)} all-to-all(bf16[32,4,1280]{2,1,0:T(4,128)(2,1)S(1)} %get-tuple-element.57), channel_id=1, replica_groups=mesh['dom'=8,'sub'=4] {'dom','sub'}, dimensions={0} | all-to-all | bytes 655360 | tf_op jit(solution)/shard_map/all_to_all | solution.py:35
  66.1 1.5 %finish.1 = (bf16[1024,256]{1,0:T(8,128)(2,1)}, f32[1024,256]{1,0:T(8,128)}, f32[1,256]{1,0:T(1,128)}) custom-call(s32[1]{0:T(128)} %bitcast.core, bf16[32,4,1280]{2,1,0:T(4,128)(2,1)S(1)} %all_to_all.20.received, bf16[128,256]{1,0:T(8,128)(2,1)S(1)} %get-tuple-element.58.mirrored, bf16[128,1024]{1,0:T(8,128)(2,1)S(1)} %get-tuple-element.44.picking, ...), custom_call_target="tpu_custom_call" | custom-call | flops 201326592 | tf_op jit(solution)/shard_map/finish/pallas_call | solution.py:41
  67.6 0.2 collective-permute-done.1.received
  67.7 0.8 %finish_other.1 = f32[1024,256]{1,0:T(8,128)} custom-call(s32[1]{0:T(128)} %bitcast.core, f32[1024,256]{1,0:T(8,128)} %get-tuple-element.63.weights_in, bf16[32,4,1280]{2,1,0:T(4,128)(2,1)S(1)} %collective-permute-done.1.received), custom_call_target="tpu_custom_call", output_to_operand_aliasing={{}: (1, {})} | custom-call | tf_op jit(solution)/shard_map/finish_other/pallas_call | solution.py:41
  (12 shorter events, 0.1 us)
Async XLA Ops:
  3.7 15.5 %all-to-all-start = ((bf16[32,4,512]{2,1,0:T(4,128)(2,1)}), bf16[32,4,512]{2,1,0:T(4,128)(2,1)S(1)}, u32[]{:S(2)}, u32[]{:S(2)}) async-start(bf16[32,4,512]{2,1,0:T(4,128)(2,1)} %get-tuple-element.39), calls=%async_computation | async-start | bytes 262144 | tf_op jit(solution)/shard_map/all_to_all | solution.py:35
  20.2 11.1 %copy-start = (bf16[256,256]{1,0:T(8,128)(2,1)S(1)}, bf16[256,256]{1,0:T(8,128)(2,1)}, u32[]{:S(2)}) copy-start(bf16[256,256]{1,0:T(8,128)(2,1)} %w_nbr_one.3) | copy-start | bytes 393220
  20.2 11.1 %copy-start.1 = (bf16[256,256]{1,0:T(8,128)(2,1)S(1)}, bf16[256,256]{1,0:T(8,128)(2,1)}, u32[]{:S(2)}) copy-start(bf16[256,256]{1,0:T(8,128)(2,1)} %w_self_one.3) | copy-start | bytes 393220
  20.2 11.1 %copy-start.2 = (s32[1024]{0:T(1024)S(1)}, s32[1024]{0:T(1024)}, u32[]{:S(2)}) copy-start(s32[1024]{0:T(1024)} %param.19) | copy-start | bytes 12292
  20.2 11.0 %copy-start.3 = (bf16[256,256]{1,0:T(8,128)(2,1)S(1)}, bf16[256,256]{1,0:T(8,128)(2,1)}, u32[]{:S(2)}) copy-start(bf16[256,256]{1,0:T(8,128)(2,1)} %w_nbr_two.1) | copy-start | bytes 393220
  20.2 11.0 %copy-start.4 = (bf16[256,256]{1,0:T(8,128)(2,1)S(1)}, bf16[256,256]{1,0:T(8,128)(2,1)}, u32[]{:S(2)}) copy-start(bf16[256,256]{1,0:T(8,128)(2,1)} %w_self_two.1) | copy-start | bytes 393220
  20.2 11.0 %copy-start.5 = (f32[256]{0:T(256)S(1)}, f32[256]{0:T(256)}, u32[]{:S(2)}) copy-start(f32[256]{0:T(256)} %param.16) | copy-start | bytes 3076
  20.2 10.9 %all-to-all-start.1 = ((bf16[32,4,512]{2,1,0:T(4,128)(2,1)}), bf16[32,4,512]{2,1,0:T(4,128)(2,1)S(1)}, u32[]{:S(2)}, u32[]{:S(2)}) async-start(bf16[32,4,512]{2,1,0:T(4,128)(2,1)} %mirror_sums.1), calls=%async_computation.1 | async-start | bytes 262144 | tf_op jit(solution)/shard_map/all_to_all | solution.py:35
  33.9 1.6 %collective-permute-start = (bf16[512,256]{1,0:T(8,128)(2,1)S(1)}, bf16[512,256]{1,0:T(8,128)(2,1)S(1)}, u32[]{:S(2)}, u32[]{:S(2)}) collective-permute-start(bf16[512,256]{1,0:T(8,128)(2,1)S(1)} %get-tuple-element.52), channel_id=1, source_target_pairs={{0,1},{1,0},{2,3},{3,2},{4,5},{5,4},{6,7},{7,6},{8,9},{9,8},{10,11... | collective-permute-start | bytes 786440 | tf_op jit(solution)/shard_map/ppermute | solution.py:680
  36.4 15.2 %all-to-all-start.2 = ((bf16[32,4,1408]{2,1,0:T(4,128)(2,1)}), bf16[32,4,1408]{2,1,0:T(4,128)(2,1)S(1)}, u32[]{:S(2)}, u32[]{:S(2)}) async-start(bf16[32,4,1408]{2,1,0:T(4,128)(2,1)} %join_first.1), calls=%async_computation.2 | async-start | bytes 720896 | tf_op jit(solution)/shard_map/all_to_all | solution.py:35
  66.1 1.6 %collective-permute-start.1 = (bf16[32,4,1280]{2,1,0:T(4,128)(2,1)S(1)}, bf16[32,4,1280]{2,1,0:T(4,128)(2,1)S(1)}, u32[]{:S(2)}, u32[]{:S(2)}) collective-permute-start(bf16[32,4,1280]{2,1,0:T(4,128)(2,1)S(1)} %all_to_all.20.received), channel_id=1, source_target_pairs={{0,1},{1,0},{2,3},{3,2},{4,5},{5,4},{6,7},{7,6},{8,9},{9,8},{10,11... | collective-permute-start | bytes 983048 | tf_op jit(solution)/shard_map/ppermute | solution.py:735

commit v6 on v5

--- a/solution.py
+++ b/solution.py
@@ -103,7 +103,6 @@
 
 
 def pick_rows(
-    edge_count,
     features_at,
     cotangent_at,
     in_count_at,
@@ -113,13 +112,12 @@
     payload,
     scaled,
     picking,
-    source_columns,
+    sources,
     targets,
     features,
     cotangent,
     in_count,
     sent,
-    sources,
     semaphores,
     rows_out,
     out_semaphore,
@@ -164,20 +162,19 @@
             cotangent[rows, :].astype(F32) * columns[:, block : block + 1]
         ).astype(BF16)
     copies[4].wait()
-    edge_ids = iota(sources.shape, 0) * LANES + iota(sources.shape, 1)
-    source_columns[...] = jnp.where(edge_ids < edge_count[0], sources[...], -1).T
     copies[5].wait()
     out_copy.wait()
 
 
 def count_edges(
+    edge_count,
     features_at,
     scaled,
-    source_columns,
+    sources,
     targets,
     counts_out,
-    scaled_out,
-    mirror_out,
+    scaled_at,
+    mirror_rows,
     partial_out,
     features,
     semaphore,
@@ -190,19 +187,17 @@
     slots, edges = into_hot.shape
     feature_copy = pltpu.make_async_copy(features_at, features, semaphore)
     feature_copy.start()
-    sends = [
-        pltpu.make_async_copy(
-            scaled, scaled_out, out_semaphores.at[out_semaphores.shape[0] - 1]
-        )
-    ]
+    sends = [pltpu.make_async_copy(scaled, scaled_at, out_semaphores.at[node_dev // BLOCK])]
     sends[0].start()
+    source_columns = sources[...].T
     lane_ids = iota((LANES, slots), 1, I16)
     for block in range(edges // LANES):
         column = jnp.broadcast_to(source_columns[:, block : block + 1], (LANES, LANES)).astype(I16)
         column = jnp.concatenate([column] * (slots // LANES), axis=1)
         from_hot[pl.ds(block * LANES, LANES), :] = edge_hot(lane_ids == column)
+    edge_ids = iota(targets.shape, 0) * LANES + iota(targets.shape, 1)
+    target_rows = jnp.where(edge_ids < edge_count[0], targets[...], -1).astype(I16)
     row_ids = iota((LANES, LANES), 0, I16)
-    target_rows = targets[...].astype(I16)
     for start in range(0, slots, BLOCK):
         size = min(BLOCK, slots - start)
         for block in range(edges // LANES):
@@ -212,26 +207,30 @@
                     row_ids + jnp.int16(part) == target_row
                 )
         rows = pl.ds(start, size)
-        counts[rows, :] = dot(into_hot[rows, :], from_hot[...]).astype(BF16)
-        copy = pltpu.make_async_copy(
-            counts.at[rows], counts_out.at[rows], out_semaphores.at[start // BLOCK]
-        )
-        copy.start()
-        sends.append(copy)
+        block_counts = dot(into_hot[rows, :], from_hot[...]).astype(BF16)
+        if start < node_dev:
+            counts[rows, :] = block_counts
+            copy = pltpu.make_async_copy(
+                counts.at[rows], counts_out.at[rows], out_semaphores.at[start // BLOCK]
+            )
+            copy.start()
+            sends.append(copy)
+        else:
+            mirror_rows[pl.ds(start - node_dev, size), :] = block_counts
     feature_copy.wait()
-    mirror_out[...] = counts[node_dev:, node_dev:]
-    partial_out[:, :width] = dot(counts[node_dev:, :node_dev], features[...])
-    partial_out[:, width:] = tdot(counts[:node_dev, node_dev:], scaled[...])
+    partial_out[:, :width] = dot(mirror_rows[:, :node_dev], features[...])
+    partial_out[:, width:] = tdot(counts[:, node_dev:], scaled[...])
     for copy in sends:
         copy.wait()
 
 
-def mirror_sums(partial_in, mirror_counts, mirrored, payload, rows_out, out_semaphore):
+def mirror_sums(partial_in, mirror_rows, mirrored, payload, rows_out, out_semaphore):
     devices, _, columns = rows_out.shape
     width = columns // 2
     received = mirrored[...]
-    front = partial_in[:, :width] + dot(mirror_counts[...], received[:, :width])
-    back = partial_in[:, width:] + tdot(mirror_counts[...], received[:, width:])
+    mirror_counts = mirror_rows[:, mirror_rows.shape[1] - mirror_rows.shape[0] :]
+    front = partial_in[:, :width] + dot(mirror_counts, received[:, :width])
+    back = partial_in[:, width:] + tdot(mirror_counts, received[:, width:])
     rows_out[:, :, :width] = by_peer(front, devices)
     rows_out[:, :, width:] = by_peer(back, devices)
     send(rows_out, payload, out_semaphore)
@@ -242,9 +241,11 @@
     features_at,
     scaled_at,
     mirrored,
+    mirror_rows,
     forward,
     features,
     backward_at,
+    mirror_at,
     counts,
     scaled,
     backward,
@@ -253,9 +254,10 @@
     semaphores,
 ):
     node_dev, width = features.shape
-    slots = counts.shape[0]
-    blocks = [(start, min(BLOCK, slots - start)) for start in range(0, slots, BLOCK)]
+    blocks = [(start, BLOCK) for start in range(0, node_dev, BLOCK)]
     loads = start_all([scaled_at], [scaled], semaphores)
+    mirror_copy = pltpu.make_async_copy(mirror_rows, mirror_at, semaphores.at[2])
+    mirror_copy.start()
     copies = []
     for index, (start, size) in enumerate(blocks):
         rows = pl.ds(start, size)
@@ -271,8 +273,8 @@
     sends = []
     for index, start in enumerate(range(0, node_dev, BLOCK)):
         rows = pl.ds(start, BLOCK)
-        backward[rows, :] = tdot(counts[:node_dev, rows], scaled[...]) + tdot(
-            counts[node_dev:, rows], mirrored[:, width:]
+        backward[rows, :] = tdot(counts[:, rows], scaled[...]) + tdot(
+            mirror_rows[:, rows], mirrored[:, width:]
         )
         copy = pltpu.make_async_copy(
             backward.at[rows], backward_at.at[rows], out_semaphores.at[index]
@@ -286,7 +288,7 @@
         forward[rows, :] = dot(counts[rows, :node_dev], features[...]) + dot(
             counts[rows, node_dev:], mirrored[:, :width]
         )
-    for copy in sends:
+    for copy in sends + [mirror_copy]:
         copy.wait()
 
 
@@ -424,6 +426,7 @@
 
 def local_back(
     counts_at,
+    mirror_at,
     message_one,
     grad_z,
     w_self_one,
@@ -434,30 +437,23 @@
     semaphores,
 ):
     node_dev, width = grad_z.shape
-    copies = [
-        pltpu.make_async_copy(counts_at.at[pl.ds(0, node_dev)], counts, semaphores.at[0]),
-        pltpu.make_async_copy(
-            counts_at.at[pl.ds(node_dev, mirror_rows.shape[0])], mirror_rows, semaphores.at[1]
-        ),
-    ]
-    for copy in copies:
-        copy.start()
+    copies = start_all([counts_at, mirror_at], [counts, mirror_rows], semaphores)
     for start in range(0, node_dev, BLOCK):
         rows = pl.ds(start, BLOCK)
         local_out[rows, :] = dot_transposed(grad_z[rows, :], w_self_one[...])
-    copies[0].wait()
+    for copy in copies:
+        copy.wait()
     mirror_out[...] = tdot(counts[:, node_dev:], message_one[...])
     for start in range(0, node_dev, BLOCK):
         rows = pl.ds(start, BLOCK)
         local_out[rows, :] += tdot(counts[:, rows], message_one[...])
-    copies[1].wait()
 
 
 def join_second(
     norm_factor,
     received,
     mirror_partial,
-    mirror_counts,
+    mirror_rows,
     payload,
     mirrored_out,
     bias_total,
@@ -467,7 +463,9 @@
     groups = payload.shape[2] // width - 1
     mirrored = by_row(received[:, :, :width]).astype(BF16)
     mirrored_out[...] = mirrored
-    partial_sums = mirror_partial[...] + tdot(mirror_counts[...], mirrored)
+    partial_sums = mirror_partial[...] + tdot(
+        mirror_rows[:, mirror_rows.shape[1] - mirrors :], mirrored
+    )
     payload[:, :, :width] = by_peer(partial_sums, devices)
     for group in range(groups):
         lanes = slice((group + 1) * width, (group + 2) * width)
@@ -573,22 +571,21 @@
     sent = send_list[0].T
     sources = src_slot.reshape(-1, LANES)
     targets = dst_slot.reshape(-1, LANES)
-    blocks = -(-slots // BLOCK)
+    blocks = node_dev // BLOCK
 
     payload_shape = (devices, per_peer, 2 * width)
-    payload, scaled, picking, source_columns, targets = run(
+    payload, scaled, picking, sources, targets = run(
         pick_rows,
         "pick_rows",
         [
             pltpu.HBM(payload_shape, BF16),
             pltpu.VMEM((node_dev, width), BF16),
             pltpu.VMEM((mirrors, node_dev), BF16),
-            pltpu.VMEM((LANES, edges // LANES), I32),
+            pltpu.VMEM(sources.shape, I32),
             pltpu.VMEM(targets.shape, I32),
         ],
-        smem=[edge_count],
         hbm=[features, cotangent, in_count, sent, sources, targets],
-        scratch=staged_for(6, features, cotangent, in_count, sent, sources)
+        scratch=staged_for(6, features, cotangent, in_count, sent)
         + [pltpu.VMEM(payload_shape, BF16), pltpu.SemaphoreType.DMA],
         flops=4 * mirrors * node_dev * width,
     )
@@ -596,23 +593,24 @@
 
     rows_bf16 = pltpu.VMEM((node_dev, width), BF16)
     rows_f32 = pltpu.VMEM((node_dev, width), F32)
-    counts, scaled, mirror_counts, partial_sums = run(
+    counts, scaled, mirror_rows, partial_sums = run(
         count_edges,
         "count_edges",
         [
-            pltpu.HBM((slots, slots), BF16),
+            pltpu.HBM((node_dev, slots), BF16),
             pltpu.HBM((node_dev, width), BF16),
-            pltpu.VMEM((mirrors, mirrors), BF16),
+            pltpu.VMEM((mirrors, slots), BF16),
             pltpu.VMEM((mirrors, 2 * width), F32),
         ],
+        smem=[edge_count],
         hbm=[features],
-        vmem=[scaled, source_columns, targets],
+        vmem=[scaled, sources, targets],
         scratch=[
             rows_bf16,
             pltpu.SemaphoreType.DMA,
             pltpu.VMEM((edges, slots), F8),
             pltpu.VMEM((slots, edges), F8),
-            pltpu.VMEM((slots, slots), BF16),
+            pltpu.VMEM((node_dev, slots), BF16),
             pltpu.SemaphoreType.DMA((blocks + 1,)),
         ],
         flops=2 * slots * edges * slots,
@@ -621,24 +619,29 @@
         mirror_sums,
         "mirror_sums",
         [pltpu.HBM(payload_shape, BF16)],
-        vmem=[partial_sums, mirror_counts, mirrored],
+        vmem=[partial_sums, mirror_rows, mirrored],
         scratch=[pltpu.VMEM(payload_shape, BF16), pltpu.SemaphoreType.DMA],
         flops=4 * mirrors * mirrors * width,
     )
     returned = exchange(payload).reshape(mirrors, 2 * width)
-    forward, features_in, backward = run(
+    forward, features_in, backward, mirror_rows = run(
         local_sums,
         "local_sums",
-        [rows_f32, rows_bf16, pltpu.HBM((node_dev, width), F32)],
+        [
+            rows_f32,
+            rows_bf16,
+            pltpu.HBM((node_dev, width), F32),
+            pltpu.HBM((mirrors, slots), BF16),
+        ],
         hbm=[counts, features, scaled],
-        vmem=[mirrored],
+        vmem=[mirrored, mirror_rows],
         scratch=[
-            pltpu.VMEM((slots, slots), BF16),
+            pltpu.VMEM((node_dev, slots), BF16),
             rows_bf16,
             rows_f32,
             pltpu.SemaphoreType.DMA((blocks,)),
             pltpu.SemaphoreType.DMA((node_dev // BLOCK,)),
-            pltpu.SemaphoreType.DMA((2,)),
+            pltpu.SemaphoreType.DMA((3,)),
         ],
         flops=4 * node_dev * slots * width,
     )
@@ -715,7 +718,7 @@
             pltpu.VMEM((node_dev, width), F32),
             pltpu.VMEM((mirrors, slots), BF16),
         ],
-        hbm=[counts],
+        hbm=[counts, mirror_rows],
         vmem=[message_one, grad_z_one, w_self_one],
         scratch=[pltpu.VMEM((node_dev, slots), BF16), pltpu.SemaphoreType.DMA((2,))],
         flops=2 * node_dev * (slots + width) * width,
@@ -729,7 +732,7 @@
             pltpu.VMEM((mirrors, width), BF16),
             pltpu.VMEM((1, width), F32),
         ],
-        vmem=[received, mirror_back, mirror_counts],
+        vmem=[received, mirror_back, mirror_rows],
     )
     received = exchange(payload)
     other = lax.ppermute(received, AXES, swap)

time: 69 us -> 68.1 us (0.987)
  no operation moved by 1% of the time
where the time goes in v6:
time: 68.1 us; the launch traced here: 67.7 us
  Pallas kernels  20.7 us (30%)
  waiting for transfers between devices  18.4 us (27%)
  blocking collectives  14.2 us (21%)
  starting transfers between devices  12.8 us (19%)
  between operations  1.49 us (2%)
    pallas_call x11, Pallas kernels, run(): pl.pallas_call(kernel, out_shape=tuple(outs), in_specs=[pl.BlockSpec(memo...  20.7 us
    all_to_all x3, waiting for transfers between devices, exchange(): return lax.all_to_all(rows, AXES, split_axis=0, concat_axis=0, tiled=True)  18 us
    all_to_all x1, blocking collectives, exchange(): return lax.all_to_all(rows, AXES, split_axis=0, concat_axis=0, tiled=True)  14.2 us
    all_to_all x3, starting transfers between devices, exchange(): return lax.all_to_all(rows, AXES, split_axis=0, concat_axis=0, tiled=True)  12.5 us
  transfers between devices with their start and end apart: 5, of which 5 were waited for; matrix products, arithmetic and copies ran while one was open for 0% of the time, Pallas kernels for 19%

profile of v6, /device:TPU:0, one launch (start us, length us, event | category | flops | bytes accessed | tf_op | source)
XLA Modules:
  0.0 67.7 jit_solution(3871560953688744612)
XLA Ops:
  0.6 2.4 %pick_rows.1 = (bf16[32,4,512]{2,1,0:T(4,128)(2,1)}, bf16[1024,256]{1,0:T(8,128)(2,1)S(1)}, bf16[128,1024]{1,0:T(8,128)(2,1)S(1)}, s32[16,128]{1,0:T(8,128)S(1)}, s32[16,128]{1,0:T(8,128)S(1)}) custom-call(bf16[1024,256]{1,0:T(8,128)(2,1)} %features_at.5, bf16[1024,256]{1,0:T(8,128)(2,1)} %cotangent_at.3, s32[8,128]{1,0:T(8,128)} %bitcast.10, ...), custom_call_target="tpu_custom_call" | custom-call | flops 134217728 | tf_op jit(solution)/shard_map/pick_rows/pallas_call | solution.py:41
  3.1 7.3 %all-to-all-start = ((bf16[32,4,512]{2,1,0:T(4,128)(2,1)}), bf16[32,4,512]{2,1,0:T(4,128)(2,1)S(1)}, u32[]{:S(2)}, u32[]{:S(2)}) async-start(bf16[32,4,512]{2,1,0:T(4,128)(2,1)} %get-tuple-element.40), calls=%async_computation | async-start | bytes 262144 | tf_op jit(solution)/shard_map/all_to_all | solution.py:35
  11.0 3.9 %count_edges.1 = (bf16[1024,1152]{1,0:T(8,128)(2,1)}, bf16[1024,256]{1,0:T(8,128)(2,1)}, bf16[128,1152]{1,0:T(8,128)(2,1)S(1)}, f32[128,512]{1,0:T(8,128)S(1)}) custom-call(s32[1]{0:T(128)S(6)} %copy.17.edge_count, bf16[1024,256]{1,0:T(8,128)(2,1)} %features_at.5, bf16[1024,256]{1,0:T(8,128)(2,1)S(1)} %get-tuple-element.35.scaled, ...), custom_call_target="tpu_custom_call" | custom-call | flops 5435817984 | tf_op jit(solution)/shard_map/count_edges/pallas_call | solution.py:41
  15.0 3.6 %all-to-all-done = bf16[32,4,512]{2,1,0:T(4,128)(2,1)S(1)} async-done(((bf16[32,4,512]{2,1,0:T(4,128)(2,1)}), bf16[32,4,512]{2,1,0:T(4,128)(2,1)S(1)}, u32[]{:S(2)}, u32[]{:S(2)}) %all-to-all-start) | async-done | bytes 131104 | tf_op jit(solution)/shard_map/all_to_all | solution.py:35
  18.6 0.9 %mirror_sums.1 = bf16[32,4,512]{2,1,0:T(4,128)(2,1)} custom-call(f32[128,512]{1,0:T(8,128)S(1)} %get-tuple-element.44.partial_in, bf16[128,1152]{1,0:T(8,128)(2,1)S(1)} %get-tuple-element.41.mirror_rows, bf16[128,512]{1,0:T(8,128)(2,1)S(1)} %reshape.40.mirrored), custom_call_target="tpu_custom_call" | custom-call | flops 16777216 | tf_op jit(solution)/shard_map/mirror_sums/pallas_call | solution.py:41
  19.5 2.6 %all-to-all-start.1 = ((bf16[32,4,512]{2,1,0:T(4,128)(2,1)}), bf16[32,4,512]{2,1,0:T(4,128)(2,1)S(1)}, u32[]{:S(2)}, u32[]{:S(2)}) async-start(bf16[32,4,512]{2,1,0:T(4,128)(2,1)} %mirror_sums.1), calls=%async_computation.1 | async-start | bytes 262144 | tf_op jit(solution)/shard_map/all_to_all | solution.py:35
  22.1 0.0 copy-start.1
  22.1 0.0 copy-start.2
  22.2 0.0 copy-start.5
  22.2 3.8 %local_sums.1 = (f32[1024,256]{1,0:T(8,128)S(1)}, bf16[1024,256]{1,0:T(8,128)(2,1)S(1)}, f32[1024,256]{1,0:T(8,128)}, bf16[128,1152]{1,0:T(8,128)(2,1)}) custom-call(bf16[1024,1152]{1,0:T(8,128)(2,1)} %get-tuple-element.38.counts_at, bf16[1024,256]{1,0:T(8,128)(2,1)} %features_at.5, bf16[1024,256]{1,0:T(8,128)(2,1)} %get-tuple-element.39.scaled_at, ...), custom_call_target="tpu_custom_call" | custom-call | flops 1207959552 | tf_op jit(solution)/shard_map/local_sums/pallas_call | solution.py:41
  26.0 4.3 %all-to-all-done.1 = bf16[32,4,512]{2,1,0:T(4,128)(2,1)S(1)} async-done(((bf16[32,4,512]{2,1,0:T(4,128)(2,1)}), bf16[32,4,512]{2,1,0:T(4,128)(2,1)S(1)}, u32[]{:S(2)}, u32[]{:S(2)}) %all-to-all-start.1) | async-done | bytes 131104 | tf_op jit(solution)/shard_map/all_to_all | solution.py:35
  30.4 2.6 %middle.1 = (bf16[1024,256]{1,0:T(8,128)(2,1)S(1)}, bf16[512,256]{1,0:T(8,128)(2,1)S(1)}, f32[4,128]{1,0:T(4,128)S(1)}, bf16[1024,256]{1,0:T(8,128)(2,1)S(1)}, b...) custom-call(s32[1]{0:T(128)} %bitcast.core, ...), custom_call_target="tpu_custom_call" | custom-call | flops 1342177280 | tf_op jit(solution)/shard_map/middle/pallas_call | solution.py:41
  33.1 0.3 collective-permute-start
  33.4 1.0 %messages.1 = (bf16[1024,256]{1,0:T(8,128)(2,1)S(1)}, f32[128,256]{1,0:T(8,128)S(1)}, f32[512,256]{1,0:T(8,128)S(1)}) custom-call(s32[1]{0:T(128)} %bitcast.core, s32[8,128]{1,0:T(8,128)S(1)} %bitcast.12, bf16[1024,256]{1,0:T(8,128)(2,1)S(1)} %get-tuple-element.47.grad_z, bf16[256,256]{1,0:T(8,128)(2,1)S(1)} %copy-done, ...), custom_call_target="tpu_custom_call" | custom-call | flops 402653184 | tf_op jit(solution)/shard_map/messages/pallas_call | solution.py:41
  34.4 0.3 collective-permute-done.other_half
  34.7 0.9 %join_first.1 = bf16[32,4,1408]{2,1,0:T(4,128)(2,1)} custom-call(f32[512,256]{1,0:T(8,128)S(1)} %get-tuple-element.52.own_half, bf16[512,256]{1,0:T(8,128)(2,1)S(1)} %collective-permute-done.other_half, f32[128,256]{1,0:T(8,128)S(1)} %get-tuple-element.54.picked, f32[4,128]{1,0:T(4,128)S(1)} %get-tuple-element.55.bias_rows), custom_call_target="tpu_custom_call" | custom-call | tf_op jit(solution)/shard_map/join_first/pallas_call | solution.py:41
  35.5 2.6 %all-to-all-start.2 = ((bf16[32,4,1408]{2,1,0:T(4,128)(2,1)}), bf16[32,4,1408]{2,1,0:T(4,128)(2,1)S(1)}, u32[]{:S(2)}, u32[]{:S(2)}) async-start(bf16[32,4,1408]{2,1,0:T(4,128)(2,1)} %join_first.1), calls=%async_computation.2 | async-start | bytes 720896 | tf_op jit(solution)/shard_map/all_to_all | solution.py:35
  38.2 2.6 %local_back.1 = (f32[128,256]{1,0:T(8,128)S(1)}, f32[1024,256]{1,0:T(8,128)S(1)}, bf16[128,1152]{1,0:T(8,128)(2,1)S(1)}) custom-call(bf16[1024,1152]{1,0:T(8,128)(2,1)} %get-tuple-element.38.counts_at, bf16[128,1152]{1,0:T(8,128)(2,1)} %get-tuple-element.56.mirror_at, bf16[1024,256]{1,0:T(8,128)(2,1)S(1)} %get-tuple-element.57.message_one, ...), custom_call_target="tpu_custom_call" | custom-call | flops 738197504 | tf_op jit(solution)/shard_map/local_back/pallas_call | solution.py:41
  40.7 10.0 %all-to-all-done.2.received = bf16[32,4,1408]{2,1,0:T(4,128)(2,1)S(1)} async-done(((bf16[32,4,1408]{2,1,0:T(4,128)(2,1)}), bf16[32,4,1408]{2,1,0:T(4,128)(2,1)S(1)}, u32[]{:S(2)}, u32[]{:S(2)}) %all-to-all-start.2) | async-done | bytes 360480 | tf_op jit(solution)/shard_map/all_to_all | solution.py:35
  50.8 0.3 join_second.1
  51.0 14.2 %all_to_all.20.received = bf16[32,4,1280]{2,1,0:T(4,128)(2,1)S(1)} all-to-all(bf16[32,4,1280]{2,1,0:T(4,128)(2,1)S(1)} %get-tuple-element.60), channel_id=1, replica_groups=mesh['dom'=8,'sub'=4] {'dom','sub'}, dimensions={0} | all-to-all | bytes 655360 | tf_op jit(solution)/shard_map/all_to_all | solution.py:35
  65.3 1.5 %finish.1 = (bf16[1024,256]{1,0:T(8,128)(2,1)}, f32[1024,256]{1,0:T(8,128)}, f32[1,256]{1,0:T(1,128)}) custom-call(s32[1]{0:T(128)} %bitcast.core, bf16[32,4,1280]{2,1,0:T(4,128)(2,1)S(1)} %all_to_all.20.received, bf16[128,256]{1,0:T(8,128)(2,1)S(1)} %get-tuple-element.61.mirrored, bf16[128,1024]{1,0:T(8,128)(2,1)S(1)} %get-tuple-element.45.picking, ...), custom_call_target="tpu_custom_call" | custom-call | flops 201326592 | tf_op jit(solution)/shard_map/finish/pallas_call | solution.py:41
  66.7 0.2 collective-permute-done.1.received
  66.9 0.8 %finish_other.1 = f32[1024,256]{1,0:T(8,128)} custom-call(s32[1]{0:T(128)} %bitcast.core, f32[1024,256]{1,0:T(8,128)} %get-tuple-element.65.weights_in, bf16[32,4,1280]{2,1,0:T(4,128)(2,1)S(1)} %collective-permute-done.1.received), custom_call_target="tpu_custom_call", output_to_operand_aliasing={{}: (1, {})} | custom-call | tf_op jit(solution)/shard_map/finish_other/pallas_call | solution.py:41
  (12 shorter events, 0.1 us)
Async XLA Ops:
  3.1 15.5 %all-to-all-start = ((bf16[32,4,512]{2,1,0:T(4,128)(2,1)}), bf16[32,4,512]{2,1,0:T(4,128)(2,1)S(1)}, u32[]{:S(2)}, u32[]{:S(2)}) async-start(bf16[32,4,512]{2,1,0:T(4,128)(2,1)} %get-tuple-element.40), calls=%async_computation | async-start | bytes 262144 | tf_op jit(solution)/shard_map/all_to_all | solution.py:35
  19.5 10.8 %all-to-all-start.1 = ((bf16[32,4,512]{2,1,0:T(4,128)(2,1)}), bf16[32,4,512]{2,1,0:T(4,128)(2,1)S(1)}, u32[]{:S(2)}, u32[]{:S(2)}) async-start(bf16[32,4,512]{2,1,0:T(4,128)(2,1)} %mirror_sums.1), calls=%async_computation.1 | async-start | bytes 262144 | tf_op jit(solution)/shard_map/all_to_all | solution.py:35
  22.1 8.3 %copy-start = (bf16[256,256]{1,0:T(8,128)(2,1)S(1)}, bf16[256,256]{1,0:T(8,128)(2,1)}, u32[]{:S(2)}) copy-start(bf16[256,256]{1,0:T(8,128)(2,1)} %w_nbr_one.3) | copy-start | bytes 393220
  22.1 8.3 %copy-start.1 = (bf16[256,256]{1,0:T(8,128)(2,1)S(1)}, bf16[256,256]{1,0:T(8,128)(2,1)}, u32[]{:S(2)}) copy-start(bf16[256,256]{1,0:T(8,128)(2,1)} %w_self_one.3) | copy-start | bytes 393220
  22.1 8.3 %copy-start.2 = (s32[1024]{0:T(1024)S(1)}, s32[1024]{0:T(1024)}, u32[]{:S(2)}) copy-start(s32[1024]{0:T(1024)} %param.19) | copy-start | bytes 12292
  22.2 8.3 %copy-start.3 = (bf16[256,256]{1,0:T(8,128)(2,1)S(1)}, bf16[256,256]{1,0:T(8,128)(2,1)}, u32[]{:S(2)}) copy-start(bf16[256,256]{1,0:T(8,128)(2,1)} %w_nbr_two.1) | copy-start | bytes 393220
  22.2 8.2 %copy-start.4 = (bf16[256,256]{1,0:T(8,128)(2,1)S(1)}, bf16[256,256]{1,0:T(8,128)(2,1)}, u32[]{:S(2)}) copy-start(bf16[256,256]{1,0:T(8,128)(2,1)} %w_self_two.1) | copy-start | bytes 393220
  22.2 8.2 %copy-start.5 = (f32[256]{0:T(256)S(1)}, f32[256]{0:T(256)}, u32[]{:S(2)}) copy-start(f32[256]{0:T(256)} %param.16) | copy-start | bytes 3076
  33.1 1.6 %collective-permute-start = (bf16[512,256]{1,0:T(8,128)(2,1)S(1)}, bf16[512,256]{1,0:T(8,128)(2,1)S(1)}, u32[]{:S(2)}, u32[]{:S(2)}) collective-permute-start(bf16[512,256]{1,0:T(8,128)(2,1)S(1)} %get-tuple-element.53), channel_id=1, source_target_pairs={{0,1},{1,0},{2,3},{3,2},{4,5},{5,4},{6,7},{7,6},{8,9},{9,8},{10,11... | collective-permute-start | bytes 786440 | tf_op jit(solution)/shard_map/ppermute | solution.py:683
  35.5 15.2 %all-to-all-start.2 = ((bf16[32,4,1408]{2,1,0:T(4,128)(2,1)}), bf16[32,4,1408]{2,1,0:T(4,128)(2,1)S(1)}, u32[]{:S(2)}, u32[]{:S(2)}) async-start(bf16[32,4,1408]{2,1,0:T(4,128)(2,1)} %join_first.1), calls=%async_computation.2 | async-start | bytes 720896 | tf_op jit(solution)/shard_map/all_to_all | solution.py:35
  65.3 1.6 %collective-permute-start.1 = (bf16[32,4,1280]{2,1,0:T(4,128)(2,1)S(1)}, bf16[32,4,1280]{2,1,0:T(4,128)(2,1)S(1)}, u32[]{:S(2)}, u32[]{:S(2)}) collective-permute-start(bf16[32,4,1280]{2,1,0:T(4,128)(2,1)S(1)} %all_to_all.20.received), channel_id=1, source_target_pairs={{0,1},{1,0},{2,3},{3,2},{4,5},{5,4},{6,7},{7,6},{8,9},{9,8},{10,11... | collective-permute-start | bytes 983048 | tf_op jit(solution)/shard_map/ppermute | solution.py:738

commit v7 on v6

--- a/solution.py
+++ b/solution.py
@@ -16,6 +16,7 @@
 LANES = 128
 BLOCK = 256
 ROWS = 512
+EARLY = 2
 VMEM_LIMIT = 24 * 2**20
 
 
@@ -166,13 +167,35 @@
     out_copy.wait()
 
 
+def fill_from_hot(from_hot, sources):
+    edges, slots = from_hot.shape
+    source_columns = sources[...].T
+    lane_ids = iota((LANES, slots), 1, I16)
+    for block in range(edges // LANES):
+        column = jnp.broadcast_to(source_columns[:, block : block + 1], (LANES, LANES)).astype(I16)
+        column = jnp.concatenate([column] * (slots // LANES), axis=1)
+        from_hot[pl.ds(block * LANES, LANES), :] = edge_hot(lane_ids == column)
+
+
+def fill_into_hot(into_hot, targets, edge_count, first, place, size):
+    edge_ids = iota(targets.shape, 0) * LANES + iota(targets.shape, 1)
+    target_rows = jnp.where(edge_ids < edge_count[0], targets[...], -1).astype(I16)
+    row_ids = iota((LANES, LANES), 0, I16)
+    for block in range(into_hot.shape[1] // LANES):
+        target_row = target_rows[block : block + 1, :]
+        for part in range(0, size, LANES):
+            into_hot[pl.ds(place + part, LANES), pl.ds(block * LANES, LANES)] = edge_hot(
+                row_ids + jnp.int16(first + part) == target_row
+            )
+
+
 def count_edges(
     edge_count,
     features_at,
     scaled,
     sources,
     targets,
-    counts_out,
+    counts_at,
     scaled_at,
     mirror_rows,
     partial_out,
@@ -185,41 +208,29 @@
 ):
     node_dev, width = features.shape
     slots, edges = into_hot.shape
+    early = counts.shape[0]
     feature_copy = pltpu.make_async_copy(features_at, features, semaphore)
     feature_copy.start()
-    sends = [pltpu.make_async_copy(scaled, scaled_at, out_semaphores.at[node_dev // BLOCK])]
+    sends = [pltpu.make_async_copy(scaled, scaled_at, out_semaphores.at[early // BLOCK])]
     sends[0].start()
-    source_columns = sources[...].T
-    lane_ids = iota((LANES, slots), 1, I16)
-    for block in range(edges // LANES):
-        column = jnp.broadcast_to(source_columns[:, block : block + 1], (LANES, LANES)).astype(I16)
-        column = jnp.concatenate([column] * (slots // LANES), axis=1)
-        from_hot[pl.ds(block * LANES, LANES), :] = edge_hot(lane_ids == column)
-    edge_ids = iota(targets.shape, 0) * LANES + iota(targets.shape, 1)
-    target_rows = jnp.where(edge_ids < edge_count[0], targets[...], -1).astype(I16)
-    row_ids = iota((LANES, LANES), 0, I16)
-    for start in range(0, slots, BLOCK):
-        size = min(BLOCK, slots - start)
-        for block in range(edges // LANES):
-            target_row = target_rows[block : block + 1, :]
-            for part in range(start, start + size, LANES):
-                into_hot[pl.ds(part, LANES), pl.ds(block * LANES, LANES)] = edge_hot(
-                    row_ids + jnp.int16(part) == target_row
-                )
-        rows = pl.ds(start, size)
-        block_counts = dot(into_hot[rows, :], from_hot[...]).astype(BF16)
-        if start < node_dev:
-            counts[rows, :] = block_counts
-            copy = pltpu.make_async_copy(
-                counts.at[rows], counts_out.at[rows], out_semaphores.at[start // BLOCK]
-            )
-            copy.start()
-            sends.append(copy)
-        else:
-            mirror_rows[pl.ds(start - node_dev, size), :] = block_counts
+    fill_from_hot(from_hot, sources)
+    for start in range(0, early, BLOCK):
+        rows = pl.ds(start, BLOCK)
+        fill_into_hot(into_hot, targets, edge_count, start, start, BLOCK)
+        counts[rows, :] = dot(into_hot[rows, :], from_hot[...]).astype(BF16)
+        copy = pltpu.make_async_copy(
+            counts.at[rows], counts_at.at[rows], out_semaphores.at[start // BLOCK]
+        )
+        copy.start()
+        sends.append(copy)
+    fill_into_hot(into_hot, targets, edge_count, early, early, slots - early)
+    mirror_rows[...] = dot(into_hot[node_dev:, :], from_hot[...]).astype(BF16)
+    late_columns = dot(into_hot[early:node_dev, :], from_hot[:, node_dev:]).astype(BF16)
     feature_copy.wait()
     partial_out[:, :width] = dot(mirror_rows[:, :node_dev], features[...])
-    partial_out[:, width:] = tdot(counts[:, node_dev:], scaled[...])
+    partial_out[:, width:] = tdot(counts[:, node_dev:], scaled[:early, :]) + tdot(
+        late_columns, scaled[early:, :]
+    )
     for copy in sends:
         copy.wait()
 
@@ -237,40 +248,49 @@
 
 
 def local_sums(
-    counts_at,
+    edge_count,
+    early_at,
     features_at,
     scaled_at,
+    sources,
+    targets,
     mirrored,
     mirror_rows,
     forward,
     features,
     backward_at,
     mirror_at,
+    late_at,
+    from_hot,
+    into_hot,
     counts,
     scaled,
     backward,
-    block_semaphores,
+    semaphores,
     out_semaphores,
-    semaphores,
 ):
     node_dev, width = features.shape
-    blocks = [(start, BLOCK) for start in range(0, node_dev, BLOCK)]
-    loads = start_all([scaled_at], [scaled], semaphores)
-    mirror_copy = pltpu.make_async_copy(mirror_rows, mirror_at, semaphores.at[2])
-    mirror_copy.start()
-    copies = []
-    for index, (start, size) in enumerate(blocks):
-        rows = pl.ds(start, size)
-        copy = pltpu.make_async_copy(
-            counts_at.at[rows], counts.at[rows], block_semaphores.at[index]
-        )
-        copy.start()
-        copies.append(copy)
-    loads.append(pltpu.make_async_copy(features_at, features, semaphores.at[1]))
-    loads[1].start()
-    for copy in [loads[0]] + copies:
+    early = early_at.shape[0]
+    loads = start_all(
+        [scaled_at, early_at, features_at],
+        [scaled, counts.at[pl.ds(0, early)], features],
+        semaphores,
+    )
+    blocks = node_dev // BLOCK
+    sends = [pltpu.make_async_copy(mirror_rows, mirror_at, out_semaphores.at[blocks])]
+    sends[0].start()
+    fill_from_hot(from_hot, sources)
+    for start in range(early, node_dev, BLOCK):
+        rows = pl.ds(start - early, BLOCK)
+        fill_into_hot(into_hot, targets, edge_count, start, start - early, BLOCK)
+        counts[pl.ds(start, BLOCK), :] = dot(into_hot[rows, :], from_hot[...]).astype(BF16)
+    late = pl.ds(early, node_dev - early)
+    sends.append(
+        pltpu.make_async_copy(counts.at[late], late_at, out_semaphores.at[blocks + 1])
+    )
+    sends[1].start()
+    for copy in loads:
         copy.wait()
-    sends = []
     for index, start in enumerate(range(0, node_dev, BLOCK)):
         rows = pl.ds(start, BLOCK)
         backward[rows, :] = tdot(counts[:, rows], scaled[...]) + tdot(
@@ -281,14 +301,12 @@
         )
         copy.start()
         sends.append(copy)
-    for copy in loads[1:]:
-        copy.wait()
     for start in range(0, node_dev, BLOCK):
         rows = pl.ds(start, BLOCK)
         forward[rows, :] = dot(counts[rows, :node_dev], features[...]) + dot(
             counts[rows, node_dev:], mirrored[:, :width]
         )
-    for copy in sends + [mirror_copy]:
+    for copy in sends:
         copy.wait()
 
 
@@ -425,7 +443,8 @@
 
 
 def local_back(
-    counts_at,
+    early_at,
+    late_at,
     mirror_at,
     message_one,
     grad_z,
@@ -437,7 +456,12 @@
     semaphores,
 ):
     node_dev, width = grad_z.shape
-    copies = start_all([counts_at, mirror_at], [counts, mirror_rows], semaphores)
+    early = early_at.shape[0]
+    copies = start_all(
+        [early_at, late_at, mirror_at],
+        [counts.at[pl.ds(0, early)], counts.at[pl.ds(early, node_dev - early)], mirror_rows],
+        semaphores,
+    )
     for start in range(0, node_dev, BLOCK):
         rows = pl.ds(start, BLOCK)
         local_out[rows, :] = dot_transposed(grad_z[rows, :], w_self_one[...])
@@ -593,11 +617,12 @@
 
     rows_bf16 = pltpu.VMEM((node_dev, width), BF16)
     rows_f32 = pltpu.VMEM((node_dev, width), F32)
-    counts, scaled, mirror_rows, partial_sums = run(
+    early = node_dev * EARLY // 4
+    early_counts, scaled, mirror_rows, partial_sums = run(
         count_edges,
         "count_edges",
         [
-            pltpu.HBM((node_dev, slots), BF16),
+            pltpu.HBM((early, slots), BF16),
             pltpu.HBM((node_dev, width), BF16),
             pltpu.VMEM((mirrors, slots), BF16),
             pltpu.VMEM((mirrors, 2 * width), F32),
@@ -610,10 +635,10 @@
             pltpu.SemaphoreType.DMA,
             pltpu.VMEM((edges, slots), F8),
             pltpu.VMEM((slots, edges), F8),
-            pltpu.VMEM((node_dev, slots), BF16),
-            pltpu.SemaphoreType.DMA((blocks + 1,)),
-        ],
-        flops=2 * slots * edges * slots,
+            pltpu.VMEM((early, slots), BF16),
+            pltpu.SemaphoreType.DMA((early // BLOCK + 1,)),
+        ],
+        flops=2 * (early + 2 * mirrors) * edges * slots,
     )
     (payload,) = run(
         mirror_sums,
@@ -624,7 +649,7 @@
         flops=4 * mirrors * mirrors * width,
     )
     returned = exchange(payload).reshape(mirrors, 2 * width)
-    forward, features_in, backward, mirror_rows = run(
+    forward, features_in, backward, mirror_rows, late_counts = run(
         local_sums,
         "local_sums",
         [
@@ -632,18 +657,21 @@
             rows_bf16,
             pltpu.HBM((node_dev, width), F32),
             pltpu.HBM((mirrors, slots), BF16),
-        ],
-        hbm=[counts, features, scaled],
-        vmem=[mirrored, mirror_rows],
+            pltpu.HBM((node_dev - early, slots), BF16),
+        ],
+        smem=[edge_count],
+        hbm=[early_counts, features, scaled],
+        vmem=[sources, targets, mirrored, mirror_rows],
         scratch=[
+            pltpu.VMEM((edges, slots), F8),
+            pltpu.VMEM((node_dev - early, edges), F8),
             pltpu.VMEM((node_dev, slots), BF16),
             rows_bf16,
             rows_f32,
-            pltpu.SemaphoreType.DMA((blocks,)),
-            pltpu.SemaphoreType.DMA((node_dev // BLOCK,)),
             pltpu.SemaphoreType.DMA((3,)),
-        ],
-        flops=4 * node_dev * slots * width,
+            pltpu.SemaphoreType.DMA((blocks + 2,)),
+        ],
+        flops=4 * node_dev * slots * width + 2 * (node_dev - early) * edges * slots,
     )
 
     half = 2 * width
@@ -718,9 +746,9 @@
             pltpu.VMEM((node_dev, width), F32),
             pltpu.VMEM((mirrors, slots), BF16),
         ],
-        hbm=[counts, mirror_rows],
+        hbm=[early_counts, late_counts, mirror_rows],
         vmem=[message_one, grad_z_one, w_self_one],
-        scratch=[pltpu.VMEM((node_dev, slots), BF16), pltpu.SemaphoreType.DMA((2,))],
+        scratch=[pltpu.VMEM((node_dev, slots), BF16), pltpu.SemaphoreType.DMA((3,))],
         flops=2 * node_dev * (slots + width) * width,
     )
     norm_factor = float(node_dev * devices) ** -0.5

time: 68.1 us -> 68.2 us (level)
  waiting for transfers between devices: 18.4 us -> 19.3 us
  Pallas kernels: 20.7 us -> 19.8 us
    all_to_all x3, waiting for transfers between devices: 18 us -> 18.9 us  [exchange(): return lax.all_to_all(rows, AXES, split_axis=0, concat_axis=0, tiled=True)]
    pallas_call x11, Pallas kernels: 20.7 us -> 19.8 us  [run(): pl.pallas_call(kernel, out_shape=tuple(outs), in_specs=[pl.BlockSpec(memo...]
  transfers between devices with their start and end apart: 5 -> 5, of which waited for: 5 -> 5; matrix products, arithmetic and copies ran while one was open for 0% -> 0% of each run, Pallas kernels for 19% -> 18%
where the time goes in v7:
time: 68.2 us; the launch traced here: 67.7 us
  Pallas kernels  19.8 us (29%)
  waiting for transfers between devices  19.3 us (28%)
  blocking collectives  14.2 us (21%)
  starting transfers between devices  12.8 us (19%)
  between operations  1.49 us (2%)
    pallas_call x11, Pallas kernels, run(): pl.pallas_call(kernel, out_shape=tuple(outs), in_specs=[pl.BlockSpec(memo...  19.8 us
    all_to_all x3, waiting for transfers between devices, exchange(): return lax.all_to_all(rows, AXES, split_axis=0, concat_axis=0, tiled=True)  18.9 us
    all_to_all x1, blocking collectives, exchange(): return lax.all_to_all(rows, AXES, split_axis=0, concat_axis=0, tiled=True)  14.2 us
    all_to_all x3, starting transfers between devices, exchange(): return lax.all_to_all(rows, AXES, split_axis=0, concat_axis=0, tiled=True)  12.5 us
  transfers between devices with their start and end apart: 5, of which 5 were waited for; matrix products, arithmetic and copies ran while one was open for 0% of the time, Pallas kernels for 18%

profile of v7, /device:TPU:0, one launch (start us, length us, event | category | flops | bytes accessed | tf_op | source)
XLA Modules:
  0.0 67.7 jit_solution(1860955544574240910)
XLA Ops:
  0.6 2.4 %pick_rows.1 = (bf16[32,4,512]{2,1,0:T(4,128)(2,1)}, bf16[1024,256]{1,0:T(8,128)(2,1)S(1)}, bf16[128,1024]{1,0:T(8,128)(2,1)S(1)}, s32[16,128]{1,0:T(8,128)S(1)}, s32[16,128]{1,0:T(8,128)S(1)}) custom-call(bf16[1024,256]{1,0:T(8,128)(2,1)} %features_at.5, bf16[1024,256]{1,0:T(8,128)(2,1)} %cotangent_at.3, s32[8,128]{1,0:T(8,128)} %bitcast.10, ...), custom_call_target="tpu_custom_call" | custom-call | flops 134217728 | tf_op jit(solution)/shard_map/pick_rows/pallas_call | solution.py:42
  3.1 7.3 %all-to-all-start = ((bf16[32,4,512]{2,1,0:T(4,128)(2,1)}), bf16[32,4,512]{2,1,0:T(4,128)(2,1)S(1)}, u32[]{:S(2)}, u32[]{:S(2)}) async-start(bf16[32,4,512]{2,1,0:T(4,128)(2,1)} %get-tuple-element.41), calls=%async_computation | async-start | bytes 262144 | tf_op jit(solution)/shard_map/all_to_all | solution.py:36
  11.0 2.9 %count_edges.1 = (bf16[512,1152]{1,0:T(8,128)(2,1)}, bf16[1024,256]{1,0:T(8,128)(2,1)}, bf16[128,1152]{1,0:T(8,128)(2,1)S(1)}, f32[128,512]{1,0:T(8,128)S(1)}) custom-call(s32[1]{0:T(128)S(6)} %copy.17.edge_count, bf16[1024,256]{1,0:T(8,128)(2,1)} %features_at.5, bf16[1024,256]{1,0:T(8,128)(2,1)S(1)} %get-tuple-element.36.scaled, ...), custom_call_target="tpu_custom_call" | custom-call | flops 3623878656 | tf_op jit(solution)/shard_map/count_edges/pallas_call | solution.py:42
  14.0 4.6 %all-to-all-done = bf16[32,4,512]{2,1,0:T(4,128)(2,1)S(1)} async-done(((bf16[32,4,512]{2,1,0:T(4,128)(2,1)}), bf16[32,4,512]{2,1,0:T(4,128)(2,1)S(1)}, u32[]{:S(2)}, u32[]{:S(2)}) %all-to-all-start) | async-done | bytes 131104 | tf_op jit(solution)/shard_map/all_to_all | solution.py:36
  18.6 0.9 %mirror_sums.1 = bf16[32,4,512]{2,1,0:T(4,128)(2,1)} custom-call(f32[128,512]{1,0:T(8,128)S(1)} %get-tuple-element.45.partial_in, bf16[128,1152]{1,0:T(8,128)(2,1)S(1)} %get-tuple-element.42.mirror_rows, bf16[128,512]{1,0:T(8,128)(2,1)S(1)} %reshape.40.mirrored), custom_call_target="tpu_custom_call" | custom-call | flops 16777216 | tf_op jit(solution)/shard_map/mirror_sums/pallas_call | solution.py:42
  19.5 2.6 %all-to-all-start.1 = ((bf16[32,4,512]{2,1,0:T(4,128)(2,1)}), bf16[32,4,512]{2,1,0:T(4,128)(2,1)S(1)}, u32[]{:S(2)}, u32[]{:S(2)}) async-start(bf16[32,4,512]{2,1,0:T(4,128)(2,1)} %mirror_sums.1), calls=%async_computation.1 | async-start | bytes 262144 | tf_op jit(solution)/shard_map/all_to_all | solution.py:36
  22.1 0.0 copy-start.2
  22.1 0.0 copy-start.3
  22.2 0.0 copy-start.5
  22.2 3.9 %local_sums.1 = (f32[1024,256]{1,0:T(8,128)S(1)}, bf16[1024,256]{1,0:T(8,128)(2,1)S(1)}, f32[1024,256]{1,0:T(8,128)}, bf16[128,1152]{1,0:T(8,128)(2,1)}, bf16[512,1152]{1,0:T(8,128)(2,1)}) custom-call(s32[1]{0:T(128)S(6)} %copy.17.edge_count, bf16[512,1152]{1,0:T(8,128)(2,1)} %get-tuple-element.39.early_at, bf16[1024,256]{1,0:T(8,128)(2,1)} %features_at.5, ...), custom_call_target="tpu_custom_call" | custom-call | flops 3623878656 | tf_op jit(solution)/shard_map/local_sums/pallas_call | solution.py:42
  26.1 4.3 %all-to-all-done.1 = bf16[32,4,512]{2,1,0:T(4,128)(2,1)S(1)} async-done(((bf16[32,4,512]{2,1,0:T(4,128)(2,1)}), bf16[32,4,512]{2,1,0:T(4,128)(2,1)S(1)}, u32[]{:S(2)}, u32[]{:S(2)}) %all-to-all-start.1) | async-done | bytes 131104 | tf_op jit(solution)/shard_map/all_to_all | solution.py:36
  30.4 2.7 %middle.1 = (bf16[1024,256]{1,0:T(8,128)(2,1)S(1)}, bf16[512,256]{1,0:T(8,128)(2,1)S(1)}, f32[4,128]{1,0:T(4,128)S(1)}, bf16[1024,256]{1,0:T(8,128)(2,1)S(1)}, b...) custom-call(s32[1]{0:T(128)} %bitcast.core, ...), custom_call_target="tpu_custom_call" | custom-call | flops 1342177280 | tf_op jit(solution)/shard_map/middle/pallas_call | solution.py:42
  33.1 0.3 collective-permute-start
  33.4 1.1 %messages.1 = (bf16[1024,256]{1,0:T(8,128)(2,1)S(1)}, f32[128,256]{1,0:T(8,128)S(1)}, f32[512,256]{1,0:T(8,128)S(1)}) custom-call(s32[1]{0:T(128)} %bitcast.core, s32[8,128]{1,0:T(8,128)S(1)} %bitcast.12, bf16[1024,256]{1,0:T(8,128)(2,1)S(1)} %get-tuple-element.48.grad_z, bf16[256,256]{1,0:T(8,128)(2,1)S(1)} %copy-done, ...), custom_call_target="tpu_custom_call" | custom-call | flops 402653184 | tf_op jit(solution)/shard_map/messages/pallas_call | solution.py:42
  34.5 0.2 collective-permute-done.other_half
  34.7 0.8 %join_first.1 = bf16[32,4,1408]{2,1,0:T(4,128)(2,1)} custom-call(f32[512,256]{1,0:T(8,128)S(1)} %get-tuple-element.53.own_half, bf16[512,256]{1,0:T(8,128)(2,1)S(1)} %collective-permute-done.other_half, f32[128,256]{1,0:T(8,128)S(1)} %get-tuple-element.55.picked, f32[4,128]{1,0:T(4,128)S(1)} %get-tuple-element.56.bias_rows), custom_call_target="tpu_custom_call" | custom-call | tf_op jit(solution)/shard_map/join_first/pallas_call | solution.py:42
  35.6 2.6 %all-to-all-start.2 = ((bf16[32,4,1408]{2,1,0:T(4,128)(2,1)}), bf16[32,4,1408]{2,1,0:T(4,128)(2,1)S(1)}, u32[]{:S(2)}, u32[]{:S(2)}) async-start(bf16[32,4,1408]{2,1,0:T(4,128)(2,1)} %join_first.1), calls=%async_computation.2 | async-start | bytes 720896 | tf_op jit(solution)/shard_map/all_to_all | solution.py:36
  38.2 2.6 %local_back.1 = (f32[128,256]{1,0:T(8,128)S(1)}, f32[1024,256]{1,0:T(8,128)S(1)}, bf16[128,1152]{1,0:T(8,128)(2,1)S(1)}) custom-call(bf16[512,1152]{1,0:T(8,128)(2,1)} %get-tuple-element.39.early_at, bf16[512,1152]{1,0:T(8,128)(2,1)} %get-tuple-element.57.late_at, bf16[128,1152]{1,0:T(8,128)(2,1)} %get-tuple-element.58.mirror_at, ...), custom_call_target="tpu_custom_call" | custom-call | flops 738197504 | tf_op jit(solution)/shard_map/local_back/pallas_call | solution.py:42
  40.8 10.0 %all-to-all-done.2.received = bf16[32,4,1408]{2,1,0:T(4,128)(2,1)S(1)} async-done(((bf16[32,4,1408]{2,1,0:T(4,128)(2,1)}), bf16[32,4,1408]{2,1,0:T(4,128)(2,1)S(1)}, u32[]{:S(2)}, u32[]{:S(2)}) %all-to-all-start.2) | async-done | bytes 360480 | tf_op jit(solution)/shard_map/all_to_all | solution.py:36
  50.8 0.3 join_second.1
  51.0 14.2 %all_to_all.20.received = bf16[32,4,1280]{2,1,0:T(4,128)(2,1)S(1)} all-to-all(bf16[32,4,1280]{2,1,0:T(4,128)(2,1)S(1)} %get-tuple-element.62), channel_id=1, replica_groups=mesh['dom'=8,'sub'=4] {'dom','sub'}, dimensions={0} | all-to-all | bytes 655360 | tf_op jit(solution)/shard_map/all_to_all | solution.py:36
  65.3 1.5 %finish.1 = (bf16[1024,256]{1,0:T(8,128)(2,1)}, f32[1024,256]{1,0:T(8,128)}, f32[1,256]{1,0:T(1,128)}) custom-call(s32[1]{0:T(128)} %bitcast.core, bf16[32,4,1280]{2,1,0:T(4,128)(2,1)S(1)} %all_to_all.20.received, bf16[128,256]{1,0:T(8,128)(2,1)S(1)} %get-tuple-element.63.mirrored, bf16[128,1024]{1,0:T(8,128)(2,1)S(1)} %get-tuple-element.46.picking, ...), custom_call_target="tpu_custom_call" | custom-call | flops 201326592 | tf_op jit(solution)/shard_map/finish/pallas_call | solution.py:42
  66.7 0.2 collective-permute-done.1.received
  66.9 0.8 %finish_other.1 = f32[1024,256]{1,0:T(8,128)} custom-call(s32[1]{0:T(128)} %bitcast.core, f32[1024,256]{1,0:T(8,128)} %get-tuple-element.67.weights_in, bf16[32,4,1280]{2,1,0:T(4,128)(2,1)S(1)} %collective-permute-done.1.received), custom_call_target="tpu_custom_call", output_to_operand_aliasing={{}: (1, {})} | custom-call | tf_op jit(solution)/shard_map/finish_other/pallas_call | solution.py:42
  (12 shorter events, 0.1 us)
Async XLA Ops:
  3.1 15.5 %all-to-all-start = ((bf16[32,4,512]{2,1,0:T(4,128)(2,1)}), bf16[32,4,512]{2,1,0:T(4,128)(2,1)S(1)}, u32[]{:S(2)}, u32[]{:S(2)}) async-start(bf16[32,4,512]{2,1,0:T(4,128)(2,1)} %get-tuple-element.41), calls=%async_computation | async-start | bytes 262144 | tf_op jit(solution)/shard_map/all_to_all | solution.py:36
  19.5 10.8 %all-to-all-start.1 = ((bf16[32,4,512]{2,1,0:T(4,128)(2,1)}), bf16[32,4,512]{2,1,0:T(4,128)(2,1)S(1)}, u32[]{:S(2)}, u32[]{:S(2)}) async-start(bf16[32,4,512]{2,1,0:T(4,128)(2,1)} %mirror_sums.1), calls=%async_computation.1 | async-start | bytes 262144 | tf_op jit(solution)/shard_map/all_to_all | solution.py:36
  22.1 8.3 %copy-start = (bf16[256,256]{1,0:T(8,128)(2,1)S(1)}, bf16[256,256]{1,0:T(8,128)(2,1)}, u32[]{:S(2)}) copy-start(bf16[256,256]{1,0:T(8,128)(2,1)} %w_nbr_one.3) | copy-start | bytes 393220
  22.1 8.3 %copy-start.1 = (bf16[256,256]{1,0:T(8,128)(2,1)S(1)}, bf16[256,256]{1,0:T(8,128)(2,1)}, u32[]{:S(2)}) copy-start(bf16[256,256]{1,0:T(8,128)(2,1)} %w_self_one.3) | copy-start | bytes 393220
  22.1 8.3 %copy-start.2 = (s32[1024]{0:T(1024)S(1)}, s32[1024]{0:T(1024)}, u32[]{:S(2)}) copy-start(s32[1024]{0:T(1024)} %param.19) | copy-start | bytes 12292
  22.1 8.3 %copy-start.3 = (bf16[256,256]{1,0:T(8,128)(2,1)S(1)}, bf16[256,256]{1,0:T(8,128)(2,1)}, u32[]{:S(2)}) copy-start(bf16[256,256]{1,0:T(8,128)(2,1)} %w_nbr_two.1) | copy-start | bytes 393220
  22.2 8.3 %copy-start.4 = (bf16[256,256]{1,0:T(8,128)(2,1)S(1)}, bf16[256,256]{1,0:T(8,128)(2,1)}, u32[]{:S(2)}) copy-start(bf16[256,256]{1,0:T(8,128)(2,1)} %w_self_two.1) | copy-start | bytes 393220
  22.2 8.3 %copy-start.5 = (f32[256]{0:T(256)S(1)}, f32[256]{0:T(256)}, u32[]{:S(2)}) copy-start(f32[256]{0:T(256)} %param.16) | copy-start | bytes 3076
  33.1 1.6 %collective-permute-start = (bf16[512,256]{1,0:T(8,128)(2,1)S(1)}, bf16[512,256]{1,0:T(8,128)(2,1)S(1)}, u32[]{:S(2)}, u32[]{:S(2)}) collective-permute-start(bf16[512,256]{1,0:T(8,128)(2,1)S(1)} %get-tuple-element.54), channel_id=1, source_target_pairs={{0,1},{1,0},{2,3},{3,2},{4,5},{5,4},{6,7},{7,6},{8,9},{9,8},{10,11... | collective-permute-start | bytes 786440 | tf_op jit(solution)/shard_map/ppermute | solution.py:711
  35.6 15.2 %all-to-all-start.2 = ((bf16[32,4,1408]{2,1,0:T(4,128)(2,1)}), bf16[32,4,1408]{2,1,0:T(4,128)(2,1)S(1)}, u32[]{:S(2)}, u32[]{:S(2)}) async-start(bf16[32,4,1408]{2,1,0:T(4,128)(2,1)} %join_first.1), calls=%async_computation.2 | async-start | bytes 720896 | tf_op jit(solution)/shard_map/all_to_all | solution.py:36
  65.3 1.6 %collective-permute-start.1 = (bf16[32,4,1280]{2,1,0:T(4,128)(2,1)S(1)}, bf16[32,4,1280]{2,1,0:T(4,128)(2,1)S(1)}, u32[]{:S(2)}, u32[]{:S(2)}) collective-permute-start(bf16[32,4,1280]{2,1,0:T(4,128)(2,1)S(1)} %all_to_all.20.received), channel_id=1, source_target_pairs={{0,1},{1,0},{2,3},{3,2},{4,5},{5,4},{6,7},{7,6},{8,9},{9,8},{10,11... | collective-permute-start | bytes 983048 | tf_op jit(solution)/shard_map/ppermute | solution.py:766

commit v8 on v7

--- a/solution.py
+++ b/solution.py
@@ -36,7 +36,7 @@
     return lax.all_to_all(rows, AXES, split_axis=0, concat_axis=0, tiled=True)
 
 
-def run(kernel, name, outs, vmem=(), hbm=(), smem=(), scratch=(), flops=0, moved=0, aliases=None):
+def run(kernel, name, outs, vmem=(), hbm=(), smem=(), scratch=(), flops=0, moved=0):
     in_place = pl.BlockSpec(memory_space=pltpu.VMEM)
     remote = pl.BlockSpec(memory_space=pltpu.HBM)
     return pl.pallas_call(
@@ -49,7 +49,6 @@
         scratch_shapes=tuple(scratch),
         compiler_params=pltpu.CompilerParams(vmem_limit_bytes=VMEM_LIMIT),
         cost_estimate=pl.CostEstimate(flops=flops, bytes_accessed=moved, transcendentals=0),
-        input_output_aliases=aliases or {},
         name=name,
     )(
         *smem,
@@ -321,6 +320,7 @@
     core,
     cotangent_at,
     backward_at,
+    early_at,
     forward,
     returned,
     picking,
@@ -338,6 +338,7 @@
     h_one,
     pulled,
     cotangent,
+    early_counts,
     backward,
     semaphores,
     slope,
@@ -362,6 +363,8 @@
         slope[rows, :] = sigmoid * (1.0 + z_one * (1.0 - sigmoid))
     for copy in copies:
         copy.wait()
+    early_copy = pltpu.make_async_copy(early_at, early_counts, semaphores.at[2])
+    early_copy.start()
     bias_total = jnp.zeros((1, width), F32)
     for rows in blocks:
         pull = (backward[rows, :] + tdot(picking[:, rows], returned[:, width:])).astype(BF16)
@@ -390,9 +393,13 @@
         sent_half[:width, :] = tdot(features[...], grad_z[...]).astype(BF16)
         sent_half[width:, :] = tdot(mean_one[...], grad_z[...]).astype(BF16)
 
+    early_copy.wait()
+
 
 def messages(
     core,
+    late_at,
+    mirror_at,
     in_count,
     grad_z,
     w_nbr_one,
@@ -405,8 +412,12 @@
     message_one,
     picked,
     own_half,
+    late_counts,
+    mirror_rows,
+    semaphores,
 ):
     node_dev, width = grad_z.shape
+    copies = start_all([late_at, mirror_at], [late_counts, mirror_rows], semaphores)
     columns = inverse_columns(in_count)
     for index, start in enumerate(range(0, node_dev, BLOCK)):
         rows = pl.ds(start, BLOCK)
@@ -425,70 +436,47 @@
         own_half[:width, :] = tdot(h_one[...], cotangent[...])
         own_half[width:, :] = tdot(h_one[...], pulled[...])
 
-
-def join_first(own_half, other_half, picked, bias_rows, payload, rows_out, out_semaphore):
-    devices, per_peer, _ = rows_out.shape
+    for copy in copies:
+        copy.wait()
+
+
+def join_first(own_half, other_half, picked, bias_rows, payload):
+    devices, per_peer, _ = payload.shape
     mirrors, width = picked.shape
     groups = own_half.shape[0] // mirrors
-    rows_out[:, :, :width] = by_peer(picked[...], devices)
+    payload[:, :, :width] = by_peer(picked[...], devices)
     for group in range(groups):
         rows = pl.ds(group * mirrors, mirrors)
-        rows_out[:, :, (group + 1) * width : (group + 2) * width] = by_peer(
+        payload[:, :, (group + 1) * width : (group + 2) * width] = by_peer(
             own_half[rows, :] + other_half[rows, :].astype(F32), devices
         )
-    rows_out[:, :, (groups + 1) * width :] = jnp.broadcast_to(
+    payload[:, :, (groups + 1) * width :] = jnp.broadcast_to(
         bias_rows[...][None], (devices, per_peer, LANES)
     ).astype(BF16)
-    send(rows_out, payload, out_semaphore)
-
-
-def local_back(
-    early_at,
-    late_at,
-    mirror_at,
-    message_one,
-    grad_z,
-    w_self_one,
-    mirror_out,
-    local_out,
-    mirror_rows,
-    counts,
-    semaphores,
-):
-    node_dev, width = grad_z.shape
-    early = early_at.shape[0]
-    copies = start_all(
-        [early_at, late_at, mirror_at],
-        [counts.at[pl.ds(0, early)], counts.at[pl.ds(early, node_dev - early)], mirror_rows],
-        semaphores,
-    )
-    for start in range(0, node_dev, BLOCK):
-        rows = pl.ds(start, BLOCK)
-        local_out[rows, :] = dot_transposed(grad_z[rows, :], w_self_one[...])
-    for copy in copies:
-        copy.wait()
-    mirror_out[...] = tdot(counts[:, node_dev:], message_one[...])
-    for start in range(0, node_dev, BLOCK):
-        rows = pl.ds(start, BLOCK)
-        local_out[rows, :] += tdot(counts[:, rows], message_one[...])
 
 
 def join_second(
     norm_factor,
     received,
-    mirror_partial,
+    message_one,
+    early_counts,
+    late_counts,
     mirror_rows,
     payload,
     mirrored_out,
     bias_total,
 ):
     devices, per_peer, _ = payload.shape
-    mirrors, width = mirror_partial.shape
+    node_dev, width = message_one.shape
+    mirrors = mirror_rows.shape[0]
+    early = early_counts.shape[0]
     groups = payload.shape[2] // width - 1
     mirrored = by_row(received[:, :, :width]).astype(BF16)
     mirrored_out[...] = mirrored
-    partial_sums = mirror_partial[...] + tdot(
-        mirror_rows[:, mirror_rows.shape[1] - mirrors :], mirrored
+    partial_sums = (
+        tdot(early_counts[:, node_dev:], message_one[:early, :])
+        + tdot(late_counts[:, node_dev:], message_one[early:, :])
+        + tdot(mirror_rows[:, node_dev:], mirrored)
     )
     payload[:, :, :width] = by_peer(partial_sums, devices)
     for group in range(groups):
@@ -513,60 +501,72 @@
 
 
 def finish(
-    core,
     received,
     mirrored,
     picking,
+    early_counts,
+    late_counts,
     mirror_rows,
-    local_grad,
+    message_one,
+    grad_z,
+    w_self_one,
+    grad_features,
+    own_weights,
+):
+    node_dev, width = grad_z.shape
+    mirrors = picking.shape[0]
+    early = early_counts.shape[0]
+    returned = by_row(received[:, :, :width]).astype(BF16)
+    for start in range(0, node_dev, BLOCK):
+        rows = pl.ds(start, BLOCK)
+        grad_features[rows, :] = (
+            dot_transposed(grad_z[rows, :], w_self_one[...])
+            + tdot(early_counts[:, rows], message_one[:early, :])
+            + tdot(late_counts[:, rows], message_one[early:, :])
+            + tdot(picking[:, rows], returned)
+            + tdot(mirror_rows[:, rows], mirrored[...])
+        ).astype(BF16)
+    for group in range(own_weights.shape[0] // mirrors):
+        own_weights[pl.ds(group * mirrors, mirrors), :] = by_row(
+            received[:, :, (group + 1) * width : (group + 2) * width]
+        )
+
+
+def write_out(
+    core,
+    other,
+    grad_features,
+    own_weights,
     bias_total,
     features_at,
     weights_at,
     bias_at,
-    features_out,
-    weights_out,
+    other_weights,
     semaphores,
 ):
-    devices, per_peer, _ = received.shape
-    node_dev, width = local_grad.shape
-    mirrors = picking.shape[0]
-    half = weights_out.shape[0]
+    half, width = own_weights.shape
+    mirrors = other.shape[0] * other.shape[1]
+    mine = pl.multiple_of(core[0] * half, half)
+    theirs = pl.multiple_of((1 - core[0]) * half, half)
+    copies = [
+        pltpu.make_async_copy(grad_features, features_at, semaphores.at[0]),
+        pltpu.make_async_copy(own_weights, weights_at.at[pl.ds(mine, half)], semaphores.at[1]),
+        pltpu.make_async_copy(bias_total, bias_at, semaphores.at[2]),
+    ]
+    for copy in copies:
+        copy.start()
     for group in range(half // mirrors):
-        weights_out[pl.ds(group * mirrors, mirrors), :] = by_row(
-            received[:, :, (group + 1) * width : (group + 2) * width]
-        )
-    mine = pl.multiple_of(core[0] * half, half)
-    weights_copy = pltpu.make_async_copy(
-        weights_out, weights_at.at[pl.ds(mine, half)], semaphores.at[0]
-    )
-    weights_copy.start()
-    bias_copy = pltpu.make_async_copy(bias_total, bias_at, semaphores.at[2])
-    bias_copy.start()
-    returned = by_row(received[:, :, :width]).astype(BF16)
-    for start in range(0, node_dev, BLOCK):
-        rows = pl.ds(start, BLOCK)
-        features_out[rows, :] = (
-            local_grad[rows, :]
-            + tdot(picking[:, rows], returned)
-            + tdot(mirror_rows[:, rows], mirrored[...])
-        ).astype(BF16)
-    features_copy = pltpu.make_async_copy(features_out, features_at, semaphores.at[1])
-    features_copy.start()
-    weights_copy.wait()
-    bias_copy.wait()
-    features_copy.wait()
-
-
-def finish_other(core, weights_in, received, weights_at, weights_out, semaphore):
-    half, width = weights_out.shape
-    devices, per_peer, columns = received.shape
-    mirrors = devices * per_peer
-    for group in range(half // mirrors):
-        weights_out[pl.ds(group * mirrors, mirrors), :] = by_row(
-            received[:, :, (group + 1) * width : (group + 2) * width]
-        )
-    other = pl.multiple_of((1 - core[0]) * half, half)
-    send(weights_out, weights_at.at[pl.ds(other, half)], semaphore)
+        other_weights[pl.ds(group * mirrors, mirrors), :] = by_row(
+            other[:, :, (group + 1) * width : (group + 2) * width]
+        )
+    copies.append(
+        pltpu.make_async_copy(
+            other_weights, weights_at.at[pl.ds(theirs, half)], semaphores.at[3]
+        )
+    )
+    copies[3].start()
+    for copy in copies:
+        copy.wait()
 
 
 def shards(
@@ -675,7 +675,7 @@
     )
 
     half = 2 * width
-    grad_z_one, sent_half, bias_rows, mean_one, h_one, pulled, cotangent_in = run(
+    grad_z_one, sent_half, bias_rows, mean_one, h_one, pulled, cotangent_in, early_counts = run(
         middle,
         "middle",
         [
@@ -686,9 +686,10 @@
             rows_bf16,
             rows_bf16,
             rows_bf16,
+            pltpu.VMEM((early, slots), BF16),
         ],
         smem=[core.reshape(1)],
-        hbm=[cotangent, backward],
+        hbm=[cotangent, backward, early_counts],
         vmem=[
             forward,
             returned,
@@ -703,17 +704,25 @@
         ],
         scratch=[
             rows_f32,
-            pltpu.SemaphoreType.DMA((2,)),
+            pltpu.SemaphoreType.DMA((3,)),
             rows_f32,
         ],
         flops=20 * node_dev * width * width,
     )
     other_half = lax.ppermute(sent_half, AXES, swap)
-    message_one, picked, own_half = run(
+    message_one, picked, own_half, late_counts, mirror_rows = run(
         messages,
         "messages",
-        [rows_bf16, pltpu.VMEM((mirrors, width), F32), pltpu.VMEM((half, width), F32)],
+        [
+            rows_bf16,
+            pltpu.VMEM((mirrors, width), F32),
+            pltpu.VMEM((half, width), F32),
+            pltpu.VMEM((node_dev - early, slots), BF16),
+            pltpu.VMEM((mirrors, slots), BF16),
+        ],
         smem=[core.reshape(1)],
+        hbm=[late_counts, mirror_rows],
+        scratch=[pltpu.SemaphoreType.DMA((2,))],
         vmem=[
             in_count,
             grad_z_one,
@@ -733,24 +742,10 @@
     (payload,) = run(
         join_first,
         "join_first",
-        [pltpu.HBM(payload_shape, BF16)],
+        [pltpu.VMEM(payload_shape, BF16)],
         vmem=[own_half, other_half, picked, bias_rows],
-        scratch=[pltpu.VMEM(payload_shape, BF16), pltpu.SemaphoreType.DMA],
     )
     received = exchange(payload)
-    mirror_back, local_grad, mirror_rows = run(
-        local_back,
-        "local_back",
-        [
-            pltpu.VMEM((mirrors, width), F32),
-            pltpu.VMEM((node_dev, width), F32),
-            pltpu.VMEM((mirrors, slots), BF16),
-        ],
-        hbm=[early_counts, late_counts, mirror_rows],
-        vmem=[message_one, grad_z_one, w_self_one],
-        scratch=[pltpu.VMEM((node_dev, slots), BF16), pltpu.SemaphoreType.DMA((3,))],
-        flops=2 * node_dev * (slots + width) * width,
-    )
     norm_factor = float(node_dev * devices) ** -0.5
     payload, mirrored, bias_total = run(
         functools.partial(join_second, norm_factor),
@@ -760,36 +755,39 @@
             pltpu.VMEM((mirrors, width), BF16),
             pltpu.VMEM((1, width), F32),
         ],
-        vmem=[received, mirror_back, mirror_rows],
+        vmem=[received, message_one, early_counts, late_counts, mirror_rows],
     )
     received = exchange(payload)
     other = lax.ppermute(received, AXES, swap)
-    grad_features, grad_weights, grad_bias = run(
+    grad_features, own_weights = run(
         finish,
         "finish",
+        [rows_bf16, pltpu.VMEM((half, width), F32)],
+        vmem=[
+            received,
+            mirrored,
+            picking,
+            early_counts,
+            late_counts,
+            mirror_rows,
+            message_one,
+            grad_z_one,
+            w_self_one,
+        ],
+        flops=2 * node_dev * (slots + mirrors + width) * width,
+        moved=4 * node_dev * slots,
+    )
+    grad_features, grad_weights, grad_bias = run(
+        write_out,
+        "write_out",
         [
             pltpu.HBM((node_dev, width), BF16),
             pltpu.HBM((2 * half, width), F32),
             pltpu.HBM((1, width), F32),
         ],
         smem=[core.reshape(1)],
-        vmem=[received, mirrored, picking, mirror_rows, local_grad, bias_total],
-        scratch=[
-            pltpu.VMEM((node_dev, width), BF16),
-            pltpu.VMEM((half, width), F32),
-            pltpu.SemaphoreType.DMA((3,)),
-        ],
-        flops=6 * node_dev * mirrors * width,
-    )
-    (grad_weights,) = run(
-        finish_other,
-        "finish_other",
-        [pltpu.HBM((2 * half, width), F32)],
-        smem=[core.reshape(1)],
-        hbm=[grad_weights],
-        vmem=[other],
-        scratch=[pltpu.VMEM((half, width), F32), pltpu.SemaphoreType.DMA],
-        aliases={1: 0},
+        vmem=[other, grad_features, own_weights, bias_total],
+        scratch=[pltpu.VMEM((half, width), F32), pltpu.SemaphoreType.DMA((4,))],
     )
     return (
         grad_features,

time: 68.2 us -> 67.5 us (0.990)
  blocking collectives: 14.2 us -> 28.5 us
  waiting for transfers between devices: 19.3 us -> 9.38 us
  starting transfers between devices: 12.8 us -> 10.2 us
  Pallas kernels: 19.8 us -> 17.4 us
    all_to_all x1 -> x2, blocking collectives: 14.2 us -> 28.5 us  [exchange(): return lax.all_to_all(rows, AXES, split_axis=0, concat_axis=0, tiled=True)]
    all_to_all x3 -> x2, waiting for transfers between devices: 18.9 us -> 8.92 us  [exchange(): return lax.all_to_all(rows, AXES, split_axis=0, concat_axis=0, tiled=True)]
    all_to_all x3 -> x2, starting transfers between devices: 12.5 us -> 9.88 us  [exchange(): return lax.all_to_all(rows, AXES, split_axis=0, concat_axis=0, tiled=True)]
    pallas_call x11 -> x10, Pallas kernels: 19.8 us -> 17.4 us  [run(): pl.pallas_call(kernel, out_shape=tuple(outs), in_specs=[pl.BlockSpec(memo...]
  transfers between devices with their start and end apart: 5 -> 4, of which waited for: 5 -> 3; matrix products, arithmetic and copies ran while one was open for 0% -> 0% of each run, Pallas kernels for 18% -> 14%
where the time goes in v8:
time: 67.5 us; the launch traced here: 67 us
  blocking collectives  28.5 us (42%)
  Pallas kernels  17.4 us (26%)
  starting transfers between devices  10.2 us (15%)
  waiting for transfers between devices  9.38 us (14%)
  between operations  1.48 us (2%)
    all_to_all x2, blocking collectives, exchange(): return lax.all_to_all(rows, AXES, split_axis=0, concat_axis=0, tiled=True)  28.5 us
    pallas_call x10, Pallas kernels, run(): pl.pallas_call(kernel, out_shape=tuple(outs), in_specs=[pl.BlockSpec(memo...  17.4 us
    all_to_all x2, starting transfers between devices, exchange(): return lax.all_to_all(rows, AXES, split_axis=0, concat_axis=0, tiled=True)  9.88 us
    all_to_all x2, waiting for transfers between devices, exchange(): return lax.all_to_all(rows, AXES, split_axis=0, concat_axis=0, tiled=True)  8.92 us
  transfers between devices with their start and end apart: 4, of which 3 were waited for; matrix products, arithmetic and copies ran while one was open for 0% of the time, Pallas kernels for 14%

profile of v8, /device:TPU:0, one launch (start us, length us, event | category | flops | bytes accessed | tf_op | source)
XLA Modules:
  0.0 67.0 jit_solution(3278983283080415579)
XLA Ops:
  0.6 2.4 %pick_rows.1 = (bf16[32,4,512]{2,1,0:T(4,128)(2,1)}, bf16[1024,256]{1,0:T(8,128)(2,1)S(1)}, bf16[128,1024]{1,0:T(8,128)(2,1)S(1)}, s32[16,128]{1,0:T(8,128)S(1)}, s32[16,128]{1,0:T(8,128)S(1)}) custom-call(bf16[1024,256]{1,0:T(8,128)(2,1)} %features_at.5, bf16[1024,256]{1,0:T(8,128)(2,1)} %cotangent_at.3, s32[8,128]{1,0:T(8,128)} %bitcast.10, ...), custom_call_target="tpu_custom_call" | custom-call | flops 134217728 | tf_op jit(solution)/shard_map/pick_rows/pallas_call | solution.py:42
  3.1 7.3 %all-to-all-start = ((bf16[32,4,512]{2,1,0:T(4,128)(2,1)}), bf16[32,4,512]{2,1,0:T(4,128)(2,1)S(1)}, u32[]{:S(2)}, u32[]{:S(2)}) async-start(bf16[32,4,512]{2,1,0:T(4,128)(2,1)} %get-tuple-element.43), calls=%async_computation | async-start | bytes 262144 | tf_op jit(solution)/shard_map/all_to_all | solution.py:36
  11.0 2.9 %count_edges.1 = (bf16[512,1152]{1,0:T(8,128)(2,1)}, bf16[1024,256]{1,0:T(8,128)(2,1)}, bf16[128,1152]{1,0:T(8,128)(2,1)S(1)}, f32[128,512]{1,0:T(8,128)S(1)}) custom-call(s32[1]{0:T(128)S(6)} %copy.15.edge_count, bf16[1024,256]{1,0:T(8,128)(2,1)} %features_at.5, bf16[1024,256]{1,0:T(8,128)(2,1)S(1)} %get-tuple-element.38.scaled, ...), custom_call_target="tpu_custom_call" | custom-call | flops 3623878656 | tf_op jit(solution)/shard_map/count_edges/pallas_call | solution.py:42
  14.0 4.6 %all-to-all-done = bf16[32,4,512]{2,1,0:T(4,128)(2,1)S(1)} async-done(((bf16[32,4,512]{2,1,0:T(4,128)(2,1)}), bf16[32,4,512]{2,1,0:T(4,128)(2,1)S(1)}, u32[]{:S(2)}, u32[]{:S(2)}) %all-to-all-start) | async-done | bytes 131104 | tf_op jit(solution)/shard_map/all_to_all | solution.py:36
  18.6 0.9 %mirror_sums.1 = bf16[32,4,512]{2,1,0:T(4,128)(2,1)} custom-call(f32[128,512]{1,0:T(8,128)S(1)} %get-tuple-element.49.partial_in, bf16[128,1152]{1,0:T(8,128)(2,1)S(1)} %get-tuple-element.44.mirror_rows, bf16[128,512]{1,0:T(8,128)(2,1)S(1)} %reshape.39.mirrored), custom_call_target="tpu_custom_call" | custom-call | flops 16777216 | tf_op jit(solution)/shard_map/mirror_sums/pallas_call | solution.py:42
  19.5 2.6 %all-to-all-start.1 = ((bf16[32,4,512]{2,1,0:T(4,128)(2,1)}), bf16[32,4,512]{2,1,0:T(4,128)(2,1)S(1)}, u32[]{:S(2)}, u32[]{:S(2)}) async-start(bf16[32,4,512]{2,1,0:T(4,128)(2,1)} %mirror_sums.1), calls=%async_computation.1 | async-start | bytes 262144 | tf_op jit(solution)/shard_map/all_to_all | solution.py:36
  22.1 0.0 copy-start
  22.1 0.0 copy-start.1
  22.1 0.0 copy-start.2
  22.1 0.0 copy-start.3
  22.2 0.0 copy-start.4
  22.2 0.0 copy-start.5
  22.2 3.9 %local_sums.1 = (f32[1024,256]{1,0:T(8,128)S(1)}, bf16[1024,256]{1,0:T(8,128)(2,1)S(1)}, f32[1024,256]{1,0:T(8,128)}, bf16[128,1152]{1,0:T(8,128)(2,1)}, bf16[512,1152]{1,0:T(8,128)(2,1)}) custom-call(s32[1]{0:T(128)S(6)} %copy.15.edge_count, bf16[512,1152]{1,0:T(8,128)(2,1)} %get-tuple-element.41.early_at, bf16[1024,256]{1,0:T(8,128)(2,1)} %features_at.5, ...), custom_call_target="tpu_custom_call" | custom-call | flops 3623878656 | tf_op jit(solution)/shard_map/local_sums/pallas_call | solution.py:42
  26.1 4.3 %all-to-all-done.1 = bf16[32,4,512]{2,1,0:T(4,128)(2,1)S(1)} async-done(((bf16[32,4,512]{2,1,0:T(4,128)(2,1)}), bf16[32,4,512]{2,1,0:T(4,128)(2,1)S(1)}, u32[]{:S(2)}, u32[]{:S(2)}) %all-to-all-start.1) | async-done | bytes 131104 | tf_op jit(solution)/shard_map/all_to_all | solution.py:36
  30.4 3.1 %middle.1 = (bf16[1024,256]{1,0:T(8,128)(2,1)S(1)}, bf16[512,256]{1,0:T(8,128)(2,1)S(1)}, f32[4,128]{1,0:T(4,128)S(1)}, bf16[1024,256]{1,0:T(8,128)(2,1)S(1)}, b...) custom-call(s32[1]{0:T(128)} %bitcast.core, ...), custom_call_target="tpu_custom_call" | custom-call | flops 1342177280 | tf_op jit(solution)/shard_map/middle/pallas_call | solution.py:42
  33.6 0.3 collective-permute-start
  33.9 1.3 %messages.1 = (bf16[1024,256]{1,0:T(8,128)(2,1)S(1)}, f32[128,256]{1,0:T(8,128)S(1)}, f32[512,256]{1,0:T(8,128)S(1)}, bf16[512,1152]{1,0:T(8,128)(2,1)S(1)}, bf16[128,1152]{1,0:T(8,128)(2,1)S(1)}) custom-call(s32[1]{0:T(128)} %bitcast.core, bf16[512,1152]{1,0:T(8,128)(2,1)} %get-tuple-element.45.late_at, bf16[128,1152]{1,0:T(8,128)(2,1)} %get-tuple-element.46.mirror_at, ...), custom_call_target="tpu_custom_call" | custom-call | flops 402653184 | tf_op jit(solution)/shard_map/messages/pallas_call | solution.py:42
  35.2 0.1 join_first.1
  35.3 14.3 %all_to_all.20.received = bf16[32,4,1408]{2,1,0:T(4,128)(2,1)S(1)} all-to-all(bf16[32,4,1408]{2,1,0:T(4,128)(2,1)S(1)} %join_first.1), channel_id=1, replica_groups=mesh['dom'=8,'sub'=4] {'dom','sub'}, dimensions={0} | all-to-all | bytes 720896 | tf_op jit(solution)/shard_map/all_to_all | solution.py:36
  49.6 0.4 join_second.1
  50.0 14.2 %all_to_all.21.received = bf16[32,4,1280]{2,1,0:T(4,128)(2,1)S(1)} all-to-all(bf16[32,4,1280]{2,1,0:T(4,128)(2,1)S(1)} %get-tuple-element.65), channel_id=1, replica_groups=mesh['dom'=8,'sub'=4] {'dom','sub'}, dimensions={0} | all-to-all | bytes 655360 | tf_op jit(solution)/shard_map/all_to_all | solution.py:36
  64.2 1.2 %finish.1 = (bf16[1024,256]{1,0:T(8,128)(2,1)S(1)}, f32[512,256]{1,0:T(8,128)S(1)}) custom-call(bf16[32,4,1280]{2,1,0:T(4,128)(2,1)S(1)} %all_to_all.21.received, bf16[128,256]{1,0:T(8,128)(2,1)S(1)} %get-tuple-element.66.mirrored, bf16[128,1024]{1,0:T(8,128)(2,1)S(1)} %get-tuple-element.50.picking, bf16[512,1152]{1,0:T(8,128)(2,1)S(1)} %get-tuple-element.62.early_counts, ...), custom_call_target="tpu_custom_call" | custom-call | flops 805306368 | bytes 4718592 | tf_op jit(solution)/shard_map/finish/pallas_call | solution.py:42
  65.4 0.5 collective-permute-done.1.other
  65.9 1.2 %write_out.1 = (bf16[1024,256]{1,0:T(8,128)(2,1)}, f32[1024,256]{1,0:T(8,128)}, f32[1,256]{1,0:T(1,128)}) custom-call(s32[1]{0:T(128)} %bitcast.core, bf16[32,4,1280]{2,1,0:T(4,128)(2,1)S(1)} %collective-permute-done.1.other, bf16[1024,256]{1,0:T(8,128)(2,1)S(1)} %get-tuple-element.67.grad_features, f32[512,256]{1,0:T(8,128)S(1)} %get-tuple-element.68.own_weights, ...), custom_call_target="tpu_custom_call" | custom-call | tf_op jit(solution)/shard_map/write_out/pallas_call | solution.py:42
  (10 shorter events, 0.1 us)
Async XLA Ops:
  3.1 15.5 %all-to-all-start = ((bf16[32,4,512]{2,1,0:T(4,128)(2,1)}), bf16[32,4,512]{2,1,0:T(4,128)(2,1)S(1)}, u32[]{:S(2)}, u32[]{:S(2)}) async-start(bf16[32,4,512]{2,1,0:T(4,128)(2,1)} %get-tuple-element.43), calls=%async_computation | async-start | bytes 262144 | tf_op jit(solution)/shard_map/all_to_all | solution.py:36
  19.5 10.8 %all-to-all-start.1 = ((bf16[32,4,512]{2,1,0:T(4,128)(2,1)}), bf16[32,4,512]{2,1,0:T(4,128)(2,1)S(1)}, u32[]{:S(2)}, u32[]{:S(2)}) async-start(bf16[32,4,512]{2,1,0:T(4,128)(2,1)} %mirror_sums.1), calls=%async_computation.1 | async-start | bytes 262144 | tf_op jit(solution)/shard_map/all_to_all | solution.py:36
  22.1 8.3 %copy-start = (bf16[256,256]{1,0:T(8,128)(2,1)S(1)}, bf16[256,256]{1,0:T(8,128)(2,1)}, u32[]{:S(2)}) copy-start(bf16[256,256]{1,0:T(8,128)(2,1)} %w_nbr_one.3) | copy-start | bytes 393220
  22.1 8.3 %copy-start.1 = (bf16[256,256]{1,0:T(8,128)(2,1)S(1)}, bf16[256,256]{1,0:T(8,128)(2,1)}, u32[]{:S(2)}) copy-start(bf16[256,256]{1,0:T(8,128)(2,1)} %w_self_one.3) | copy-start | bytes 393220
  22.1 8.3 %copy-start.2 = (bf16[256,256]{1,0:T(8,128)(2,1)S(1)}, bf16[256,256]{1,0:T(8,128)(2,1)}, u32[]{:S(2)}) copy-start(bf16[256,256]{1,0:T(8,128)(2,1)} %w_nbr_two.1) | copy-start | bytes 393220
  22.1 8.3 %copy-start.3 = (bf16[256,256]{1,0:T(8,128)(2,1)S(1)}, bf16[256,256]{1,0:T(8,128)(2,1)}, u32[]{:S(2)}) copy-start(bf16[256,256]{1,0:T(8,128)(2,1)} %w_self_two.1) | copy-start | bytes 393220
  22.2 8.3 %copy-start.4 = (s32[1024]{0:T(1024)S(1)}, s32[1024]{0:T(1024)}, u32[]{:S(2)}) copy-start(s32[1024]{0:T(1024)} %param.19) | copy-start | bytes 12292
  22.2 8.3 %copy-start.5 = (f32[256]{0:T(256)S(1)}, f32[256]{0:T(256)}, u32[]{:S(2)}) copy-start(f32[256]{0:T(256)} %param.16) | copy-start | bytes 3076
  33.6 1.6 %collective-permute-start = (bf16[512,256]{1,0:T(8,128)(2,1)S(1)}, bf16[512,256]{1,0:T(8,128)(2,1)S(1)}, u32[]{:S(2)}, u32[]{:S(2)}) collective-permute-start(bf16[512,256]{1,0:T(8,128)(2,1)S(1)} %get-tuple-element.58), channel_id=1, source_target_pairs={{0,1},{1,0},{2,3},{3,2},{4,5},{5,4},{6,7},{7,6},{8,9},{9,8},{10,11... | collective-permute-start | bytes 786440 | tf_op jit(solution)/shard_map/ppermute | solution.py:712
  64.2 1.6 %collective-permute-start.1 = (bf16[32,4,1280]{2,1,0:T(4,128)(2,1)S(1)}, bf16[32,4,1280]{2,1,0:T(4,128)(2,1)S(1)}, u32[]{:S(2)}, u32[]{:S(2)}) collective-permute-start(bf16[32,4,1280]{2,1,0:T(4,128)(2,1)S(1)} %all_to_all.21.received), channel_id=1, source_target_pairs={{0,1},{1,0},{2,3},{3,2},{4,5},{5,4},{6,7},{7,6},{8,9},{9,8},{10,11... | collective-permute-start | bytes 983048 | tf_op jit(solution)/shard_map/ppermute | solution.py:761

commit v9 on v8

--- a/solution.py
+++ b/solution.py
@@ -320,7 +320,6 @@
     core,
     cotangent_at,
     backward_at,
-    early_at,
     forward,
     returned,
     picking,
@@ -338,7 +337,6 @@
     h_one,
     pulled,
     cotangent,
-    early_counts,
     backward,
     semaphores,
     slope,
@@ -363,8 +361,6 @@
         slope[rows, :] = sigmoid * (1.0 + z_one * (1.0 - sigmoid))
     for copy in copies:
         copy.wait()
-    early_copy = pltpu.make_async_copy(early_at, early_counts, semaphores.at[2])
-    early_copy.start()
     bias_total = jnp.zeros((1, width), F32)
     for rows in blocks:
         pull = (backward[rows, :] + tdot(picking[:, rows], returned[:, width:])).astype(BF16)
@@ -393,13 +389,9 @@
         sent_half[:width, :] = tdot(features[...], grad_z[...]).astype(BF16)
         sent_half[width:, :] = tdot(mean_one[...], grad_z[...]).astype(BF16)
 
-    early_copy.wait()
-
 
 def messages(
     core,
-    late_at,
-    mirror_at,
     in_count,
     grad_z,
     w_nbr_one,
@@ -412,12 +404,8 @@
     message_one,
     picked,
     own_half,
-    late_counts,
-    mirror_rows,
-    semaphores,
 ):
     node_dev, width = grad_z.shape
-    copies = start_all([late_at, mirror_at], [late_counts, mirror_rows], semaphores)
     columns = inverse_columns(in_count)
     for index, start in enumerate(range(0, node_dev, BLOCK)):
         rows = pl.ds(start, BLOCK)
@@ -435,9 +423,6 @@
     def _():
         own_half[:width, :] = tdot(h_one[...], cotangent[...])
         own_half[width:, :] = tdot(h_one[...], pulled[...])
-
-    for copy in copies:
-        copy.wait()
 
 
 def join_first(own_half, other_half, picked, bias_rows, payload):
@@ -675,7 +660,7 @@
     )
 
     half = 2 * width
-    grad_z_one, sent_half, bias_rows, mean_one, h_one, pulled, cotangent_in, early_counts = run(
+    grad_z_one, sent_half, bias_rows, mean_one, h_one, pulled, cotangent_in = run(
         middle,
         "middle",
         [
@@ -686,10 +671,9 @@
             rows_bf16,
             rows_bf16,
             rows_bf16,
-            pltpu.VMEM((early, slots), BF16),
         ],
         smem=[core.reshape(1)],
-        hbm=[cotangent, backward, early_counts],
+        hbm=[cotangent, backward],
         vmem=[
             forward,
             returned,
@@ -704,25 +688,21 @@
         ],
         scratch=[
             rows_f32,
-            pltpu.SemaphoreType.DMA((3,)),
+            pltpu.SemaphoreType.DMA((2,)),
             rows_f32,
         ],
         flops=20 * node_dev * width * width,
     )
     other_half = lax.ppermute(sent_half, AXES, swap)
-    message_one, picked, own_half, late_counts, mirror_rows = run(
+    message_one, picked, own_half = run(
         messages,
         "messages",
         [
             rows_bf16,
             pltpu.VMEM((mirrors, width), F32),
             pltpu.VMEM((half, width), F32),
-            pltpu.VMEM((node_dev - early, slots), BF16),
-            pltpu.VMEM((mirrors, slots), BF16),
         ],
         smem=[core.reshape(1)],
-        hbm=[late_counts, mirror_rows],
-        scratch=[pltpu.SemaphoreType.DMA((2,))],
         vmem=[
             in_count,
             grad_z_one,

time: 67.5 us -> 67.1 us (level)
  Pallas kernels: 17.4 us -> 16.6 us
    pallas_call x10, Pallas kernels: 17.4 us -> 16.6 us  [run(): pl.pallas_call(kernel, out_shape=tuple(outs), in_specs=[pl.BlockSpec(memo...]
  transfers between devices with their start and end apart: 4 -> 4, of which waited for: 3 -> 4; matrix products, arithmetic and copies ran while one was open for 0% -> 0% of each run, Pallas kernels for 14% -> 14%
where the time goes in v9:
time: 67.1 us; the launch traced here: 66.7 us
  blocking collectives  28.7 us (43%)
  Pallas kernels  16.6 us (25%)
  starting transfers between devices  10.2 us (15%)
  waiting for transfers between devices  9.61 us (14%)
  between operations  1.49 us (2%)
    all_to_all x2, blocking collectives, exchange(): return lax.all_to_all(rows, AXES, split_axis=0, concat_axis=0, tiled=True)  28.7 us
    pallas_call x10, Pallas kernels, run(): pl.pallas_call(kernel, out_shape=tuple(outs), in_specs=[pl.BlockSpec(memo...  16.6 us
    all_to_all x2, starting transfers between devices, exchange(): return lax.all_to_all(rows, AXES, split_axis=0, concat_axis=0, tiled=True)  9.89 us
    all_to_all x2, waiting for transfers between devices, exchange(): return lax.all_to_all(rows, AXES, split_axis=0, concat_axis=0, tiled=True)  8.9 us
  transfers between devices with their start and end apart: 4, of which 4 were waited for; matrix products, arithmetic and copies ran while one was open for 0% of the time, Pallas kernels for 14%

profile of v9, /device:TPU:0, one launch (start us, length us, event | category | flops | bytes accessed | tf_op | source)
XLA Modules:
  0.0 66.7 jit_solution(12789153501943827856)
XLA Ops:
  0.6 2.4 %pick_rows.1 = (bf16[32,4,512]{2,1,0:T(4,128)(2,1)}, bf16[1024,256]{1,0:T(8,128)(2,1)S(1)}, bf16[128,1024]{1,0:T(8,128)(2,1)S(1)}, s32[16,128]{1,0:T(8,128)S(1)}, s32[16,128]{1,0:T(8,128)S(1)}) custom-call(bf16[1024,256]{1,0:T(8,128)(2,1)} %features_at.5, bf16[1024,256]{1,0:T(8,128)(2,1)} %cotangent_at.3, s32[8,128]{1,0:T(8,128)} %bitcast.10, ...), custom_call_target="tpu_custom_call" | custom-call | flops 134217728 | tf_op jit(solution)/shard_map/pick_rows/pallas_call | solution.py:42
  3.1 7.3 %all-to-all-start = ((bf16[32,4,512]{2,1,0:T(4,128)(2,1)}), bf16[32,4,512]{2,1,0:T(4,128)(2,1)S(1)}, u32[]{:S(2)}, u32[]{:S(2)}) async-start(bf16[32,4,512]{2,1,0:T(4,128)(2,1)} %get-tuple-element.40), calls=%async_computation | async-start | bytes 262144 | tf_op jit(solution)/shard_map/all_to_all | solution.py:36
  11.0 2.9 %count_edges.1 = (bf16[512,1152]{1,0:T(8,128)(2,1)}, bf16[1024,256]{1,0:T(8,128)(2,1)}, bf16[128,1152]{1,0:T(8,128)(2,1)S(1)}, f32[128,512]{1,0:T(8,128)S(1)}) custom-call(s32[1]{0:T(128)S(6)} %copy.15.edge_count, bf16[1024,256]{1,0:T(8,128)(2,1)} %features_at.5, bf16[1024,256]{1,0:T(8,128)(2,1)S(1)} %get-tuple-element.35.scaled, ...), custom_call_target="tpu_custom_call" | custom-call | flops 3623878656 | tf_op jit(solution)/shard_map/count_edges/pallas_call | solution.py:42
  14.0 4.6 %all-to-all-done = bf16[32,4,512]{2,1,0:T(4,128)(2,1)S(1)} async-done(((bf16[32,4,512]{2,1,0:T(4,128)(2,1)}), bf16[32,4,512]{2,1,0:T(4,128)(2,1)S(1)}, u32[]{:S(2)}, u32[]{:S(2)}) %all-to-all-start) | async-done | bytes 131104 | tf_op jit(solution)/shard_map/all_to_all | solution.py:36
  18.6 0.9 %mirror_sums.1 = bf16[32,4,512]{2,1,0:T(4,128)(2,1)} custom-call(f32[128,512]{1,0:T(8,128)S(1)} %get-tuple-element.44.partial_in, bf16[128,1152]{1,0:T(8,128)(2,1)S(1)} %get-tuple-element.41.mirror_rows, bf16[128,512]{1,0:T(8,128)(2,1)S(1)} %reshape.39.mirrored), custom_call_target="tpu_custom_call" | custom-call | flops 16777216 | tf_op jit(solution)/shard_map/mirror_sums/pallas_call | solution.py:42
  19.5 2.6 %all-to-all-start.1 = ((bf16[32,4,512]{2,1,0:T(4,128)(2,1)}), bf16[32,4,512]{2,1,0:T(4,128)(2,1)S(1)}, u32[]{:S(2)}, u32[]{:S(2)}) async-start(bf16[32,4,512]{2,1,0:T(4,128)(2,1)} %mirror_sums.1), calls=%async_computation.1 | async-start | bytes 262144 | tf_op jit(solution)/shard_map/all_to_all | solution.py:36
  22.1 0.0 copy-start.3
  22.1 0.0 copy-start.4
  22.2 0.0 copy-start.5
  22.2 0.0 copy-start.6
  22.2 0.0 copy-start.7
  22.2 3.9 %local_sums.1 = (f32[1024,256]{1,0:T(8,128)S(1)}, bf16[1024,256]{1,0:T(8,128)(2,1)S(1)}, f32[1024,256]{1,0:T(8,128)}, bf16[128,1152]{1,0:T(8,128)(2,1)}, bf16[512,1152]{1,0:T(8,128)(2,1)}) custom-call(s32[1]{0:T(128)S(6)} %copy.15.edge_count, bf16[512,1152]{1,0:T(8,128)(2,1)} %get-tuple-element.38.early_at.early_counts, bf16[1024,256]{1,0:T(8,128)(2,1)} %features_at.5, ...), custom_call_target="tpu_custom_call" | custom-call | flops 3623878656 | tf_op jit(solution)/shard_map/local_sums/pallas_call | solution.py:42
  26.1 4.3 %all-to-all-done.1 = bf16[32,4,512]{2,1,0:T(4,128)(2,1)S(1)} async-done(((bf16[32,4,512]{2,1,0:T(4,128)(2,1)}), bf16[32,4,512]{2,1,0:T(4,128)(2,1)S(1)}, u32[]{:S(2)}, u32[]{:S(2)}) %all-to-all-start.1) | async-done | bytes 131104 | tf_op jit(solution)/shard_map/all_to_all | solution.py:36
  30.5 2.7 %middle.1 = (bf16[1024,256]{1,0:T(8,128)(2,1)S(1)}, bf16[512,256]{1,0:T(8,128)(2,1)S(1)}, f32[4,128]{1,0:T(4,128)S(1)}, bf16[1024,256]{1,0:T(8,128)(2,1)S(1)}, b...) custom-call(s32[1]{0:T(128)} %bitcast.core, ...), custom_call_target="tpu_custom_call" | custom-call | flops 1342177280 | tf_op jit(solution)/shard_map/middle/pallas_call | solution.py:42
  33.1 0.3 collective-permute-start
  33.4 1.0 %messages.1 = (bf16[1024,256]{1,0:T(8,128)(2,1)S(1)}, f32[128,256]{1,0:T(8,128)S(1)}, f32[512,256]{1,0:T(8,128)S(1)}) custom-call(s32[1]{0:T(128)} %bitcast.core, s32[8,128]{1,0:T(8,128)S(1)} %bitcast.12, bf16[1024,256]{1,0:T(8,128)(2,1)S(1)} %get-tuple-element.47.grad_z, bf16[256,256]{1,0:T(8,128)(2,1)S(1)} %copy-done.3, ...), custom_call_target="tpu_custom_call" | custom-call | flops 402653184 | tf_op jit(solution)/shard_map/messages/pallas_call | solution.py:42
  34.5 0.2 collective-permute-done.other_half
  34.7 0.1 join_first.1
  34.8 14.4 %all_to_all.20.received = bf16[32,4,1408]{2,1,0:T(4,128)(2,1)S(1)} all-to-all(bf16[32,4,1408]{2,1,0:T(4,128)(2,1)S(1)} %join_first.1), channel_id=1, replica_groups=mesh['dom'=8,'sub'=4] {'dom','sub'}, dimensions={0} | all-to-all | bytes 720896 | tf_op jit(solution)/shard_map/all_to_all | solution.py:36
  49.3 0.4 join_second.1
  49.7 14.2 %all_to_all.21.received = bf16[32,4,1280]{2,1,0:T(4,128)(2,1)S(1)} all-to-all(bf16[32,4,1280]{2,1,0:T(4,128)(2,1)S(1)} %get-tuple-element.59), channel_id=1, replica_groups=mesh['dom'=8,'sub'=4] {'dom','sub'}, dimensions={0} | all-to-all | bytes 655360 | tf_op jit(solution)/shard_map/all_to_all | solution.py:36
  63.9 1.2 %finish.1 = (bf16[1024,256]{1,0:T(8,128)(2,1)S(1)}, f32[512,256]{1,0:T(8,128)S(1)}) custom-call(bf16[32,4,1280]{2,1,0:T(4,128)(2,1)S(1)} %all_to_all.21.received, bf16[128,256]{1,0:T(8,128)(2,1)S(1)} %get-tuple-element.60.mirrored, bf16[128,1024]{1,0:T(8,128)(2,1)S(1)} %get-tuple-element.45.picking, bf16[512,1152]{1,0:T(8,128)(2,1)S(1)} %copy-done, ...), custom_call_target="tpu_custom_call" | custom-call | flops 805306368 | bytes 4718592 | tf_op jit(solution)/shard_map/finish/pallas_call | solution.py:42
  65.1 0.5 collective-permute-done.1.other
  65.5 1.2 %write_out.1 = (bf16[1024,256]{1,0:T(8,128)(2,1)}, f32[1024,256]{1,0:T(8,128)}, f32[1,256]{1,0:T(1,128)}) custom-call(s32[1]{0:T(128)} %bitcast.core, bf16[32,4,1280]{2,1,0:T(4,128)(2,1)S(1)} %collective-permute-done.1.other, bf16[1024,256]{1,0:T(8,128)(2,1)S(1)} %get-tuple-element.61.grad_features, f32[512,256]{1,0:T(8,128)S(1)} %get-tuple-element.62.own_weights, ...), custom_call_target="tpu_custom_call" | custom-call | tf_op jit(solution)/shard_map/write_out/pallas_call | solution.py:42
  (16 shorter events, 0.1 us)
Async XLA Ops:
  3.1 15.5 %all-to-all-start = ((bf16[32,4,512]{2,1,0:T(4,128)(2,1)}), bf16[32,4,512]{2,1,0:T(4,128)(2,1)S(1)}, u32[]{:S(2)}, u32[]{:S(2)}) async-start(bf16[32,4,512]{2,1,0:T(4,128)(2,1)} %get-tuple-element.40), calls=%async_computation | async-start | bytes 262144 | tf_op jit(solution)/shard_map/all_to_all | solution.py:36
  19.5 10.8 %all-to-all-start.1 = ((bf16[32,4,512]{2,1,0:T(4,128)(2,1)}), bf16[32,4,512]{2,1,0:T(4,128)(2,1)S(1)}, u32[]{:S(2)}, u32[]{:S(2)}) async-start(bf16[32,4,512]{2,1,0:T(4,128)(2,1)} %mirror_sums.1), calls=%async_computation.1 | async-start | bytes 262144 | tf_op jit(solution)/shard_map/all_to_all | solution.py:36
  22.1 8.3 %copy-start.3 = (bf16[256,256]{1,0:T(8,128)(2,1)S(1)}, bf16[256,256]{1,0:T(8,128)(2,1)}, u32[]{:S(2)}) copy-start(bf16[256,256]{1,0:T(8,128)(2,1)} %w_nbr_one.3) | copy-start | bytes 393220
  22.1 8.3 %copy-start.4 = (bf16[256,256]{1,0:T(8,128)(2,1)S(1)}, bf16[256,256]{1,0:T(8,128)(2,1)}, u32[]{:S(2)}) copy-start(bf16[256,256]{1,0:T(8,128)(2,1)} %w_self_one.3) | copy-start | bytes 393220
  22.2 8.3 %copy-start.5 = (s32[1024]{0:T(1024)S(1)}, s32[1024]{0:T(1024)}, u32[]{:S(2)}) copy-start(s32[1024]{0:T(1024)} %param.19) | copy-start | bytes 12292
  22.2 8.3 %copy-start.6 = (bf16[256,256]{1,0:T(8,128)(2,1)S(1)}, bf16[256,256]{1,0:T(8,128)(2,1)}, u32[]{:S(2)}) copy-start(bf16[256,256]{1,0:T(8,128)(2,1)} %w_nbr_two.1) | copy-start | bytes 393220
  22.2 8.3 %copy-start.7 = (bf16[256,256]{1,0:T(8,128)(2,1)S(1)}, bf16[256,256]{1,0:T(8,128)(2,1)}, u32[]{:S(2)}) copy-start(bf16[256,256]{1,0:T(8,128)(2,1)} %w_self_two.1) | copy-start | bytes 393220
  22.2 8.3 %copy-start.8 = (f32[256]{0:T(256)S(1)}, f32[256]{0:T(256)}, u32[]{:S(2)}) copy-start(f32[256]{0:T(256)} %param.16) | copy-start | bytes 3076
  33.1 1.6 %collective-permute-start = (bf16[512,256]{1,0:T(8,128)(2,1)S(1)}, bf16[512,256]{1,0:T(8,128)(2,1)S(1)}, u32[]{:S(2)}, u32[]{:S(2)}) collective-permute-start(bf16[512,256]{1,0:T(8,128)(2,1)S(1)} %get-tuple-element.53), channel_id=1, source_target_pairs={{0,1},{1,0},{2,3},{3,2},{4,5},{5,4},{6,7},{7,6},{8,9},{9,8},{10,11... | collective-permute-start | bytes 786440 | tf_op jit(solution)/shard_map/ppermute | solution.py:696
  33.4 15.9 %copy-start.1 = (bf16[512,1152]{1,0:T(8,128)(2,1)S(1)}, bf16[512,1152]{1,0:T(8,128)(2,1)}, u32[]{:S(2)}) copy-start(bf16[512,1152]{1,0:T(8,128)(2,1)} %get-tuple-element.57.late_counts) | copy-start | bytes 3538948
  34.5 14.8 %copy-start = (bf16[512,1152]{1,0:T(8,128)(2,1)S(1)}, bf16[512,1152]{1,0:T(8,128)(2,1)}, u32[]{:S(2)}) copy-start(bf16[512,1152]{1,0:T(8,128)(2,1)} %get-tuple-element.38.early_at.early_counts) | copy-start | bytes 3538948
  34.5 14.8 %copy-start.2 = (bf16[128,1152]{1,0:T(8,128)(2,1)S(1)}, bf16[128,1152]{1,0:T(8,128)(2,1)}, u32[]{:S(2)}) copy-start(bf16[128,1152]{1,0:T(8,128)(2,1)} %get-tuple-element.58.mirror_rows) | copy-start | bytes 884740
  63.9 1.6 %collective-permute-start.1 = (bf16[32,4,1280]{2,1,0:T(4,128)(2,1)S(1)}, bf16[32,4,1280]{2,1,0:T(4,128)(2,1)S(1)}, u32[]{:S(2)}, u32[]{:S(2)}) collective-permute-start(bf16[32,4,1280]{2,1,0:T(4,128)(2,1)S(1)} %all_to_all.21.received), channel_id=1, source_target_pairs={{0,1},{1,0},{2,3},{3,2},{4,5},{5,4},{6,7},{7,6},{8,9},{9,8},{10,11... | collective-permute-start | bytes 983048 | tf_op jit(solution)/shard_map/ppermute | solution.py:741

commit v10 on v9

--- a/solution.py
+++ b/solution.py
@@ -495,8 +495,10 @@
     message_one,
     grad_z,
     w_self_one,
+    features_at,
+    own_weights,
     grad_features,
-    own_weights,
+    semaphore,
 ):
     node_dev, width = grad_z.shape
     mirrors = picking.shape[0]
@@ -511,19 +513,20 @@
             + tdot(picking[:, rows], returned)
             + tdot(mirror_rows[:, rows], mirrored[...])
         ).astype(BF16)
+    copy = pltpu.make_async_copy(grad_features, features_at, semaphore)
+    copy.start()
     for group in range(own_weights.shape[0] // mirrors):
         own_weights[pl.ds(group * mirrors, mirrors), :] = by_row(
             received[:, :, (group + 1) * width : (group + 2) * width]
         )
+    copy.wait()
 
 
 def write_out(
     core,
     other,
-    grad_features,
     own_weights,
     bias_total,
-    features_at,
     weights_at,
     bias_at,
     other_weights,
@@ -534,9 +537,8 @@
     mine = pl.multiple_of(core[0] * half, half)
     theirs = pl.multiple_of((1 - core[0]) * half, half)
     copies = [
-        pltpu.make_async_copy(grad_features, features_at, semaphores.at[0]),
-        pltpu.make_async_copy(own_weights, weights_at.at[pl.ds(mine, half)], semaphores.at[1]),
-        pltpu.make_async_copy(bias_total, bias_at, semaphores.at[2]),
+        pltpu.make_async_copy(own_weights, weights_at.at[pl.ds(mine, half)], semaphores.at[0]),
+        pltpu.make_async_copy(bias_total, bias_at, semaphores.at[1]),
     ]
     for copy in copies:
         copy.start()
@@ -546,10 +548,10 @@
         )
     copies.append(
         pltpu.make_async_copy(
-            other_weights, weights_at.at[pl.ds(theirs, half)], semaphores.at[3]
-        )
-    )
-    copies[3].start()
+            other_weights, weights_at.at[pl.ds(theirs, half)], semaphores.at[2]
+        )
+    )
+    copies[2].start()
     for copy in copies:
         copy.wait()
 
@@ -742,7 +744,8 @@
     grad_features, own_weights = run(
         finish,
         "finish",
-        [rows_bf16, pltpu.VMEM((half, width), F32)],
+        [pltpu.HBM((node_dev, width), BF16), pltpu.VMEM((half, width), F32)],
+        scratch=[rows_bf16, pltpu.SemaphoreType.DMA],
         vmem=[
             received,
             mirrored,
@@ -757,17 +760,16 @@
         flops=2 * node_dev * (slots + mirrors + width) * width,
         moved=4 * node_dev * slots,
     )
-    grad_features, grad_weights, grad_bias = run(
+    grad_weights, grad_bias = run(
         write_out,
         "write_out",
         [
-            pltpu.HBM((node_dev, width), BF16),
             pltpu.HBM((2 * half, width), F32),
             pltpu.HBM((1, width), F32),
         ],
         smem=[core.reshape(1)],
-        vmem=[other, grad_features, own_weights, bias_total],
-        scratch=[pltpu.VMEM((half, width), F32), pltpu.SemaphoreType.DMA((4,))],
+        vmem=[other, own_weights, bias_total],
+        scratch=[pltpu.VMEM((half, width), F32), pltpu.SemaphoreType.DMA((3,))],
     )
     return (
         grad_features,

time: 67.1 us -> 67.3 us (level)
  Pallas kernels: 16.6 us -> 17.3 us
  transfers between devices with their start and end apart: 4 -> 4, of which waited for: 4 -> 3; matrix products, arithmetic and copies ran while one was open for 0% -> 0% of each run, Pallas kernels for 14% -> 15%
where the time goes in v10:
time: 67.3 us; the launch traced here: 66.9 us
  blocking collectives  28.7 us (43%)
  Pallas kernels  17.3 us (26%)
  starting transfers between devices  10.2 us (15%)
  waiting for transfers between devices  9.15 us (14%)
  between operations  1.5 us (2%)
    all_to_all x2, blocking collectives, exchange(): return lax.all_to_all(rows, AXES, split_axis=0, concat_axis=0, tiled=True)  28.7 us
    pallas_call x10, Pallas kernels, run(): pl.pallas_call(kernel, out_shape=tuple(outs), in_specs=[pl.BlockSpec(memo...  17.3 us
    all_to_all x2, starting transfers between devices, exchange(): return lax.all_to_all(rows, AXES, split_axis=0, concat_axis=0, tiled=True)  9.89 us
    all_to_all x2, waiting for transfers between devices, exchange(): return lax.all_to_all(rows, AXES, split_axis=0, concat_axis=0, tiled=True)  8.9 us
  transfers between devices with their start and end apart: 4, of which 3 were waited for; matrix products, arithmetic and copies ran while one was open for 0% of the time, Pallas kernels for 15%

profile of v10, /device:TPU:0, one launch (start us, length us, event | category | flops | bytes accessed | tf_op | source)
XLA Modules:
  0.0 66.9 jit_solution(6957417615930173156)
XLA Ops:
  0.6 2.4 %pick_rows.1 = (bf16[32,4,512]{2,1,0:T(4,128)(2,1)}, bf16[1024,256]{1,0:T(8,128)(2,1)S(1)}, bf16[128,1024]{1,0:T(8,128)(2,1)S(1)}, s32[16,128]{1,0:T(8,128)S(1)}, s32[16,128]{1,0:T(8,128)S(1)}) custom-call(bf16[1024,256]{1,0:T(8,128)(2,1)} %features_at.5, bf16[1024,256]{1,0:T(8,128)(2,1)} %cotangent_at.3, s32[8,128]{1,0:T(8,128)} %bitcast.10, ...), custom_call_target="tpu_custom_call" | custom-call | flops 134217728 | tf_op jit(solution)/shard_map/pick_rows/pallas_call | solution.py:42
  3.1 7.3 %all-to-all-start = ((bf16[32,4,512]{2,1,0:T(4,128)(2,1)}), bf16[32,4,512]{2,1,0:T(4,128)(2,1)S(1)}, u32[]{:S(2)}, u32[]{:S(2)}) async-start(bf16[32,4,512]{2,1,0:T(4,128)(2,1)} %get-tuple-element.39), calls=%async_computation | async-start | bytes 262144 | tf_op jit(solution)/shard_map/all_to_all | solution.py:36
  11.0 2.9 %count_edges.1 = (bf16[512,1152]{1,0:T(8,128)(2,1)}, bf16[1024,256]{1,0:T(8,128)(2,1)}, bf16[128,1152]{1,0:T(8,128)(2,1)S(1)}, f32[128,512]{1,0:T(8,128)S(1)}) custom-call(s32[1]{0:T(128)S(6)} %copy.15.edge_count, bf16[1024,256]{1,0:T(8,128)(2,1)} %features_at.5, bf16[1024,256]{1,0:T(8,128)(2,1)S(1)} %get-tuple-element.34.scaled, ...), custom_call_target="tpu_custom_call" | custom-call | flops 3623878656 | tf_op jit(solution)/shard_map/count_edges/pallas_call | solution.py:42
  14.0 4.6 %all-to-all-done = bf16[32,4,512]{2,1,0:T(4,128)(2,1)S(1)} async-done(((bf16[32,4,512]{2,1,0:T(4,128)(2,1)}), bf16[32,4,512]{2,1,0:T(4,128)(2,1)S(1)}, u32[]{:S(2)}, u32[]{:S(2)}) %all-to-all-start) | async-done | bytes 131104 | tf_op jit(solution)/shard_map/all_to_all | solution.py:36
  18.6 0.9 %mirror_sums.1 = bf16[32,4,512]{2,1,0:T(4,128)(2,1)} custom-call(f32[128,512]{1,0:T(8,128)S(1)} %get-tuple-element.43.partial_in, bf16[128,1152]{1,0:T(8,128)(2,1)S(1)} %get-tuple-element.40.mirror_rows, bf16[128,512]{1,0:T(8,128)(2,1)S(1)} %reshape.39.mirrored), custom_call_target="tpu_custom_call" | custom-call | flops 16777216 | tf_op jit(solution)/shard_map/mirror_sums/pallas_call | solution.py:42
  19.5 2.6 %all-to-all-start.1 = ((bf16[32,4,512]{2,1,0:T(4,128)(2,1)}), bf16[32,4,512]{2,1,0:T(4,128)(2,1)S(1)}, u32[]{:S(2)}, u32[]{:S(2)}) async-start(bf16[32,4,512]{2,1,0:T(4,128)(2,1)} %mirror_sums.1), calls=%async_computation.1 | async-start | bytes 262144 | tf_op jit(solution)/shard_map/all_to_all | solution.py:36
  22.1 0.0 copy-start.3
  22.1 0.0 copy-start.4
  22.2 0.0 copy-start.5
  22.2 0.0 copy-start.6
  22.2 0.0 copy-start.7
  22.2 0.0 copy-start.8
  22.2 3.9 %local_sums.1 = (f32[1024,256]{1,0:T(8,128)S(1)}, bf16[1024,256]{1,0:T(8,128)(2,1)S(1)}, f32[1024,256]{1,0:T(8,128)}, bf16[128,1152]{1,0:T(8,128)(2,1)}, bf16[512,1152]{1,0:T(8,128)(2,1)}) custom-call(s32[1]{0:T(128)S(6)} %copy.15.edge_count, bf16[512,1152]{1,0:T(8,128)(2,1)} %get-tuple-element.37.early_at.early_counts, bf16[1024,256]{1,0:T(8,128)(2,1)} %features_at.5, ...), custom_call_target="tpu_custom_call" | custom-call | flops 3623878656 | tf_op jit(solution)/shard_map/local_sums/pallas_call | solution.py:42
  26.1 4.3 %all-to-all-done.1 = bf16[32,4,512]{2,1,0:T(4,128)(2,1)S(1)} async-done(((bf16[32,4,512]{2,1,0:T(4,128)(2,1)}), bf16[32,4,512]{2,1,0:T(4,128)(2,1)S(1)}, u32[]{:S(2)}, u32[]{:S(2)}) %all-to-all-start.1) | async-done | bytes 131104 | tf_op jit(solution)/shard_map/all_to_all | solution.py:36
  30.5 2.7 %middle.1 = (bf16[1024,256]{1,0:T(8,128)(2,1)S(1)}, bf16[512,256]{1,0:T(8,128)(2,1)S(1)}, f32[4,128]{1,0:T(4,128)S(1)}, bf16[1024,256]{1,0:T(8,128)(2,1)S(1)}, b...) custom-call(s32[1]{0:T(128)} %bitcast.core, ...), custom_call_target="tpu_custom_call" | custom-call | flops 1342177280 | tf_op jit(solution)/shard_map/middle/pallas_call | solution.py:42
  33.1 0.3 collective-permute-start
  33.4 1.0 %messages.1 = (bf16[1024,256]{1,0:T(8,128)(2,1)S(1)}, f32[128,256]{1,0:T(8,128)S(1)}, f32[512,256]{1,0:T(8,128)S(1)}) custom-call(s32[1]{0:T(128)} %bitcast.core, s32[8,128]{1,0:T(8,128)S(1)} %bitcast.12, bf16[1024,256]{1,0:T(8,128)(2,1)S(1)} %get-tuple-element.46.grad_z, bf16[256,256]{1,0:T(8,128)(2,1)S(1)} %copy-done.3, ...), custom_call_target="tpu_custom_call" | custom-call | flops 402653184 | tf_op jit(solution)/shard_map/messages/pallas_call | solution.py:42
  34.5 0.2 collective-permute-done.other_half
  34.7 0.1 join_first.1
  34.8 14.4 %all_to_all.20.received = bf16[32,4,1408]{2,1,0:T(4,128)(2,1)S(1)} all-to-all(bf16[32,4,1408]{2,1,0:T(4,128)(2,1)S(1)} %join_first.1), channel_id=1, replica_groups=mesh['dom'=8,'sub'=4] {'dom','sub'}, dimensions={0} | all-to-all | bytes 720896 | tf_op jit(solution)/shard_map/all_to_all | solution.py:36
  49.3 0.4 join_second.1
  49.7 14.2 %all_to_all.21.received = bf16[32,4,1280]{2,1,0:T(4,128)(2,1)S(1)} all-to-all(bf16[32,4,1280]{2,1,0:T(4,128)(2,1)S(1)} %get-tuple-element.58), channel_id=1, replica_groups=mesh['dom'=8,'sub'=4] {'dom','sub'}, dimensions={0} | all-to-all | bytes 655360 | tf_op jit(solution)/shard_map/all_to_all | solution.py:36
  63.9 2.0 %finish.1 = (bf16[1024,256]{1,0:T(8,128)(2,1)}, f32[512,256]{1,0:T(8,128)S(1)}) custom-call(bf16[32,4,1280]{2,1,0:T(4,128)(2,1)S(1)} %all_to_all.21.received, bf16[128,256]{1,0:T(8,128)(2,1)S(1)} %get-tuple-element.59.mirrored, bf16[128,1024]{1,0:T(8,128)(2,1)S(1)} %get-tuple-element.44.picking, bf16[512,1152]{1,0:T(8,128)(2,1)S(1)} %copy-done, ...), custom_call_target="tpu_custom_call" | custom-call | flops 805306368 | bytes 4718592 | tf_op jit(solution)/shard_map/finish/pallas_call | solution.py:42
  65.9 1.0 %write_out.1 = (f32[1024,256]{1,0:T(8,128)}, f32[1,256]{1,0:T(1,128)}) custom-call(s32[1]{0:T(128)} %bitcast.core, bf16[32,4,1280]{2,1,0:T(4,128)(2,1)S(1)} %collective-permute-done.1.other, f32[512,256]{1,0:T(8,128)S(1)} %get-tuple-element.61.own_weights, f32[1,256]{1,0:T(1,128)S(1)} %get-tuple-element.62.bias_total), custom_call_target="tpu_custom_call" | custom-call | tf_op jit(solution)/shard_map/write_out/pallas_call | solution.py:42
  (16 shorter events, 0.1 us)
Async XLA Ops:
  3.1 15.5 %all-to-all-start = ((bf16[32,4,512]{2,1,0:T(4,128)(2,1)}), bf16[32,4,512]{2,1,0:T(4,128)(2,1)S(1)}, u32[]{:S(2)}, u32[]{:S(2)}) async-start(bf16[32,4,512]{2,1,0:T(4,128)(2,1)} %get-tuple-element.39), calls=%async_computation | async-start | bytes 262144 | tf_op jit(solution)/shard_map/all_to_all | solution.py:36
  19.5 10.8 %all-to-all-start.1 = ((bf16[32,4,512]{2,1,0:T(4,128)(2,1)}), bf16[32,4,512]{2,1,0:T(4,128)(2,1)S(1)}, u32[]{:S(2)}, u32[]{:S(2)}) async-start(bf16[32,4,512]{2,1,0:T(4,128)(2,1)} %mirror_sums.1), calls=%async_computation.1 | async-start | bytes 262144 | tf_op jit(solution)/shard_map/all_to_all | solution.py:36
  22.1 8.3 %copy-start.3 = (bf16[256,256]{1,0:T(8,128)(2,1)S(1)}, bf16[256,256]{1,0:T(8,128)(2,1)}, u32[]{:S(2)}) copy-start(bf16[256,256]{1,0:T(8,128)(2,1)} %w_nbr_one.3) | copy-start | bytes 393220
  22.1 8.3 %copy-start.4 = (bf16[256,256]{1,0:T(8,128)(2,1)S(1)}, bf16[256,256]{1,0:T(8,128)(2,1)}, u32[]{:S(2)}) copy-start(bf16[256,256]{1,0:T(8,128)(2,1)} %w_self_one.3) | copy-start | bytes 393220
  22.2 8.3 %copy-start.5 = (s32[1024]{0:T(1024)S(1)}, s32[1024]{0:T(1024)}, u32[]{:S(2)}) copy-start(s32[1024]{0:T(1024)} %param.19) | copy-start | bytes 12292
  22.2 8.3 %copy-start.6 = (bf16[256,256]{1,0:T(8,128)(2,1)S(1)}, bf16[256,256]{1,0:T(8,128)(2,1)}, u32[]{:S(2)}) copy-start(bf16[256,256]{1,0:T(8,128)(2,1)} %w_nbr_two.1) | copy-start | bytes 393220
  22.2 8.3 %copy-start.7 = (bf16[256,256]{1,0:T(8,128)(2,1)S(1)}, bf16[256,256]{1,0:T(8,128)(2,1)}, u32[]{:S(2)}) copy-start(bf16[256,256]{1,0:T(8,128)(2,1)} %w_self_two.1) | copy-start | bytes 393220
  22.2 8.3 %copy-start.8 = (f32[256]{0:T(256)S(1)}, f32[256]{0:T(256)}, u32[]{:S(2)}) copy-start(f32[256]{0:T(256)} %param.16) | copy-start | bytes 3076
  33.1 1.6 %collective-permute-start = (bf16[512,256]{1,0:T(8,128)(2,1)S(1)}, bf16[512,256]{1,0:T(8,128)(2,1)S(1)}, u32[]{:S(2)}, u32[]{:S(2)}) collective-permute-start(bf16[512,256]{1,0:T(8,128)(2,1)S(1)} %get-tuple-element.52), channel_id=1, source_target_pairs={{0,1},{1,0},{2,3},{3,2},{4,5},{5,4},{6,7},{7,6},{8,9},{9,8},{10,11... | collective-permute-start | bytes 786440 | tf_op jit(solution)/shard_map/ppermute | solution.py:698
  33.4 15.9 %copy-start.1 = (bf16[512,1152]{1,0:T(8,128)(2,1)S(1)}, bf16[512,1152]{1,0:T(8,128)(2,1)}, u32[]{:S(2)}) copy-start(bf16[512,1152]{1,0:T(8,128)(2,1)} %get-tuple-element.56.late_counts) | copy-start | bytes 3538948
  34.5 14.8 %copy-start = (bf16[512,1152]{1,0:T(8,128)(2,1)S(1)}, bf16[512,1152]{1,0:T(8,128)(2,1)}, u32[]{:S(2)}) copy-start(bf16[512,1152]{1,0:T(8,128)(2,1)} %get-tuple-element.37.early_at.early_counts) | copy-start | bytes 3538948
  34.5 14.8 %copy-start.2 = (bf16[128,1152]{1,0:T(8,128)(2,1)S(1)}, bf16[128,1152]{1,0:T(8,128)(2,1)}, u32[]{:S(2)}) copy-start(bf16[128,1152]{1,0:T(8,128)(2,1)} %get-tuple-element.57.mirror_rows) | copy-start | bytes 884740
  63.9 2.0 %collective-permute-start.1 = (bf16[32,4,1280]{2,1,0:T(4,128)(2,1)S(1)}, bf16[32,4,1280]{2,1,0:T(4,128)(2,1)S(1)}, u32[]{:S(2)}, u32[]{:S(2)}) collective-permute-start(bf16[32,4,1280]{2,1,0:T(4,128)(2,1)S(1)} %all_to_all.21.received), channel_id=1, source_target_pairs={{0,1},{1,0},{2,3},{3,2},{4,5},{5,4},{6,7},{7,6},{8,9},{9,8},{10,11... | collective-permute-start | bytes 983048 | tf_op jit(solution)/shard_map/ppermute | solution.py:743
